TPU v7x, 32 devices: a whole 2x2x4 slice. The times are simulated.
32 devices in a mesh: ctx: 4 (over z), head: 4 (over y, x), dp: 2 (over core).
Axes of the slice: x: 2, y: 2, z: 4, core: 2. Of those that a mesh axis runs over, the one named last changes fastest.
Arguments:
- query_raw: bfloat16 [4096, 2048], P(('dp', 'ctx', 'head')), parts along dimension 0, may hold values from -6 to 6
- key_raw: bfloat16 [4096, 2048], P(('dp', 'ctx', 'head')), parts along dimension 0, may hold values from -6 to 6
- value_raw: bfloat16 [4096, 2048], P(('dp', 'ctx', 'head')), parts along dimension 0, may hold values from -6 to 6
- log_decay: bfloat16 [4096, 2048], P(('dp', 'ctx', 'head')), parts along dimension 0, may hold values from -1 to 0, as said below
- beta: bfloat16 [4096, 16], P(('dp', 'ctx', 'head')), parts along dimension 0, may hold values from 0.0029 to 1
- conv_weight: float32 [3, 4, 2048], replicated, may hold values from -3 to 3
- out_gate: bfloat16 [4096, 2048], P(('dp', 'ctx', 'head')), parts along dimension 0, may hold values from -6 to 6
- norm_gain: float32 [128], replicated, may hold values from 0.1 to 1.9
Outputs:
- mixed: bfloat16 [4096, 2048], P(('dp', 'ctx', 'head')), parts along dimension 0
There are 2 independent parts, one for each index of `dp`. A program takes and returns all parts, laid end to end along the dimension named above; an argument that names none is the same for every part. Nothing has to cross between parts.
Inputs may be any that keep to these rules, and one draw needn't show every extreme that they name: `log_decay`: logarithms (all <= 0) of the decay factors of the state.
All inputs are finite; a program needn't handle non-finite values.
Results may differ from a plain program's by a relative error of at most 0.013.
Values may be sent and summed in bfloat16 or wider, within the bound.
No kernel may reach another device: no remote copies, remote signals or barrier semaphores. Data moves between devices by JAX's collectives and lax.ppermute only.
A program may use at most 64 MiB of HBM per device.

v0:
```python
import jax
import jax.numpy as jnp
from jax import lax
from jax.sharding import PartitionSpec as P

HEAD_WIDTH = 128
STRETCH = 64


def shifted(block, axis, distance):
    devices = range(lax.axis_size(axis))
    route = [(i - distance, i) for i in devices if i - distance in devices]
    return lax.ppermute(block, axis, route)


def matmul(left, right):
    return jnp.einsum("...ij,...jk->...ik", left, right, precision=lax.Precision.HIGHEST)


def short_conv(values_in, rim_rows, taps):
    count = values_in.shape[0]
    width = taps.shape[0]
    padded = jnp.concatenate([rim_rows, values_in], 0).astype(jnp.float32)
    total = taps[0] * padded[0:count]
    for offset in range(1, width):
        total = total + taps[offset] * padded[offset : offset + count]
    return jax.nn.silu(total).astype(jnp.bfloat16)


def block_terms(query, keys, values, log_gate, rates):
    keys = keys * lax.rsqrt(jnp.sum(keys * keys, -1, keepdims=True) + 1e-06)
    cumul = jnp.cumsum(log_gate, axis=-2)
    last_cum = cumul[..., -1:, :]
    query_up = query * jnp.exp(cumul)
    key_up = keys * jnp.exp(cumul)
    key_down = keys * jnp.exp(-cumul)
    key_end = keys * jnp.exp(last_cum - cumul)
    length = query.shape[-2]
    positions = jnp.arange(length)
    strict = positions[:, None] > positions[None, :]
    weak = positions[:, None] >= positions[None, :]
    inner = jnp.einsum("...cd,...jd->...cj", key_up, key_down, precision=lax.Precision.HIGHEST)
    unit_lower = jnp.eye(length, dtype=jnp.float32) + jnp.where(
        strict, inner * rates[..., :, None], 0.0
    )
    right_side = jnp.concatenate([rates[..., None] * values, rates[..., None] * key_up], -1)
    solved = lax.linalg.triangular_solve(
        unit_lower, right_side, left_side=True, lower=True, unit_diagonal=True
    )
    width = values.shape[-1]
    update_rows = solved[..., :width]
    correct_rows = solved[..., width:]
    scores = jnp.where(
        weak,
        jnp.einsum("...cd,...jd->...cj", query_up, key_down, precision=lax.Precision.HIGHEST),
        0.0,
    )
    return (query_up, key_end, update_rows, correct_rows, scores, last_cum)


def finish(attention, gate_logits, gain):
    rows_count = attention.shape[0]
    heads_view = attention.astype(jnp.float32).reshape(rows_count, -1, HEAD_WIDTH)
    scale = lax.rsqrt(jnp.mean(heads_view * heads_view, -1, keepdims=True) + 1e-05)
    gate_view = jax.nn.sigmoid(gate_logits.astype(jnp.float32).reshape(rows_count, -1, HEAD_WIDTH))
    final_output = heads_view * scale * gain * gate_view
    return final_output.reshape(rows_count, -1).astype(jnp.bfloat16)


def shards(query_raw, key_raw, value_raw, log_decay, beta, conv_weight, out_gate, norm_gain):
    rim_width = conv_weight.shape[1] - 1
    query_in, key_in, value_in = (query_raw, key_raw, value_raw)
    moved = (
        lax.all_to_all(query_in, "head", split_axis=1, concat_axis=0, tiled=True),
        lax.all_to_all(key_in, "head", split_axis=1, concat_axis=0, tiled=True),
        lax.all_to_all(value_in, "head", split_axis=1, concat_axis=0, tiled=True),
        lax.all_to_all(log_decay, "head", split_axis=1, concat_axis=0, tiled=True),
        lax.all_to_all(beta, "head", split_axis=1, concat_axis=0, tiled=True),
    )
    query_here, key_here, value_here, gate_here, rate_here = moved
    group_width = query_here.shape[1]
    taps_here = lax.dynamic_slice_in_dim(
        conv_weight, lax.axis_index("head") * group_width, group_width, 2
    )
    rim_rows = shifted(
        (query_here[-rim_width:], key_here[-rim_width:], value_here[-rim_width:]), "ctx", 1
    )
    query_here = short_conv(query_here, rim_rows[0], taps_here[0])
    key_here = short_conv(key_here, rim_rows[1], taps_here[1])
    value_here = short_conv(value_here, rim_rows[2], taps_here[2])
    tokens_here = query_here.shape[0]
    heads_here = rate_here.shape[1]
    blocks_count = tokens_here // STRETCH

    def to_blocks(array):
        return (
            array.astype(jnp.float32)
            .reshape(blocks_count, STRETCH, heads_here, HEAD_WIDTH)
            .transpose(2, 0, 1, 3)
        )

    rates = (
        rate_here.astype(jnp.float32).reshape(blocks_count, STRETCH, heads_here).transpose(2, 0, 1)
    )
    query_up, key_end, update_rows, correct_rows, scores, last_cum = block_terms(
        to_blocks(query_here),
        to_blocks(key_here),
        to_blocks(value_here),
        to_blocks(gate_here),
        rates,
    )
    identity = jnp.eye(HEAD_WIDTH, dtype=jnp.float32)
    transition = jnp.exp(last_cum)[..., 0, :, None] * identity - jnp.einsum(
        "...cd,...ce->...de", key_end, correct_rows, precision=lax.Precision.HIGHEST
    )
    addend = jnp.einsum("...cd,...ce->...de", key_end, update_rows, precision=lax.Precision.HIGHEST)
    trans_steps = jnp.moveaxis(transition, 1, 0)
    add_steps = jnp.moveaxis(addend, 1, 0)

    def absorb(carry, pair):
        moving, adding = carry
        step_move, step_add = pair
        return ((matmul(step_move, moving), matmul(step_move, adding) + step_add), None)

    eye_batch = jnp.broadcast_to(identity, (heads_here, HEAD_WIDTH, HEAD_WIDTH))
    zero_state = jnp.zeros((heads_here, HEAD_WIDTH, HEAD_WIDTH), jnp.float32)
    (dev_move, dev_add), _ = lax.scan(absorb, (eye_batch, zero_state), (trans_steps, add_steps))

    def relay_step(step_index, state):
        return shifted(matmul(dev_move, state) + dev_add, "ctx", 1)

    incoming = lax.fori_loop(0, lax.axis_size("ctx") - 1, relay_step, zero_state)

    def advance(state, pair):
        step_move, step_add = pair
        return (matmul(step_move, state) + step_add, state)

    _, starts = lax.scan(advance, incoming, (trans_steps, add_steps))
    starts = jnp.moveaxis(starts, 0, 1)
    written = update_rows - matmul(correct_rows, starts)
    output = matmul(query_up, starts) + matmul(scores, written)
    attention = (
        output.transpose(1, 2, 0, 3)
        .reshape(tokens_here, heads_here * HEAD_WIDTH)
        .astype(jnp.bfloat16)
    )
    back_rows = lax.all_to_all(attention, "head", split_axis=0, concat_axis=1, tiled=True)
    return finish(back_rows, out_gate, norm_gain)


def solution(mesh):
    placed = (
        P(("dp", "ctx", "head"), None),
        P(("dp", "ctx", "head"), None),
        P(("dp", "ctx", "head"), None),
        P(("dp", "ctx", "head"), None),
        P(("dp", "ctx", "head"), None),
        P(),
        P(("dp", "ctx", "head"), None),
        P(),
    )
    return jax.shard_map(
        shards,
        mesh=mesh,
        in_specs=placed,
        out_specs=P(("dp", "ctx", "head"), None),
        check_vma=False,
    )
```

profile of v0, /device:TPU:0, one launch (start us, length us, event | category | flops | bytes accessed | tf_op | source)
XLA Modules:
  0.0 341.9 jit_solution(4705319947971545409)
XLA Ops:
  0.0 5.3 %all-to-all-start.3 = ((bf16[128,4,4]{0,2,1:T(4,128)(2,1)}), bf16[128,4,4]{0,2,1:T(4,128)(2,1)S(1)}, u32[]{:S(2)}, u32[]{:S(2)}) async-start(bf16[128,4,4]{0,2,1:T(4,128)(2,1)} %bitcast.165), calls=%async_computation.3 | async-start | bytes 8192 | tf_op jit(solution)/shard_map/all_to_all | solution.py:78
  5.3 2.1 copy.41
  7.4 2.6 all-to-all-done.3
  10.0 3.5 %all-to-all-start.2 = ((bf16[128,4,512]{0,2,1:T(8,128)(2,1)}), bf16[128,4,512]{0,2,1:T(8,128)(2,1)S(1)}, u32[]{:S(2)}, u32[]{:S(2)}) async-start(bf16[128,4,512]{0,2,1:T(8,128)(2,1)} %bitcast.16), calls=%async_computation.2 | async-start | bytes 1048576 | tf_op jit(solution)/shard_map/all_to_all | solution.py:75
  14.5 1.6 constant_dynamic-slice_fusion
  16.1 4.2 %all-to-all-done.2 = bf16[128,4,512]{0,2,1:T(8,128)(2,1)S(1)} async-done(((bf16[128,4,512]{0,2,1:T(8,128)(2,1)}), bf16[128,4,512]{0,2,1:T(8,128)(2,1)S(1)}, u32[]{:S(2)}, u32[]{:S(2)}) %all-to-all-start.2) | async-done | bytes 524320 | tf_op jit(solution)/shard_map/all_to_all | solution.py:75
  20.3 3.5 %all-to-all-start.4 = ((bf16[128,4,512]{0,2,1:T(8,128)(2,1)}), bf16[128,4,512]{0,2,1:T(8,128)(2,1)S(1)}, u32[]{:S(2)}, u32[]{:S(2)}) async-start(bf16[128,4,512]{0,2,1:T(8,128)(2,1)} %bitcast.30), calls=%async_computation.4 | async-start | bytes 1048576 | tf_op jit(solution)/shard_map/all_to_all | solution.py:76
  26.0 4.4 %all-to-all-done.4 = bf16[128,4,512]{0,2,1:T(8,128)(2,1)S(1)} async-done(((bf16[128,4,512]{0,2,1:T(8,128)(2,1)}), bf16[128,4,512]{0,2,1:T(8,128)(2,1)S(1)}, u32[]{:S(2)}, u32[]{:S(2)}) %all-to-all-start.4) | async-done | bytes 524320 | tf_op jit(solution)/shard_map/all_to_all | solution.py:76
  30.4 3.5 %all-to-all-start.1 = ((bf16[128,4,512]{2,0,1:T(8,128)(2,1)}), bf16[128,4,512]{2,0,1:T(8,128)(2,1)S(1)}, u32[]{:S(2)}, u32[]{:S(2)}) async-start(bf16[128,4,512]{2,0,1:T(8,128)(2,1)} %bitcast.118), calls=%async_computation.1 | async-start | bytes 1048576 | tf_op jit(solution)/shard_map/all_to_all | solution.py:77
  35.8 4.1 %collective-permute-start.2 = (bf16[3,512]{1,0:T(4,128)(2,1)}, bf16[3,512]{1,0:T(4,128)(2,1)}, u32[]{:S(2)}, u32[]{:S(2)}) collective-permute-start(bf16[3,512]{1,0:T(4,128)(2,1)} %slice.157), channel_id=1, source_target_pairs={{0,8},{8,16},{16,24},{1,9},{9,17},{17,25},{2,10},{10,18},{18,26},{... | collective-permute-start | bytes 9224 | tf_op jit(solution)/shard_map/ppermute | solution.py:13
  40.8 3.5 %collective-permute-start.3 = (bf16[3,512]{1,0:T(4,128)(2,1)}, bf16[3,512]{1,0:T(4,128)(2,1)}, u32[]{:S(2)}, u32[]{:S(2)}) collective-permute-start(bf16[3,512]{1,0:T(4,128)(2,1)} %slice.162), channel_id=1, source_target_pairs={{0,8},{8,16},{16,24},{1,9},{9,17},{17,25},{2,10},{10,18},{18,26},{... | collective-permute-start | bytes 9224 | tf_op jit(solution)/shard_map/ppermute | solution.py:13
  44.3 4.2 %all-to-all-start = ((bf16[128,4,512]{0,2,1:T(8,128)(2,1)}), bf16[128,4,512]{0,2,1:T(8,128)(2,1)S(1)}, u32[]{:S(2)}, u32[]{:S(2)}) async-start(bf16[128,4,512]{0,2,1:T(8,128)(2,1)} %bitcast.4), calls=%async_computation | async-start | bytes 1048576 | tf_op jit(solution)/shard_map/all_to_all | solution.py:74
  49.6 5.4 %all-to-all-done = bf16[128,4,512]{0,2,1:T(8,128)(2,1)S(1)} async-done(((bf16[128,4,512]{0,2,1:T(8,128)(2,1)}), bf16[128,4,512]{0,2,1:T(8,128)(2,1)S(1)}, u32[]{:S(2)}, u32[]{:S(2)}) %all-to-all-start) | async-done | bytes 524320 | tf_op jit(solution)/shard_map/all_to_all | solution.py:74
  55.9 3.5 %collective-permute-start.1 = (bf16[3,512]{1,0:T(4,128)(2,1)}, bf16[3,512]{1,0:T(4,128)(2,1)}, u32[]{:S(2)}, u32[]{:S(2)}) collective-permute-start(bf16[3,512]{1,0:T(4,128)(2,1)} %slice.151), channel_id=1, source_target_pairs={{0,8},{8,16},{16,24},{1,9},{9,17},{17,25},{2,10},{10,18},{18,26},{... | collective-permute-start | bytes 9224 | tf_op jit(solution)/shard_map/ppermute | solution.py:13
  64.9 2.6 bitcast_multiply_fusion.1
  67.5 3.2 fusion.32
  70.7 158.7 %custom-call.3 = f32[4,8,1,64,64]{3,4,2,1,0:T(8,128)} custom-call(f32[4,8,1,64,64]{4,3,2,1,0:T(8,128)} %fusion.32), custom_call_target="InvertDiagBlocksLowerTriangular" | custom-call | tf_op jit(solution)/shard_map/triangular_solve | solution.py:47
  229.4 3.5 %fusion.14 = f32[4,8,64,256]{3,2,1,0:T(8,128)S(1)} fusion(f32[4,8,64,128]{3,2,1,0:T(8,128)} %get-tuple-element.177, f32[4,8,64,128]{3,2,1,0:T(8,128)S(1)} %get-tuple-element.176, f32[4,8,1,64,64]{3,4,2,1,0:T(8,128)} %custom-call.3), kind=kOutput, calls=%fused_computation.18 | convolution fusion | flops 403177472 | bytes 4718592 | tf_op jit(solution)/shard_map/triangular_solve | solution.py:47
  232.9 3.8 %convolution_bitcast_fusion = f32[8,4,128,128]{3,2,0,1:T(8,128)S(1)} fusion(f32[4,8,64,256]{3,2,1,0:T(8,128)S(1)} %fusion.14, f32[4,8,64,128]{3,1,2,0:T(8,128)S(1)} %fusion.54, f32[8,64,4,128]{3,2,1,0:T(4,128)S(1)} %reshape.120, f32[4,8,128]{2,1,0:T(8,128)S(1)} %get-tuple-element.162, f32[4,8,64]{2,1,0:T(8,128)S(1)} %add_rsqrt_fusion), kind=kOutput, calls=%fused_computation.27 | convolution fusion | flops 403439616 | bytes 5275648 | tf_op jit(solution)/shard_map/...cd,...ce->...de/dot_general | solution.py:116
  236.8 1.5 copy.52
  238.3 4.3 %bitcast_subtract_fusion = f32[8,4,128,128]{3,2,0,1:T(8,128)S(1)} fusion(f32[128,128]{1,0:T(8,128)S(1)} %fusion.62, f32[8,4,128]{2,0,1:T(8,128)S(1)} %get-tuple-element.163, f32[4,8,64,256]{3,2,1,0:T(8,128)S(1)} %fusion.14, f32[4,8,64,128]{3,1,2,0:T(8,128)S(1)} %fusion.54, f32[8,64,4,128]{3,2,1,0:T(4,128)S(1)} %reshape.120, ...), kind=kOutput, calls=%fused_computation.22 | convolution fusion | flops 404488192 | bytes 5357568 | tf_op jit(solution)/shard_map/...cd,...ce->...de/dot_general | solution.py:113
  242.6 1.5 copy.51
  244.1 22.9 %while.37 = (s32[]{:T(128)}, f32[4,128,128]{2,1,0:T(8,128)S(1)}, f32[4,128,128]{2,1,0:T(8,128)S(1)}, f32[8,4,128,128]{3,2,1,0:T(8,128)}, f32[8,4,128,128]{3,2,1,0:T(8,128)}, /*index=5*/s32[]{:T(128)}, s32[]{:T(128)}) while((s32[]{:T(128)}, f32[4,128,128]{2,1,0:T(8,128)S(1)}, f32[4,128,128]{2,1,0:T(8,128)S(1)}, ...), condition=%wide.region_3.4_spmd.clone, body=%wide.region_2.3_spmd.clone.sunk | while | flops 201457664 | bytes 2885207 | solution.py:127
  244.2 1.4 convolution_add_fusion.8
  247.0 1.4 convolution_add_fusion.8
  249.9 1.4 convolution_add_fusion.8
  252.8 1.4 convolution_add_fusion.8
  255.6 1.4 convolution_add_fusion.8
  258.5 1.4 convolution_add_fusion.8
  261.3 1.4 convolution_add_fusion.8
  264.2 1.4 convolution_add_fusion.8
  267.1 27.5 %while.35 = (s32[]{:T(128)}, f32[4,128,128]{2,1,0:T(8,128)S(1)}, f32[4,128,128]{2,1,0:T(8,128)S(1)}, f32[4,128,128]{2,1,0:T(8,128)S(1)}, s32[]{:T(128)}) while((s32[]{:T(128)}, f32[4,128,128]{2,1,0:T(8,128)S(1)}, f32[4,128,128]{2,1,0:T(8,128)S(1)}, f32[4,128,128]{2,1,0:T(8,128)S(1)}, s32[]{:T(128)}) %tuple.72), condition=%wide.region_5.6_spmd, body=%wide.region_4.5_spmd.sunk | while | flops 100728832 | bytes 2097253 | solution.py:132
  268.8 6.0 %collective-permute-done = f32[4,128,128]{2,1,0:T(8,128)S(1)} collective-permute-done((f32[4,128,128]{2,1,0:T(8,128)S(1)}, f32[4,128,128]{2,1,0:T(8,128)S(1)}, u32[]{:S(2)}, u32[]{:S(2)}) %collective-permute-start) | collective-permute-done | bytes 262176 | tf_op jit(solution)/shard_map/while/body/eval_jaxpr/ppermute | solution.py:13
  275.2 4.4 %collective-permute-start = (f32[4,128,128]{2,1,0:T(8,128)S(1)}, f32[4,128,128]{2,1,0:T(8,128)S(1)}, u32[]{:S(2)}, u32[]{:S(2)}) collective-permute-start(f32[4,128,128]{2,1,0:T(8,128)S(1)} %convolution_add_fusion.6), channel_id=1, source_target_pairs={{0,8},{8,16},{16,24},{1,9},{9,17},{17,25},{2,10},{10,18},{18,26},{... | collective-permute-start | bytes 786440 | tf_op jit(solution)/shard_map/while/body/eval_jaxpr/ppermute | solution.py:13
  279.7 6.2 %collective-permute-done = f32[4,128,128]{2,1,0:T(8,128)S(1)} collective-permute-done((f32[4,128,128]{2,1,0:T(8,128)S(1)}, f32[4,128,128]{2,1,0:T(8,128)S(1)}, u32[]{:S(2)}, u32[]{:S(2)}) %collective-permute-start) | collective-permute-done | bytes 262176 | tf_op jit(solution)/shard_map/while/body/eval_jaxpr/ppermute | solution.py:13
  286.2 4.4 %collective-permute-start = (f32[4,128,128]{2,1,0:T(8,128)S(1)}, f32[4,128,128]{2,1,0:T(8,128)S(1)}, u32[]{:S(2)}, u32[]{:S(2)}) collective-permute-start(f32[4,128,128]{2,1,0:T(8,128)S(1)} %convolution_add_fusion.6), channel_id=1, source_target_pairs={{0,8},{8,16},{16,24},{1,9},{9,17},{17,25},{2,10},{10,18},{18,26},{... | collective-permute-start | bytes 786440 | tf_op jit(solution)/shard_map/while/body/eval_jaxpr/ppermute | solution.py:13
  290.7 3.9 %collective-permute-done = f32[4,128,128]{2,1,0:T(8,128)S(1)} collective-permute-done((f32[4,128,128]{2,1,0:T(8,128)S(1)}, f32[4,128,128]{2,1,0:T(8,128)S(1)}, u32[]{:S(2)}, u32[]{:S(2)}) %collective-permute-start) | collective-permute-done | bytes 262176 | tf_op jit(solution)/shard_map/while/body/eval_jaxpr/ppermute | solution.py:13
  294.5 17.6 %while.36 = (s32[]{:T(128)}, f32[4,128,128]{2,1,0:T(8,128)S(1)}, f32[8,4,128,128]{3,2,1,0:T(8,128)}, f32[8,4,128,128]{3,2,1,0:T(8,128)}, f32[8,4,128,128]{3,2,1,0:T(8,128)}, /*index=5*/s32[]{:T(128)}) while((s32[]{:T(128)}, f32[4,128,128]{2,1,0:T(8,128)S(1)}, f32[8,4,128,128]{3,2,1,0:T(8,128)}, f32[8,4,128,128]{3,2,1,0:T(8,128)}, ...), condition=%wide.region_7.8_spmd, body=%wide.region_6.7_spmd.sunk | while | flops 100728832 | bytes 2098757 | solution.py:138
  297.5 1.4 convolution_add_fusion.7
  301.8 1.4 convolution_add_fusion.7
  306.2 1.4 convolution_add_fusion.7
  312.1 5.2 %fusion.25 = f32[4,8,64,128]{3,2,1,0:T(8,128)} fusion(f32[4,8,64,256]{3,2,1,0:T(8,128)} %copy-done.1, f32[8,4,128,128]{3,2,1,0:T(8,128)} %get-tuple-element.85), kind=kOutput, calls=%fused_computation.29 | convolution fusion | flops 402915328 | bytes 5242880 | tf_op jit(solution)/shard_map/...ij,...jk->...ik/dot_general | solution.py:17
  318.2 1.6 fusion.59
  319.8 1.6 reshape.118
  321.4 2.2 convolution_select_fusion
  325.2 2.3 fusion.36
  328.9 3.5 %all-to-all-start.5 = ((bf16[4,128,512]{2,1,0:T(8,128)(2,1)}), bf16[4,128,512]{2,1,0:T(8,128)(2,1)S(1)}, u32[]{:S(2)}, u32[]{:S(2)}) async-start(bf16[4,128,512]{2,1,0:T(8,128)(2,1)} %convert_element_type.98), calls=%async_computation.5 | async-start | bytes 1048576 | tf_op jit(solution)/shard_map/all_to_all | solution.py:147
  333.4 5.5 %all-to-all-done.5 = bf16[4,128,512]{2,1,0:T(8,128)(2,1)S(1)} async-done(((bf16[4,128,512]{2,1,0:T(8,128)(2,1)}), bf16[4,128,512]{2,1,0:T(8,128)(2,1)S(1)}, u32[]{:S(2)}, u32[]{:S(2)}) %all-to-all-start.5) | async-done | bytes 524320 | tf_op jit(solution)/shard_map/all_to_all | solution.py:147
  (146 shorter events, 47.9 us)
Async XLA Ops:
  0.0 333.4 %copy-start = (f32[128]{0:T(128)S(1)}, f32[128]{0:T(128)}, u32[]{:S(2)}) copy-start(f32[128]{0:T(128)} %param.21) | copy-start | bytes 1540
  0.0 13.5 %copy-start.8 = (bf16[128,2048]{1,0:T(8,128)(2,1)S(1)}, bf16[128,2048]{1,0:T(8,128)(2,1)}, u32[]{:S(2)}) copy-start(bf16[128,2048]{1,0:T(8,128)(2,1)} %param.16) | copy-start | bytes 1572868
  0.0 10.0 %all-to-all-start.3 = ((bf16[128,4,4]{0,2,1:T(4,128)(2,1)}), bf16[128,4,4]{0,2,1:T(4,128)(2,1)S(1)}, u32[]{:S(2)}, u32[]{:S(2)}) async-start(bf16[128,4,4]{0,2,1:T(4,128)(2,1)} %bitcast.165), calls=%async_computation.3 | async-start | bytes 8192 | tf_op jit(solution)/shard_map/all_to_all | solution.py:78
  5.3 18.5 %copy-start.9 = (bf16[128,2048]{1,0:T(8,128)(2,1)S(1)}, bf16[128,2048]{1,0:T(8,128)(2,1)}, u32[]{:S(2)}) copy-start(bf16[128,2048]{1,0:T(8,128)(2,1)} %param.17) | copy-start | bytes 1572868
  10.0 10.4 %all-to-all-start.2 = ((bf16[128,4,512]{0,2,1:T(8,128)(2,1)}), bf16[128,4,512]{0,2,1:T(8,128)(2,1)S(1)}, u32[]{:S(2)}, u32[]{:S(2)}) async-start(bf16[128,4,512]{0,2,1:T(8,128)(2,1)} %bitcast.16), calls=%async_computation.2 | async-start | bytes 1048576 | tf_op jit(solution)/shard_map/all_to_all | solution.py:75
  13.5 20.4 %copy-start.10 = (bf16[128,2048]{1,0:T(8,128)(2,1)S(1)}, bf16[128,2048]{1,0:T(8,128)(2,1)}, u32[]{:S(2)}) copy-start(bf16[128,2048]{1,0:T(8,128)(2,1)} %param.14) | copy-start | bytes 1572868
  20.3 10.0 %all-to-all-start.4 = ((bf16[128,4,512]{0,2,1:T(8,128)(2,1)}), bf16[128,4,512]{0,2,1:T(8,128)(2,1)S(1)}, u32[]{:S(2)}, u32[]{:S(2)}) async-start(bf16[128,4,512]{0,2,1:T(8,128)(2,1)} %bitcast.30), calls=%async_computation.4 | async-start | bytes 1048576 | tf_op jit(solution)/shard_map/all_to_all | solution.py:76
  30.4 13.9 %all-to-all-start.1 = ((bf16[128,4,512]{2,0,1:T(8,128)(2,1)}), bf16[128,4,512]{2,0,1:T(8,128)(2,1)S(1)}, u32[]{:S(2)}, u32[]{:S(2)}) async-start(bf16[128,4,512]{2,0,1:T(8,128)(2,1)} %bitcast.118), calls=%async_computation.1 | async-start | bytes 1048576 | tf_op jit(solution)/shard_map/all_to_all | solution.py:77
  35.8 23.6 %collective-permute-start.2 = (bf16[3,512]{1,0:T(4,128)(2,1)}, bf16[3,512]{1,0:T(4,128)(2,1)}, u32[]{:S(2)}, u32[]{:S(2)}) collective-permute-start(bf16[3,512]{1,0:T(4,128)(2,1)} %slice.157), channel_id=1, source_target_pairs={{0,8},{8,16},{16,24},{1,9},{9,17},{17,25},{2,10},{10,18},{18,26},{... | collective-permute-start | bytes 9224 | tf_op jit(solution)/shard_map/ppermute | solution.py:13
  40.1 4.1 %copy-start.6 = (bf16[4,128,512]{2,1,0:T(8,128)(2,1)}, bf16[4,128,512]{2,1,0:T(8,128)(2,1)S(1)}, u32[]{:S(2)}) copy-start(bf16[4,128,512]{2,1,0:T(8,128)(2,1)S(1)} %copy.48) | copy-start | bytes 1572868
  40.8 20.9 %collective-permute-start.3 = (bf16[3,512]{1,0:T(4,128)(2,1)}, bf16[3,512]{1,0:T(4,128)(2,1)}, u32[]{:S(2)}, u32[]{:S(2)}) collective-permute-start(bf16[3,512]{1,0:T(4,128)(2,1)} %slice.162), channel_id=1, source_target_pairs={{0,8},{8,16},{16,24},{1,9},{9,17},{17,25},{2,10},{10,18},{18,26},{... | collective-permute-start | bytes 9224 | tf_op jit(solution)/shard_map/ppermute | solution.py:13
  44.3 10.7 %all-to-all-start = ((bf16[128,4,512]{0,2,1:T(8,128)(2,1)}), bf16[128,4,512]{0,2,1:T(8,128)(2,1)S(1)}, u32[]{:S(2)}, u32[]{:S(2)}) async-start(bf16[128,4,512]{0,2,1:T(8,128)(2,1)} %bitcast.4), calls=%async_computation | async-start | bytes 1048576 | tf_op jit(solution)/shard_map/all_to_all | solution.py:74
  55.2 5.0 %copy-start.4 = (bf16[4,128,512]{2,1,0:T(8,128)(2,1)}, bf16[4,128,512]{2,1,0:T(8,128)(2,1)S(1)}, u32[]{:S(2)}) copy-start(bf16[4,128,512]{2,1,0:T(8,128)(2,1)S(1)} %copy.36) | copy-start | bytes 1572868
  55.9 261.4 %collective-permute-start.1 = (bf16[3,512]{1,0:T(4,128)(2,1)}, bf16[3,512]{1,0:T(4,128)(2,1)}, u32[]{:S(2)}, u32[]{:S(2)}) collective-permute-start(bf16[3,512]{1,0:T(4,128)(2,1)} %slice.151), channel_id=1, source_target_pairs={{0,8},{8,16},{16,24},{1,9},{9,17},{17,25},{2,10},{10,18},{18,26},{... | collective-permute-start | bytes 9224 | tf_op jit(solution)/shard_map/ppermute | solution.py:13
  61.2 1.6 copy-start.19
  61.3 1.6 copy-start.20
  61.3 1.6 copy-start.21
  61.3 1.6 copy-start.22
  64.9 2.6 copy-start.12
  64.9 2.6 copy-start.13
  64.9 2.6 copy-start.14
  64.9 2.6 copy-start.15
  232.9 5.4 %copy-start.1 = (f32[4,8,64,256]{3,2,1,0:T(8,128)}, f32[4,8,64,256]{3,2,1,0:T(8,128)S(1)}, u32[]{:S(2)}) copy-start(f32[4,8,64,256]{3,2,1,0:T(8,128)S(1)} %fusion.14) | copy-start | bytes 6291460
  267.5 7.4 %collective-permute-start = (f32[4,128,128]{2,1,0:T(8,128)S(1)}, f32[4,128,128]{2,1,0:T(8,128)S(1)}, u32[]{:S(2)}, u32[]{:S(2)}) collective-permute-start(f32[4,128,128]{2,1,0:T(8,128)S(1)} %convolution_add_fusion.6), channel_id=1, source_target_pairs={{0,8},{8,16},{16,24},{1,9},{9,17},{17,25},{2,10},{10,18},{18,26},{... | collective-permute-start | bytes 786440 | tf_op jit(solution)/shard_map/while/body/eval_jaxpr/ppermute | solution.py:13
  275.2 10.6 %collective-permute-start = (f32[4,128,128]{2,1,0:T(8,128)S(1)}, f32[4,128,128]{2,1,0:T(8,128)S(1)}, u32[]{:S(2)}, u32[]{:S(2)}) collective-permute-start(f32[4,128,128]{2,1,0:T(8,128)S(1)} %convolution_add_fusion.6), channel_id=1, source_target_pairs={{0,8},{8,16},{16,24},{1,9},{9,17},{17,25},{2,10},{10,18},{18,26},{... | collective-permute-start | bytes 786440 | tf_op jit(solution)/shard_map/while/body/eval_jaxpr/ppermute | solution.py:13
  286.2 8.3 %collective-permute-start = (f32[4,128,128]{2,1,0:T(8,128)S(1)}, f32[4,128,128]{2,1,0:T(8,128)S(1)}, u32[]{:S(2)}, u32[]{:S(2)}) collective-permute-start(f32[4,128,128]{2,1,0:T(8,128)S(1)} %convolution_add_fusion.6), channel_id=1, source_target_pairs={{0,8},{8,16},{16,24},{1,9},{9,17},{17,25},{2,10},{10,18},{18,26},{... | collective-permute-start | bytes 786440 | tf_op jit(solution)/shard_map/while/body/eval_jaxpr/ppermute | solution.py:13
  312.1 5.3 %copy-start.5 = (bf16[4,128,512]{2,1,0:T(8,128)(2,1)S(1)}, bf16[4,128,512]{2,1,0:T(8,128)(2,1)}, u32[]{:S(2)}) copy-start(bf16[4,128,512]{2,1,0:T(8,128)(2,1)} %copy-done.4) | copy-start | bytes 1572868
  312.1 6.1 %copy-start.16 = (f32[1,1,512]{2,1,0:T(1,128)S(1)}, f32[1,1,512]{2,1,0:T(1,128)}, u32[]{:S(2)}) copy-start(f32[1,1,512]{2,1,0:T(1,128)} %get-tuple-element.172) | copy-start | bytes 6148
  312.1 6.1 %copy-start.17 = (f32[1,1,512]{2,1,0:T(1,128)S(1)}, f32[1,1,512]{2,1,0:T(1,128)}, u32[]{:S(2)}) copy-start(f32[1,1,512]{2,1,0:T(1,128)} %get-tuple-element.173) | copy-start | bytes 6148
  312.1 6.1 %copy-start.18 = (f32[1,1,512]{2,1,0:T(1,128)S(1)}, f32[1,1,512]{2,1,0:T(1,128)}, u32[]{:S(2)}) copy-start(f32[1,1,512]{2,1,0:T(1,128)} %get-tuple-element.174) | copy-start | bytes 6148
  321.4 2.2 copy-start.3
  323.6 1.6 copy-start.2
  327.4 4.9 %copy-start.11 = (bf16[128,2048]{1,0:T(8,128)(2,1)S(1)}, bf16[128,2048]{1,0:T(8,128)(2,1)}, u32[]{:S(2)}) copy-start(bf16[128,2048]{1,0:T(8,128)(2,1)} %param.20) | copy-start | bytes 1572868
  328.9 10.0 %all-to-all-start.5 = ((bf16[4,128,512]{2,1,0:T(8,128)(2,1)}), bf16[4,128,512]{2,1,0:T(8,128)(2,1)S(1)}, u32[]{:S(2)}, u32[]{:S(2)}) async-start(bf16[4,128,512]{2,1,0:T(8,128)(2,1)} %convert_element_type.98), calls=%async_computation.5 | async-start | bytes 1048576 | tf_op jit(solution)/shard_map/all_to_all | solution.py:147
  339.4 1.0 copy-start.7
where the time goes:
time: 343 us; the launch traced here: 342 us
  other arithmetic  170 us (50%)
  matrix products  60.5 us (18%)
  starting transfers between devices  44.5 us (13%)
  waiting for transfers between devices  38.1 us (11%)
  local copies, waits for them, and re-layouts  27.3 us (8%)
    another operation x2, other arithmetic, block_terms(): lax.linalg.triangular_solve(unit_lower, right_side, left_side=True, lower...  159 us
    dot_general x30, matrix products, matmul(): jnp.einsum('...ij,...jk->...ik', left, right, precision=lax.Precision.HIG...  43.4 us
    ppermute x6, starting transfers between devices, shifted(): return lax.ppermute(block, axis, route)  21.2 us
    ppermute x6, waiting for transfers between devices, shifted(): return lax.ppermute(block, axis, route)  16 us
    unnamed x52, local copies, waits for them, and re-layouts  9.18 us
  transfers between devices with their start and end apart: 12, of which 8 were waited for; matrix products, arithmetic and copies ran while one was open for 71% of the time, Pallas kernels for 0%

commit v1 on v0

v1 whole, which is shorter than its diff:
```python
import functools

import jax
import jax.numpy as jnp
from jax import lax
from jax.experimental import pallas as pl
from jax.experimental.pallas import tpu as pltpu
from jax.sharding import PartitionSpec as P

D = 128
SUB = 16
EDGE = 16
F32 = jnp.float32
BF16 = jnp.bfloat16
VMEM_LIMIT = 48 * 1024 * 1024


def dot(a, b):
    return jnp.dot(a, b, preferred_element_type=F32)


def dot_t(a, b):
    return lax.dot_general(a, b, (((1,), (1,)), ((), ())), preferred_element_type=F32)


def t_dot(a, b):
    return lax.dot_general(a, b, (((0,), (0,)), ((), ())), preferred_element_type=F32)


def split(x):
    hi = x.astype(BF16)
    return hi, (x - hi.astype(F32)).astype(BF16)


def dot3(a, b):
    a_hi, a_lo = a
    b_hi, b_lo = b
    rows = a_hi.shape[0]
    both = dot(jnp.concatenate([a_hi, a_lo], 0), b_hi)
    return both[:rows] + both[rows:] + dot(a_hi, b_lo)


def silu(u):
    return u / (1.0 + jnp.exp(-u))


def conv(x, taps):
    width = taps.shape[0]
    total = x * taps[width - 1 : width]
    for back in range(1, width):
        total = total + pltpu.roll(x, back, 0) * taps[width - 1 - back : width - back]
    return silu(total).astype(BF16).astype(F32)


def key_terms(keys, rates, up, down, mid, end):
    norm = lax.rsqrt(jnp.sum(keys * keys, -1, keepdims=True) + 1e-6)
    unit = keys * norm
    write = unit * rates * up
    write_hi, write_lo = split(write)
    low = unit * down
    low_hi, low_lo = split(low)
    return write_hi, write_lo, low_hi, low_lo, (write * mid).astype(BF16), (low * end).astype(BF16)


def iota(shape, dim):
    return lax.broadcasted_iota(jnp.int32, shape, dim)


def prepare_kernel(
    q_ref, k_ref, v_ref, g_ref, beta_ref, taps_ref,
    whi_ref, wlo_ref, lhi_ref, llo_ref, kin_ref, kend_ref, vb_ref, qup_ref, up_ref, down_ref, marks_ref,
):
    rows, cols = q_ref.shape
    heads = cols // D
    middle = rows // 2 - 1
    at, other = iota((rows, rows), 0), iota((rows, rows), 1)
    plus = jnp.where((other <= at) & (other > middle), 1.0, 0.0)
    minus = jnp.where((other > at) & (other <= middle), 1.0, 0.0)
    sums = dot((plus - minus).astype(BF16), g_ref[...])
    up = jnp.exp(sums)
    down = jnp.exp(-sums)
    up_ref[...] = up
    down_ref[...] = down
    mid = jnp.exp(g_ref[0:16, :].astype(F32)[0:1] - sums[0:1])
    end = up[rows - 1 : rows]
    marks_ref[...] = jnp.concatenate([mid, end] * 4, 0)
    qup_ref[...] = (conv(q_ref[...].astype(F32), taps_ref[0]) * up).astype(BF16)
    values = conv(v_ref[...].astype(F32), taps_ref[2])
    keys = conv(k_ref[...].astype(F32), taps_ref[1])
    base = pl.program_id(0) * heads
    rates = beta_ref[...].astype(F32)
    lane = iota(rates.shape, 1)
    for h in range(heads):
        c = slice(h * D, (h + 1) * D)
        rate = jnp.sum(jnp.where(lane == base + h, rates, 0.0), -1, keepdims=True)
        out = key_terms(keys[:, c], rate, up[:, c], down[:, c], mid[:, c], end[:, c])
        for ref, value in zip((whi_ref, wlo_ref, lhi_ref, llo_ref, kin_ref, kend_ref), out):
            ref[:, c] = value
        vb_ref[:, c] = (values[:, c] * rate).astype(BF16)


def edge_rows(rim, which, raw_ref, taps):
    width = taps.shape[0]
    first = which * (width - 1)
    before = pltpu.roll(rim, (8 - (width - 1) - first) % rim.shape[0], 0)[0:8]
    return conv(jnp.concatenate([before, raw_ref[...].astype(F32)], 0), taps)[8:]


def solve_heads(lows, rows):
    lane_sub = iota((SUB, rows), 1)
    blocks = rows // SUB
    at, other = iota((rows, rows), 0), iota((rows, rows), 1)
    same = (at // SUB) == (other // SUB)
    packed = []
    for low in lows:
        own = jnp.where(same, low, 0.0)
        total = own[0:SUB]
        for b in range(1, blocks):
            total = total + own[b * SUB : (b + 1) * SUB]
        packed.append(total)
    unit = jnp.where(lane_sub % SUB == iota((SUB, rows), 0), 1.0, 0.0)
    solved = [unit for _ in lows]
    group_start = lane_sub - lane_sub % SUB
    for j in range(SUB - 1):
        for n, total in enumerate(packed):
            spread = jnp.take_along_axis(total, group_start + j, axis=1, mode="promise_in_bounds")
            solved[n] = solved[n] - spread * solved[n][j : j + 1]
    full = [jnp.where(same, jnp.concatenate([x] * blocks, 0), 0.0) for x in solved]
    size = SUB
    while size < rows:
        mask = (at // (2 * size) == other // (2 * size)) & (at // size != other // size)
        lower = [slice(p * size, (p + 1) * size) for p in range(1, rows // size, 2)]
        take = lambda x: jnp.concatenate([x[s] for s in lower], 0)
        small_mask = take(mask)
        parts = [split(x) for x in full]
        links = [split(jnp.where(small_mask, take(low), 0.0)) for low in lows]
        inner = [dot3(link, part) for link, part in zip(links, parts)]
        zeros = jnp.zeros((size, rows), F32)
        spread = []
        for x in inner:
            pieces = []
            for p in range(rows // (2 * size)):
                pieces += [zeros, x[p * size : (p + 1) * size]]
            spread.append(split(jnp.concatenate(pieces, 0)))
        fixes = [dot3((take(part[0]), take(part[1])), s) for part, s in zip(parts, spread)]
        result = []
        for x, fix in zip(full, fixes):
            pieces = []
            for p in range(rows // (2 * size)):
                pieces += [
                    x[2 * p * size : (2 * p + 1) * size],
                    x[(2 * p + 1) * size : (2 * p + 2) * size] - fix[p * size : (p + 1) * size],
                ]
            result.append(jnp.concatenate(pieces, 0))
        full = result
        size *= 2
    return full


def block_kernel(
    group_ref, rim_ref, k_ref, v_ref, beta_ref, taps_ref, up_ref, down_ref, marks_ref,
    whi_ref, wlo_ref, lhi_ref, llo_ref, kin_ref, kend_ref, vb_ref,
    move_ref, rows_ref, low_ref,
):
    rows, cols = whi_ref.shape
    heads = cols // D
    rim = rim_ref[...].astype(F32)
    keys = edge_rows(rim, 1, k_ref, taps_ref[1])
    values = edge_rows(rim, 2, v_ref, taps_ref[2])
    rates = beta_ref[...].astype(F32)
    lane = iota(rates.shape, 1)
    base = group_ref[0] * heads
    at, other = iota((rows, rows), 0), iota((rows, rows), 1)
    lows, ends, sides = [], [], []
    for h in range(heads):
        c = slice(h * D, (h + 1) * D)
        rate = jnp.sum(jnp.where(lane == base + h, rates, 0.0), -1, keepdims=True)
        mid, end = marks_ref[0:1, c], marks_ref[1:2, c]
        edge = key_terms(keys[:, c], rate, up_ref[:, c], down_ref[:, c], mid, end)
        whole = [
            jnp.concatenate([e, ref[EDGE:, c]], 0)
            for e, ref in zip(edge, (whi_ref, wlo_ref, lhi_ref, llo_ref, kin_ref, kend_ref))
        ]
        vb = jnp.concatenate([(values[:, c] * rate).astype(BF16), vb_ref[EDGE:, c]], 0)
        whi, wlo, lhi, llo, kin, kend = whole
        low_ref[:, c] = lhi
        both = dot_t(jnp.concatenate([whi, wlo], 0), lhi)
        inner = both[:rows] + both[rows:] + dot_t(whi, llo)
        lows.append(jnp.where(at > other, inner, 0.0))
        ends.append(kend)
        sides.append(jnp.concatenate([kin, vb], 1))
    solved = solve_heads(lows, rows)
    made = [dot(t.astype(BF16), side).astype(BF16) for t, side in zip(solved, sides)]
    for h in range(heads):
        c = slice(h * D, (h + 1) * D)
        sums = t_dot(ends[h], made[h])
        fade = marks_ref[0:1, c] * marks_ref[1:2, c] - 1.0
        move = jnp.where(at == other, fade, 0.0) - sums[:, :D]
        rows_ref[h] = made[h]
        move_ref[h, :, :D] = move.astype(BF16)
        move_ref[h, :, D:] = sums[:, D:].astype(BF16)


def local_kernel(
    group_ref, rim_ref, q_ref, taps_ref, up_ref, marks_ref, qup_ref, low_ref, rows_ref, gate_ref, gain_ref,
    reach_ref, own_ref, scale_ref,
):
    rows, cols = qup_ref.shape
    heads = cols // D
    rim = rim_ref[...].astype(F32)
    edge = (edge_rows(rim, 0, q_ref, taps_ref[0]) * up_ref[...]).astype(BF16)
    at, other = iota((rows, rows), 0), iota((rows, rows), 1)
    for h in range(heads):
        c = slice(h * D, (h + 1) * D)
        qup = jnp.concatenate([edge[:, c], qup_ref[EDGE:, c]], 0)
        scores = jnp.where(at >= other, dot_t(qup, low_ref[:, c]), 0.0).astype(BF16)
        seen = dot(scores, rows_ref[h])
        reach_ref[:, c] = (qup.astype(F32) * marks_ref[0:1, c] - seen[:, :D]).astype(BF16)
        own_ref[:, c] = seen[:, D:]
        gate = gate_ref[:, c].astype(F32)
        scale_ref[:, c] = gain_ref[...] / (1.0 + jnp.exp(-gate))


def compose_kernel(me_ref, *refs):
    pieces, (before_ref, whole_ref) = refs[:-2], refs[-2:]
    count = len(pieces)
    heads = whole_ref.shape[0]
    for m in range(count):

        @pl.when(me_ref[0] == m)
        def _():
            order = [pieces[m ^ b] for b in range(count)]
            run = [order[0][h].astype(F32) for h in range(heads)]
            for b in range(1, count):
                for h in range(heads):
                    now = run[h].astype(BF16)
                    before_ref[b - 1, h] = now
                    step = order[b][h]
                    run[h] = run[h] + step.astype(F32) + dot(step[:, :D], now)
            for h in range(heads):
                whole_ref[h] = run[h].astype(BF16)


def absorb_kernel(count, wide, last, *refs):
    parts, rest = refs[:count], refs[count:]
    have_ref = rest[0] if wide else None
    own_ref = rest[1] if wide else rest[0]
    outs = rest[2:] if wide else rest[1:]
    heads = own_ref.shape[0]
    for h in range(heads):
        now = parts[0][h]
        for ref in parts[1:]:
            now = now + ref[h]
        if wide:
            have = have_ref[h]
            now = (have.astype(F32) + now.astype(F32) + dot(have[:, :D], now)).astype(BF16)
            outs[1][h] = now
        own = own_ref[h]
        send = now[:, D:] if last else now
        after = send.astype(F32) + (own[:, D:] if last else own).astype(F32) + dot(own[:, :D], send)
        outs[0][h] = after.astype(BF16)


def starts_kernel(count, me_ref, *refs):
    came_refs, have_ref, before_ref, outs = refs[:count], refs[count], refs[count + 1], refs[count + 2 :]
    heads = have_ref.shape[0]
    first = []
    for h in range(heads):
        came = came_refs[0][h]
        for ref in came_refs[1:]:
            came = came + ref[h]
        have = have_ref[h]
        first.append(have[:, D:].astype(F32) + came.astype(F32) + dot(have[:, :D], came))
    later = []
    for b in range(1, len(outs)):
        for h in range(heads):
            known = before_ref[b - 1, h]
            later.append(
                (first[h] + known[:, D:].astype(F32) + dot(known[:, :D], first[h].astype(BF16))).astype(BF16)
            )
    for m in range(len(outs)):

        @pl.when(me_ref[0] == m)
        def _():
            for b in range(len(outs)):
                for h in range(heads):
                    outs[m ^ b][h] = first[h].astype(BF16) if b == 0 else later[(b - 1) * heads + h]


def finish_kernel(count, me_ref, *refs):
    out_ref = refs[-1]
    reach, own, scale, starts = (refs[k * count : (k + 1) * count] for k in range(4))
    heads = starts[0].shape[0]
    for m in range(count):

        @pl.when(me_ref[0] == m)
        def _():
            for g in range(count):
                j = m ^ g
                for h in range(heads):
                    c = slice(h * D, (h + 1) * D)
                    found = own[j][:, c] + dot(reach[j][:, c], starts[j][h])
                    found = found.astype(BF16).astype(F32)
                    mean = jnp.mean(found * found, -1, keepdims=True)
                    at = slice((g * heads + h) * D, (g * heads + h + 1) * D)
                    out_ref[:, at] = (found * lax.rsqrt(mean + 1e-5) * scale[j][:, c]).astype(BF16)


def params():
    return pltpu.CompilerParams(vmem_limit_bytes=VMEM_LIMIT)


def shards(query_raw, key_raw, value_raw, log_decay, beta, conv_weight, out_gate, norm_gain):
    rows, width = query_raw.shape
    groups = lax.axis_size("head")
    spans = lax.axis_size("ctx")
    cols = width // groups
    heads = cols // D
    rim_width = conv_weight.shape[1] - 1
    me = lax.axis_index("head")
    me_arg = me.reshape(1).astype(jnp.int32)

    tails = jnp.concatenate(
        [query_raw[-rim_width:], key_raw[-rim_width:], value_raw[-rim_width:]]
        + [jnp.zeros((16 - 3 * rim_width, width), BF16)],
        0,
    )
    total = groups * spans
    rim = lax.ppermute(tails, ("ctx", "head"), [(i, i + 1) for i in range(total - 1)])

    column = lambda i: (0, i)
    whole_block = pl.BlockSpec((rows, cols), column)
    taps_block = pl.BlockSpec(conv_weight.shape[:2] + (cols,), lambda i: (0, 0, i))
    wide16 = jax.ShapeDtypeStruct((rows, width), BF16)
    wide32 = jax.ShapeDtypeStruct((rows, width), F32)
    prepared = pl.pallas_call(
        prepare_kernel,
        grid=(groups,),
        in_specs=[whole_block] * 4 + [pl.BlockSpec(beta.shape, lambda i: (0, 0)), taps_block],
        out_specs=[whole_block] * 10 + [pl.BlockSpec((8, cols), column)],
        out_shape=[wide16] * 8 + [wide32] * 2 + [jax.ShapeDtypeStruct((8, width), F32)],
        compiler_params=params(),
        cost_estimate=pl.CostEstimate(flops=20_000_000, bytes_accessed=9_000_000, transcendentals=2_000_000),
        name="prepare",
    )(query_raw, key_raw, value_raw, log_decay, beta, conv_weight)
    whi, wlo, lhi, llo, kin, kend, vb, qup, up, down, marks = prepared

    dyn = lambda i, g: (0, g[0])
    edge_block = pl.BlockSpec((EDGE, cols), dyn)
    rows_block = pl.BlockSpec((rows, cols), dyn)
    marks_block = pl.BlockSpec((8, cols), dyn)
    taps_dyn = pl.BlockSpec(conv_weight.shape[:2] + (cols,), lambda i, g: (0, 0, g[0]))
    head_block = pl.BlockSpec((heads, rows, 2 * D), lambda i, g: (0, 0, 0))
    still = pl.BlockSpec((rows, cols), lambda i, g: (0, 0))
    moves, made, lows = [None] * groups, [None] * groups, [None] * groups
    order = list(range(groups - 1, -1, -1))
    for j in order:
        moves[j], made[j], lows[j] = pl.pallas_call(
            block_kernel,
            grid_spec=pltpu.PrefetchScalarGridSpec(
                num_scalar_prefetch=1,
                grid=(1,),
                in_specs=[
                    edge_block, edge_block, edge_block,
                    pl.BlockSpec((EDGE, beta.shape[1]), lambda i, g: (0, 0)),
                    taps_dyn, edge_block, edge_block, marks_block,
                ]
                + [rows_block] * 7,
                out_specs=[head_block, head_block, still],
            ),
            out_shape=[
                jax.ShapeDtypeStruct((heads, D, 2 * D), BF16),
                jax.ShapeDtypeStruct((heads, rows, 2 * D), BF16),
                jax.ShapeDtypeStruct((rows, cols), BF16),
            ],
            compiler_params=params(),
            name="block",
        )(me_arg ^ j, rim, key_raw, value_raw, beta, conv_weight, up, down, marks, whi, wlo, lhi, llo, kin, kend, vb)

    def swap(array, j):
        return lax.ppermute(array, "head", [(i, i ^ j) for i in range(groups)])

    came = [moves[0]] + [None] * (groups - 1)
    for j in order[:-1]:
        came[j] = swap(moves[j], j)

    local = []
    for j in range(groups):
        local.append(
            pl.pallas_call(
                local_kernel,
                grid_spec=pltpu.PrefetchScalarGridSpec(
                    num_scalar_prefetch=1,
                    grid=(1,),
                    in_specs=[
                        edge_block, edge_block, taps_dyn, edge_block, marks_block, rows_block,
                        still, head_block, rows_block, pl.BlockSpec((1, D), lambda i, g: (0, 0)),
                    ],
                    out_specs=[still] * 3,
                ),
                out_shape=[
                    jax.ShapeDtypeStruct((rows, cols), BF16),
                    jax.ShapeDtypeStruct((rows, cols), F32),
                    jax.ShapeDtypeStruct((rows, cols), F32),
                ],
                compiler_params=params(),
                name="local",
            )(me_arg ^ j, rim, query_raw, conv_weight, up, marks, qup, lows[j], made[j], out_gate, norm_gain.reshape(1, D))
        )

    smem = pl.BlockSpec(memory_space=pltpu.SMEM)
    vmem = pl.BlockSpec(memory_space=pltpu.VMEM)
    pair = jax.ShapeDtypeStruct((heads, D, 2 * D), BF16)
    before, whole = pl.pallas_call(
        compose_kernel,
        in_specs=[smem] + [vmem] * groups,
        out_specs=[vmem, vmem],
        out_shape=[jax.ShapeDtypeStruct((groups - 1, heads, D, 2 * D), BF16), pair],
        compiler_params=params(),
        name="compose",
    )(me_arg, *came)

    state = jax.ShapeDtypeStruct((heads, D, D), BF16)
    have, send, half = None, whole if spans > 2 else whole[:, :, D:], 1
    parts = [jnp.zeros((heads, D, D), BF16)]
    while half < spans:
        parts = []
        for step in range(1, half + 1):
            route = [
                (low + half - 1, low + half - 1 + step)
                for low in range(0, spans, 2 * half)
                if low + half - 1 + step < spans
            ]
            parts.append(lax.ppermute(send, "ctx", route))
        half *= 2
        if half < spans:
            wide, last = have is not None, 2 * half >= spans
            kept = [have] if wide else []
            got = pl.pallas_call(
                functools.partial(absorb_kernel, len(parts), wide, last),
                in_specs=[vmem] * (len(parts) + len(kept) + 1),
                out_specs=[vmem] * (1 + len(kept)),
                out_shape=[state if last else pair] + [pair] * len(kept),
                compiler_params=params(),
                name="absorb",
            )(*parts, *kept, whole)
            send, have = got[0], got[1] if wide else parts[0]
    if have is None:
        have = jnp.zeros((heads, D, 2 * D), BF16)

    starts = pl.pallas_call(
        functools.partial(starts_kernel, len(parts)),
        in_specs=[smem] + [vmem] * (len(parts) + 2),
        out_specs=[vmem] * groups,
        out_shape=[state] * groups,
        compiler_params=params(),
        name="starts",
    )(me_arg, *parts, have, before)
    starts = [starts[0]] + [swap(starts[j], j) for j in range(1, groups)]

    reach, own, scale = zip(*local)
    return pl.pallas_call(
        functools.partial(finish_kernel, groups),
        in_specs=[smem] + [vmem] * (4 * groups),
        out_specs=vmem,
        out_shape=wide16,
        compiler_params=params(),
        name="finish",
    )(me_arg, *reach, *own, *scale, *starts)


def solution(mesh):
    tokens = P(("dp", "ctx", "head"), None)
    placed = (tokens, tokens, tokens, tokens, tokens, P(), tokens, P())
    return jax.shard_map(shards, mesh=mesh, in_specs=placed, out_specs=tokens, check_vma=False)
```

time: 343 us -> 63.1 us (0.18)
  the two profiles are of different devices: /device:TPU:0 before, /device:TPU:24 now
where the time goes in v1:
time: 63.1 us; the launch traced here: 62.2 us
  Pallas kernels  22.7 us (36%)
  waiting for transfers between devices  18.9 us (30%)
  starting transfers between devices  14 us (22%)
  local copies, waits for them, and re-layouts  6.34 us (10%)
    ppermute x3, waiting for transfers between devices, shards(): parts.append(lax.ppermute(send, 'ctx', route))  13.7 us
    pallas_call x4, Pallas kernels, shards(): pl.pallas_call(block_kernel, grid_spec=pltpu.PrefetchScalarGridSpec(num_s...  11.1 us
    ppermute x6, starting transfers between devices, swap(): return lax.ppermute(array, 'head', [(i, i ^ j) for i in range(groups)])  7.23 us
    pallas_call x1, Pallas kernels, shards(): pl.pallas_call(prepare_kernel, grid=(groups,), in_specs=[whole_block] * 4...  5.96 us
    ppermute x6, waiting for transfers between devices, swap(): return lax.ppermute(array, 'head', [(i, i ^ j) for i in range(groups)])  5.15 us
    unnamed x21, local copies, waits for them, and re-layouts  3.91 us
    ppermute x1, starting transfers between devices, shards(): lax.ppermute(tails, ('ctx', 'head'), [(i, i + 1) for i in range(total - 1)])  3.39 us
    ppermute x3, starting transfers between devices, shards(): parts.append(lax.ppermute(send, 'ctx', route))  3.38 us
  transfers between devices with their start and end apart: 10, of which 5 were waited for; matrix products, arithmetic and copies ran while one was open for 0% of the time, Pallas kernels for 28%

profile of v1, /device:TPU:24, one launch (start us, length us, event | category | flops | bytes accessed | tf_op | source)
XLA Modules:
  0.0 62.2 jit_solution(12534387408150345209)
XLA Ops:
  0.0 0.8 %slice.10 = bf16[3,2048]{1,0:T(4,128)(2,1)S(1)} slice(bf16[128,2048]{1,0:T(8,128)(2,1)} %k_ref.9), slice={[125:128], [0:2048]} | slice | bytes 24576 | tf_op jit(solution)/shard_map/slice | solution.py:324
  0.8 0.8 %slice.11 = bf16[3,2048]{1,0:T(4,128)(2,1)S(1)} slice(bf16[128,2048]{1,0:T(8,128)(2,1)} %v_ref.9), slice={[125:128], [0:2048]} | slice | bytes 24576 | tf_op jit(solution)/shard_map/slice | solution.py:324
  1.5 0.0 copy-start.7
  1.6 0.8 %slice.9 = bf16[3,2048]{1,0:T(4,128)(2,1)S(1)} slice(bf16[128,2048]{1,0:T(8,128)(2,1)} %q_ref.9), slice={[125:128], [0:2048]} | slice | bytes 24576 | tf_op jit(solution)/shard_map/slice | solution.py:324
  2.4 0.1 pad.3.clone
  2.5 0.1 maximum_maximum_fusion
  2.5 3.4 %collective-permute-start = (bf16[16,2048]{1,0:T(8,128)(2,1)S(1)}, bf16[16,2048]{1,0:T(8,128)(2,1)S(1)}, u32[]{:S(2)}, u32[]{:S(2)}) collective-permute-start(bf16[16,2048]{1,0:T(8,128)(2,1)S(1)} %maximum_maximum_fusion), channel_id=1, source_target_pairs={{0,2},{2,4},{4,6},{6,8},{8,10},{10,12},{12,14},{14,16},{16,18},{18... | collective-permute-start | bytes 196616 | tf_op jit(solution)/shard_map/ppermute | solution.py:329
  5.9 0.0 copy-done.9
  5.9 0.1 copy.9.beta_ref
  6.1 0.0 copy-done.7
  6.1 0.0 copy-start.1
  6.1 1.0 %copy-done.1 = bf16[128,2048]{1,0:T(8,128)(2,1)S(1)} copy-done((bf16[128,2048]{1,0:T(8,128)(2,1)S(1)}, bf16[128,2048]{1,0:T(8,128)(2,1)}, u32[]{:S(2)}) %copy-start.1) | copy-done | bytes 524312
  7.1 1.0 %copy-done.3 = bf16[128,2048]{1,0:T(8,128)(2,1)S(1)} copy-done((bf16[128,2048]{1,0:T(8,128)(2,1)S(1)}, bf16[128,2048]{1,0:T(8,128)(2,1)}, u32[]{:S(2)}) %copy-start.3) | copy-done | bytes 524312
  8.2 1.0 %copy-done.4 = bf16[128,2048]{1,0:T(8,128)(2,1)S(1)} copy-done((bf16[128,2048]{1,0:T(8,128)(2,1)S(1)}, bf16[128,2048]{1,0:T(8,128)(2,1)}, u32[]{:S(2)}) %copy-start.4) | copy-done | bytes 524312
  9.2 6.0 %prepare.1 = (bf16[128,2048]{1,0:T(8,128)(2,1)S(1)}, bf16[128,2048]{1,0:T(8,128)(2,1)S(1)}, bf16[128,2048]{1,0:T(8,128)(2,1)S(1)}, bf16[128,2048]{1,0:T(8,128)(2...) custom-call(bf16[128,2048]{1,0:T(8,128)(2,1)S(1)} %copy-done.4, ...), custom_call_target="tpu_custom_call" | custom-call | flops 20000000 | bytes 9000000 | tf_op jit(solution)/shard_map/prepare/pallas_call | solution.py:336
  15.2 0.0 collective-permute-done.rim_ref
  15.2 2.8 %block.7 = (bf16[4,128,256]{2,1,0:T(8,128)(2,1)S(1)}, bf16[4,128,256]{2,1,0:T(8,128)(2,1)S(1)}, bf16[128,512]{1,0:T(8,128)(2,1)S(1)}) custom-call(s32[1]{0:T(128)S(6)} %xor.14.group_ref, bf16[16,2048]{1,0:T(8,128)(2,1)S(1)} %collective-permute-done.rim_ref, bf16[128,2048]{1,0:T(8,128)(2,1)S(1)} %copy-done.3, bf16[128,2048]{1,0:T(8,128)(2,1)S(1)} %copy-done.2, ...), custom_call_target="tpu_custom_call" | custom-call | tf_op jit(solution)/shard_map/block/pallas_call | solution.py:358
  18.0 0.4 collective-permute-start.3
  18.4 2.8 %block.6 = (bf16[4,128,256]{2,1,0:T(8,128)(2,1)S(1)}, bf16[4,128,256]{2,1,0:T(8,128)(2,1)S(1)}, bf16[128,512]{1,0:T(8,128)(2,1)S(1)}) custom-call(s32[1]{0:T(128)S(6)} %xor.13.group_ref, bf16[16,2048]{1,0:T(8,128)(2,1)S(1)} %collective-permute-done.rim_ref, bf16[128,2048]{1,0:T(8,128)(2,1)S(1)} %copy-done.3, bf16[128,2048]{1,0:T(8,128)(2,1)S(1)} %copy-done.2, ...), custom_call_target="tpu_custom_call" | custom-call | tf_op jit(solution)/shard_map/block/pallas_call | solution.py:358
  21.2 2.7 %collective-permute-start.2 = (bf16[4,128,256]{2,1,0:T(8,128)(2,1)S(1)}, bf16[4,128,256]{2,1,0:T(8,128)(2,1)S(1)}, u32[]{:S(2)}, u32[]{:S(2)}) collective-permute-start(bf16[4,128,256]{2,1,0:T(8,128)(2,1)S(1)} %get-tuple-element.79), channel_id=1, source_target_pairs={{0,4},{2,6},{4,0},{6,2},{1,5},{3,7},{5,1},{7,3},{8,12},{10,14},{12... | collective-permute-start | bytes 786440 | tf_op jit(solution)/shard_map/ppermute | solution.py:381
  23.8 2.8 %block.5 = (bf16[4,128,256]{2,1,0:T(8,128)(2,1)S(1)}, bf16[4,128,256]{2,1,0:T(8,128)(2,1)S(1)}, bf16[128,512]{1,0:T(8,128)(2,1)S(1)}) custom-call(s32[1]{0:T(128)S(6)} %xor.12.group_ref, bf16[16,2048]{1,0:T(8,128)(2,1)S(1)} %collective-permute-done.rim_ref, bf16[128,2048]{1,0:T(8,128)(2,1)S(1)} %copy-done.3, bf16[128,2048]{1,0:T(8,128)(2,1)S(1)} %copy-done.2, ...), custom_call_target="tpu_custom_call" | custom-call | tf_op jit(solution)/shard_map/block/pallas_call | solution.py:358
  26.6 0.6 collective-permute-start.1
  27.2 2.8 %block.4 = (bf16[4,128,256]{2,1,0:T(8,128)(2,1)S(1)}, bf16[4,128,256]{2,1,0:T(8,128)(2,1)S(1)}, bf16[128,512]{1,0:T(8,128)(2,1)S(1)}) custom-call(s32[1]{0:T(128)} %bitcast.group_ref.me_ref, bf16[16,2048]{1,0:T(8,128)(2,1)S(1)} %collective-permute-done.rim_ref, bf16[128,2048]{1,0:T(8,128)(2,1)S(1)} %copy-done.3, bf16[128,2048]{1,0:T(8,128)(2,1)S(1)} %copy-done.2, ...), custom_call_target="tpu_custom_call" | custom-call | tf_op jit(solution)/shard_map/block/pallas_call | solution.py:358
  30.0 0.0 collective-permute-done.3.refs_3_
  30.0 2.3 %collective-permute-done.2.refs_2_ = bf16[4,128,256]{2,1,0:T(8,128)(2,1)S(1)} collective-permute-done((bf16[4,128,256]{2,1,0:T(8,128)(2,1)S(1)}, bf16[4,128,256]{2,1,0:T(8,128)(2,1)S(1)}, u32[]{:S(2)}, u32[]{:S(2)}) %collective-permute-start.2) | collective-permute-done | bytes 262176 | tf_op jit(solution)/shard_map/ppermute | solution.py:381
  32.3 1.6 %collective-permute-done.1.refs_1_ = bf16[4,128,256]{2,1,0:T(8,128)(2,1)S(1)} collective-permute-done((bf16[4,128,256]{2,1,0:T(8,128)(2,1)S(1)}, bf16[4,128,256]{2,1,0:T(8,128)(2,1)S(1)}, u32[]{:S(2)}, u32[]{:S(2)}) %collective-permute-start.1) | collective-permute-done | bytes 262176 | tf_op jit(solution)/shard_map/ppermute | solution.py:381
  33.9 0.6 compose.1
  34.5 1.4 %collective-permute-start.4 = (bf16[4,128,256]{2,1,0:T(8,128)(2,1)S(1)}, bf16[4,128,256]{2,1,0:T(8,128)(2,1)S(1)}, u32[]{:S(2)}, u32[]{:S(2)}) collective-permute-start(bf16[4,128,256]{2,1,0:T(8,128)(2,1)S(1)} %get-tuple-element.81.refs_1_), channel_id=1, source_target_pairs={{0,8},{16,24},{1,9},{17,25},{2,10},{18,26},{3,11},{19,27},{4,12},{... | collective-permute-start | bytes 786440 | tf_op jit(solution)/shard_map/ppermute | solution.py:434
  35.9 7.3 %collective-permute-done.4.refs_0_.refs_2_ = bf16[4,128,256]{2,1,0:T(8,128)(2,1)S(1)} collective-permute-done((bf16[4,128,256]{2,1,0:T(8,128)(2,1)S(1)}, bf16[4,128,256]{2,1,0:T(8,128)(2,1)S(1)}, u32[]{:S(2)}, u32[]{:S(2)}) %collective-permute-start.4) | collective-permute-done | bytes 262176 | tf_op jit(solution)/shard_map/ppermute | solution.py:434
  43.2 0.2 absorb.1
  43.4 0.7 %collective-permute-start.5 = (bf16[4,128,128]{2,1,0:T(8,128)(2,1)S(1)}, bf16[4,128,128]{2,1,0:T(8,128)(2,1)S(1)}, u32[]{:S(2)}, u32[]{:S(2)}) collective-permute-start(bf16[4,128,128]{2,1,0:T(8,128)(2,1)S(1)} %absorb.1), channel_id=1, source_target_pairs={{8,16},{9,17},{10,18},{11,19},{12,20},{13,21},{14,22},{15,23}} | collective-permute-start | bytes 393224 | tf_op jit(solution)/shard_map/ppermute | solution.py:434
  44.0 1.3 %collective-permute-start.6 = (bf16[4,128,128]{2,1,0:T(8,128)(2,1)S(1)}, bf16[4,128,128]{2,1,0:T(8,128)(2,1)S(1)}, u32[]{:S(2)}, u32[]{:S(2)}) collective-permute-start(bf16[4,128,128]{2,1,0:T(8,128)(2,1)S(1)} %absorb.1), channel_id=1, source_target_pairs={{8,24},{9,25},{10,26},{11,27},{12,28},{13,29},{14,30},{15,31}} | collective-permute-start | bytes 393224 | tf_op jit(solution)/shard_map/ppermute | solution.py:434
  45.3 0.0 collective-permute-done.5.refs_0_
  45.4 6.5 %collective-permute-done.6.refs_1_ = bf16[4,128,128]{2,1,0:T(8,128)(2,1)S(1)} collective-permute-done((bf16[4,128,128]{2,1,0:T(8,128)(2,1)S(1)}, bf16[4,128,128]{2,1,0:T(8,128)(2,1)S(1)}, u32[]{:S(2)}, u32[]{:S(2)}) %collective-permute-start.6) | collective-permute-done | bytes 131104 | tf_op jit(solution)/shard_map/ppermute | solution.py:434
  51.8 0.5 starts.1
  52.3 1.8 %collective-permute-start.7 = (bf16[4,128,128]{2,1,0:T(8,128)(2,1)S(1)}, bf16[4,128,128]{2,1,0:T(8,128)(2,1)S(1)}, u32[]{:S(2)}, u32[]{:S(2)}) collective-permute-start(bf16[4,128,128]{2,1,0:T(8,128)(2,1)S(1)} %get-tuple-element.84), channel_id=1, source_target_pairs={{0,2},{2,0},{4,6},{6,4},{1,3},{3,1},{5,7},{7,5},{8,10},{10,8},{12,... | collective-permute-start | bytes 393224 | tf_op jit(solution)/shard_map/ppermute | solution.py:381
  54.1 0.1 collective-permute-start.8
  54.2 1.7 %collective-permute-start.9 = (bf16[4,128,128]{2,1,0:T(8,128)(2,1)S(1)}, bf16[4,128,128]{2,1,0:T(8,128)(2,1)S(1)}, u32[]{:S(2)}, u32[]{:S(2)}) collective-permute-start(bf16[4,128,128]{2,1,0:T(8,128)(2,1)S(1)} %get-tuple-element.86), channel_id=1, source_target_pairs={{0,6},{2,4},{4,2},{6,0},{1,7},{3,5},{5,3},{7,1},{8,14},{10,12},{12... | collective-permute-start | bytes 393224 | tf_op jit(solution)/shard_map/ppermute | solution.py:381
  55.9 0.0 copy-done.6
  55.9 0.6 %copy-done.8 = f32[128]{0:T(128)S(1)} copy-done((f32[128]{0:T(128)S(1)}, f32[128]{0:T(128)}, u32[]{:S(2)}) %copy-start.8) | copy-done | bytes 536
  56.5 0.8 %local.7 = (bf16[128,512]{1,0:T(8,128)(2,1)S(1)}, f32[128,512]{1,0:T(8,128)S(1)}, f32[128,512]{1,0:T(8,128)S(1)}) custom-call(s32[1]{0:T(128)S(6)} %xor.14.group_ref, bf16[16,2048]{1,0:T(8,128)(2,1)S(1)} %collective-permute-done.rim_ref, bf16[128,2048]{1,0:T(8,128)(2,1)S(1)} %copy-done.5, f32[3,4,2048]{2,1,0:T(4,128)S(1)} %copy-done.7, ...), custom_call_target="tpu_custom_call" | custom-call | tf_op jit(solution)/shard_map/local/pallas_call | solution.py:390
  57.3 0.8 %local.6 = (bf16[128,512]{1,0:T(8,128)(2,1)S(1)}, f32[128,512]{1,0:T(8,128)S(1)}, f32[128,512]{1,0:T(8,128)S(1)}) custom-call(s32[1]{0:T(128)S(6)} %xor.13.group_ref, bf16[16,2048]{1,0:T(8,128)(2,1)S(1)} %collective-permute-done.rim_ref, bf16[128,2048]{1,0:T(8,128)(2,1)S(1)} %copy-done.5, f32[3,4,2048]{2,1,0:T(4,128)S(1)} %copy-done.7, ...), custom_call_target="tpu_custom_call" | custom-call | tf_op jit(solution)/shard_map/local/pallas_call | solution.py:390
  58.0 0.8 %local.5 = (bf16[128,512]{1,0:T(8,128)(2,1)S(1)}, f32[128,512]{1,0:T(8,128)S(1)}, f32[128,512]{1,0:T(8,128)S(1)}) custom-call(s32[1]{0:T(128)S(6)} %xor.12.group_ref, bf16[16,2048]{1,0:T(8,128)(2,1)S(1)} %collective-permute-done.rim_ref, bf16[128,2048]{1,0:T(8,128)(2,1)S(1)} %copy-done.5, f32[3,4,2048]{2,1,0:T(4,128)S(1)} %copy-done.7, ...), custom_call_target="tpu_custom_call" | custom-call | tf_op jit(solution)/shard_map/local/pallas_call | solution.py:390
  58.8 0.8 %local.4 = (bf16[128,512]{1,0:T(8,128)(2,1)S(1)}, f32[128,512]{1,0:T(8,128)S(1)}, f32[128,512]{1,0:T(8,128)S(1)}) custom-call(s32[1]{0:T(128)} %bitcast.group_ref.me_ref, bf16[16,2048]{1,0:T(8,128)(2,1)S(1)} %collective-permute-done.rim_ref, bf16[128,2048]{1,0:T(8,128)(2,1)S(1)} %copy-done.5, f32[3,4,2048]{2,1,0:T(4,128)S(1)} %copy-done.7, ...), custom_call_target="tpu_custom_call" | custom-call | tf_op jit(solution)/shard_map/local/pallas_call | solution.py:390
  59.6 0.0 collective-permute-done.7.refs_13_
  59.6 1.3 %collective-permute-done.8.refs_14_ = bf16[4,128,128]{2,1,0:T(8,128)(2,1)S(1)} collective-permute-done((bf16[4,128,128]{2,1,0:T(8,128)(2,1)S(1)}, bf16[4,128,128]{2,1,0:T(8,128)(2,1)S(1)}, u32[]{:S(2)}, u32[]{:S(2)}) %collective-permute-start.8) | collective-permute-done | bytes 131104 | tf_op jit(solution)/shard_map/ppermute | solution.py:381
  60.8 0.0 collective-permute-done.9.refs_15_
  60.8 1.4 %finish.1 = bf16[128,2048]{1,0:T(8,128)(2,1)} custom-call(s32[1]{0:T(128)} %bitcast.group_ref.me_ref, bf16[128,512]{1,0:T(8,128)(2,1)S(1)} %get-tuple-element.59.refs_0_, bf16[128,512]{1,0:T(8,128)(2,1)S(1)} %get-tuple-element.62.refs_1_, bf16[128,512]{1,0:T(8,128)(2,1)S(1)} %get-tuple-element.65.refs_2_, bf16[128,512]{1,0:T(8,128)(2,1)S(1)} %get-tuple-element.68.refs_3_, ...), custom_call_target="tpu_custom_call" | custom-call | tf_op jit(solution)/shard_map/finish/pallas_call | solution.py:462
  (12 shorter events, 0.0 us)
Async XLA Ops:
  1.5 4.5 %copy-start.7 = (f32[3,4,2048]{2,1,0:T(4,128)S(1)}, f32[3,4,2048]{2,1,0:T(4,128)}, u32[]{:S(2)}) copy-start(f32[3,4,2048]{2,1,0:T(4,128)} %taps_ref.17) | copy-start | bytes 294916
  2.5 3.5 %copy-start.9 = (bf16[128,16]{0,1:T(8,128)(2,1)S(1)}, bf16[128,16]{0,1:T(8,128)(2,1)}, u32[]{:S(2)}) copy-start(bf16[128,16]{0,1:T(8,128)(2,1)} %param.12) | copy-start | bytes 12292
  2.5 12.6 %collective-permute-start = (bf16[16,2048]{1,0:T(8,128)(2,1)S(1)}, bf16[16,2048]{1,0:T(8,128)(2,1)S(1)}, u32[]{:S(2)}, u32[]{:S(2)}) collective-permute-start(bf16[16,2048]{1,0:T(8,128)(2,1)S(1)} %maximum_maximum_fusion), channel_id=1, source_target_pairs={{0,2},{2,4},{4,6},{6,8},{8,10},{10,12},{12,14},{14,16},{16,18},{18... | collective-permute-start | bytes 196616 | tf_op jit(solution)/shard_map/ppermute | solution.py:329
  6.1 1.0 %copy-start.1 = (bf16[128,2048]{1,0:T(8,128)(2,1)S(1)}, bf16[128,2048]{1,0:T(8,128)(2,1)}, u32[]{:S(2)}) copy-start(bf16[128,2048]{1,0:T(8,128)(2,1)} %v_ref.9) | copy-start | bytes 1572868
  7.1 1.0 %copy-start.3 = (bf16[128,2048]{1,0:T(8,128)(2,1)S(1)}, bf16[128,2048]{1,0:T(8,128)(2,1)}, u32[]{:S(2)}) copy-start(bf16[128,2048]{1,0:T(8,128)(2,1)} %k_ref.9) | copy-start | bytes 1572868
  8.2 1.0 %copy-start.4 = (bf16[128,2048]{1,0:T(8,128)(2,1)S(1)}, bf16[128,2048]{1,0:T(8,128)(2,1)}, u32[]{:S(2)}) copy-start(bf16[128,2048]{1,0:T(8,128)(2,1)} %q_ref.9) | copy-start | bytes 1572868
  9.2 6.0 %copy-start.2 = (bf16[128,2048]{1,0:T(8,128)(2,1)S(1)}, bf16[128,2048]{1,0:T(8,128)(2,1)}, u32[]{:S(2)}) copy-start(bf16[128,2048]{1,0:T(8,128)(2,1)} %v_ref.9) | copy-start | bytes 1572868
  18.0 12.0 %collective-permute-start.3 = (bf16[4,128,256]{2,1,0:T(8,128)(2,1)S(1)}, bf16[4,128,256]{2,1,0:T(8,128)(2,1)S(1)}, u32[]{:S(2)}, u32[]{:S(2)}) collective-permute-start(bf16[4,128,256]{2,1,0:T(8,128)(2,1)S(1)} %get-tuple-element.80), channel_id=1, source_target_pairs={{0,6},{2,4},{4,2},{6,0},{1,7},{3,5},{5,3},{7,1},{8,14},{10,12},{12... | collective-permute-start | bytes 786440 | tf_op jit(solution)/shard_map/ppermute | solution.py:381
  21.2 11.2 %collective-permute-start.2 = (bf16[4,128,256]{2,1,0:T(8,128)(2,1)S(1)}, bf16[4,128,256]{2,1,0:T(8,128)(2,1)S(1)}, u32[]{:S(2)}, u32[]{:S(2)}) collective-permute-start(bf16[4,128,256]{2,1,0:T(8,128)(2,1)S(1)} %get-tuple-element.79), channel_id=1, source_target_pairs={{0,4},{2,6},{4,0},{6,2},{1,5},{3,7},{5,1},{7,3},{8,12},{10,14},{12... | collective-permute-start | bytes 786440 | tf_op jit(solution)/shard_map/ppermute | solution.py:381
  26.6 7.3 %collective-permute-start.1 = (bf16[4,128,256]{2,1,0:T(8,128)(2,1)S(1)}, bf16[4,128,256]{2,1,0:T(8,128)(2,1)S(1)}, u32[]{:S(2)}, u32[]{:S(2)}) collective-permute-start(bf16[4,128,256]{2,1,0:T(8,128)(2,1)S(1)} %get-tuple-element.78), channel_id=1, source_target_pairs={{0,2},{2,0},{4,6},{6,4},{1,3},{3,1},{5,7},{7,5},{8,10},{10,8},{12,... | collective-permute-start | bytes 786440 | tf_op jit(solution)/shard_map/ppermute | solution.py:381
  33.9 22.0 %copy-start.6 = (bf16[128,2048]{1,0:T(8,128)(2,1)S(1)}, bf16[128,2048]{1,0:T(8,128)(2,1)}, u32[]{:S(2)}) copy-start(bf16[128,2048]{1,0:T(8,128)(2,1)} %gate_ref.7) | copy-start | bytes 1572868
  34.5 21.4 %copy-start = (f32[128,2048]{1,0:T(8,128)S(1)}, f32[128,2048]{1,0:T(8,128)}, u32[]{:S(2)}) copy-start(f32[128,2048]{1,0:T(8,128)} %get-tuple-element.46.up_ref) | copy-start | bytes 3145732
  34.5 8.7 %collective-permute-start.4 = (bf16[4,128,256]{2,1,0:T(8,128)(2,1)S(1)}, bf16[4,128,256]{2,1,0:T(8,128)(2,1)S(1)}, u32[]{:S(2)}, u32[]{:S(2)}) collective-permute-start(bf16[4,128,256]{2,1,0:T(8,128)(2,1)S(1)} %get-tuple-element.81.refs_1_), channel_id=1, source_target_pairs={{0,8},{16,24},{1,9},{17,25},{2,10},{18,26},{3,11},{19,27},{4,12},{... | collective-permute-start | bytes 786440 | tf_op jit(solution)/shard_map/ppermute | solution.py:434
  43.4 2.0 %collective-permute-start.5 = (bf16[4,128,128]{2,1,0:T(8,128)(2,1)S(1)}, bf16[4,128,128]{2,1,0:T(8,128)(2,1)S(1)}, u32[]{:S(2)}, u32[]{:S(2)}) collective-permute-start(bf16[4,128,128]{2,1,0:T(8,128)(2,1)S(1)} %absorb.1), channel_id=1, source_target_pairs={{8,16},{9,17},{10,18},{11,19},{12,20},{13,21},{14,22},{15,23}} | collective-permute-start | bytes 393224 | tf_op jit(solution)/shard_map/ppermute | solution.py:434
  44.0 7.8 %collective-permute-start.6 = (bf16[4,128,128]{2,1,0:T(8,128)(2,1)S(1)}, bf16[4,128,128]{2,1,0:T(8,128)(2,1)S(1)}, u32[]{:S(2)}, u32[]{:S(2)}) collective-permute-start(bf16[4,128,128]{2,1,0:T(8,128)(2,1)S(1)} %absorb.1), channel_id=1, source_target_pairs={{8,24},{9,25},{10,26},{11,27},{12,28},{13,29},{14,30},{15,31}} | collective-permute-start | bytes 393224 | tf_op jit(solution)/shard_map/ppermute | solution.py:434
  51.8 4.1 %copy-start.5 = (bf16[128,2048]{1,0:T(8,128)(2,1)S(1)}, bf16[128,2048]{1,0:T(8,128)(2,1)}, u32[]{:S(2)}) copy-start(bf16[128,2048]{1,0:T(8,128)(2,1)} %q_ref.9) | copy-start | bytes 1572868
  52.3 7.3 %collective-permute-start.7 = (bf16[4,128,128]{2,1,0:T(8,128)(2,1)S(1)}, bf16[4,128,128]{2,1,0:T(8,128)(2,1)S(1)}, u32[]{:S(2)}, u32[]{:S(2)}) collective-permute-start(bf16[4,128,128]{2,1,0:T(8,128)(2,1)S(1)} %get-tuple-element.84), channel_id=1, source_target_pairs={{0,2},{2,0},{4,6},{6,4},{1,3},{3,1},{5,7},{7,5},{8,10},{10,8},{12,... | collective-permute-start | bytes 393224 | tf_op jit(solution)/shard_map/ppermute | solution.py:381
  54.1 6.8 %collective-permute-start.8 = (bf16[4,128,128]{2,1,0:T(8,128)(2,1)S(1)}, bf16[4,128,128]{2,1,0:T(8,128)(2,1)S(1)}, u32[]{:S(2)}, u32[]{:S(2)}) collective-permute-start(bf16[4,128,128]{2,1,0:T(8,128)(2,1)S(1)} %get-tuple-element.85), channel_id=1, source_target_pairs={{0,4},{2,6},{4,0},{6,2},{1,5},{3,7},{5,1},{7,3},{8,12},{10,14},{12... | collective-permute-start | bytes 393224 | tf_op jit(solution)/shard_map/ppermute | solution.py:381
  54.2 6.7 %collective-permute-start.9 = (bf16[4,128,128]{2,1,0:T(8,128)(2,1)S(1)}, bf16[4,128,128]{2,1,0:T(8,128)(2,1)S(1)}, u32[]{:S(2)}, u32[]{:S(2)}) collective-permute-start(bf16[4,128,128]{2,1,0:T(8,128)(2,1)S(1)} %get-tuple-element.86), channel_id=1, source_target_pairs={{0,6},{2,4},{4,2},{6,0},{1,7},{3,5},{5,3},{7,1},{8,14},{10,12},{12... | collective-permute-start | bytes 393224 | tf_op jit(solution)/shard_map/ppermute | solution.py:381
  55.9 0.7 %copy-start.8 = (f32[128]{0:T(128)S(1)}, f32[128]{0:T(128)}, u32[]{:S(2)}) copy-start(f32[128]{0:T(128)} %param.15) | copy-start | bytes 1540

commit v2 on v1

v2 whole, which is shorter than its diff:
```python
import functools

import jax
import jax.numpy as jnp
from jax import lax
from jax.experimental import pallas as pl
from jax.experimental.pallas import tpu as pltpu
from jax.sharding import PartitionSpec as P

D = 128
SUB = 16
EDGE = 16
F32 = jnp.float32
BF16 = jnp.bfloat16
VMEM_LIMIT = 32 * 1024 * 1024


def dot(a, b):
    return jnp.dot(a, b, preferred_element_type=F32)


def dot_t(a, b):
    return lax.dot_general(a, b, (((1,), (1,)), ((), ())), preferred_element_type=F32)


def t_dot(a, b):
    return lax.dot_general(a, b, (((0,), (0,)), ((), ())), preferred_element_type=F32)


def split(x):
    hi = x.astype(BF16)
    return hi, (x - hi.astype(F32)).astype(BF16)


def dot3(a, b):
    a_hi, a_lo = a
    b_hi, b_lo = b
    rows = a_hi.shape[0]
    both = dot(jnp.concatenate([a_hi, a_lo], 0), b_hi)
    return both[:rows] + both[rows:] + dot(a_hi, b_lo)


def silu(u):
    return u / (1.0 + jnp.exp(-u))


def conv(x, taps):
    width = taps.shape[0]
    total = x * taps[width - 1 : width]
    for back in range(1, width):
        total = total + pltpu.roll(x, back, 0) * taps[width - 1 - back : width - back]
    return silu(total).astype(BF16).astype(F32)


def key_terms(keys, rates, up, down, mid, end):
    norm = lax.rsqrt(jnp.sum(keys * keys, -1, keepdims=True) + 1e-6)
    unit = keys * norm
    write = unit * rates * up
    low = unit * down
    return (write.astype(BF16), low.astype(BF16), (write * mid).astype(BF16)) + split(low * end)


def iota(shape, dim):
    return lax.broadcasted_iota(jnp.int32, shape, dim)


def tails_kernel(width, *refs):
    ins, out_ref, held, sems = refs[:3], refs[3], refs[4], refs[5]
    rows = ins[0].shape[0]
    copies = [
        pltpu.make_async_copy(ref.at[pl.ds(rows - EDGE, EDGE)], held.at[n], sems.at[n]) for n, ref in enumerate(ins)
    ]
    for copy in copies:
        copy.start()
    parts = []
    for n, copy in enumerate(copies):
        copy.wait()
        parts.append(held[n].astype(F32)[EDGE - width :])
    parts.append(jnp.zeros((EDGE - 3 * width, out_ref.shape[1]), F32))
    out_ref[...] = jnp.concatenate(parts, 0).astype(BF16)


def prepare_kernel(
    groups, g_ref, k_ref, v_ref, beta_ref, taps_ref,
    write_ref, low_ref, kin_ref, khi_ref, klo_ref, vb_ref, up_ref, down_ref, marks_ref, edge_ref, rates_ref,
    held, sems,
):
    rows, width = g_ref.shape
    cols = width // groups
    heads = cols // D
    copies = {}
    for i in range(groups):
        for n, ref in enumerate((g_ref, k_ref, v_ref)):
            c = pl.ds(i * cols, cols)
            copies[n, i] = pltpu.make_async_copy(ref.at[:, c], held.at[n, :, c], sems.at[n, i])
            copies[n, i].start()
    middle = rows // 2 - 1
    at, other = iota((rows, rows), 0), iota((rows, rows), 1)
    plus = jnp.where((other <= at) & (other > middle), 1.0, 0.0)
    minus = jnp.where((other > at) & (other <= middle), 1.0, 0.0)
    summing = (plus - minus).astype(BF16)
    rates = beta_ref[...].astype(F32).T
    rates_ref[...] = rates[:EDGE]
    lane = iota(rates.shape, 1)
    for i in range(groups):
        whole = slice(i * cols, (i + 1) * cols)
        copies[0, i].wait()
        sums = dot(summing, held[0, :, whole])
        up = jnp.exp(sums)
        down = jnp.exp(-sums)
        up_ref[:, whole] = up
        down_ref[:, whole] = down[:EDGE]
        mid = jnp.exp(held[0, 0:EDGE, whole].astype(F32)[0:1] - sums[0:1])
        end = up[rows - 1 : rows]
        marks_ref[:, whole] = jnp.concatenate([mid, end] * 4, 0)
        copies[1, i].wait()
        edge_ref[0, :, whole] = held[1, 0:EDGE, whole]
        keys = conv(held[1, :, whole].astype(F32), taps_ref[1, :, whole])
        for h in range(heads):
            c = slice(h * D, (h + 1) * D)
            to = slice((i * heads + h) * D, (i * heads + h + 1) * D)
            rate = jnp.sum(jnp.where(lane == i * heads + h, rates, 0.0), -1, keepdims=True)
            out = key_terms(keys[:, c], rate, up[:, c], down[:, c], mid[:, c], end[:, c])
            for ref, value in zip((write_ref, low_ref, kin_ref, khi_ref, klo_ref), out):
                ref[:, to] = value
        copies[2, i].wait()
        edge_ref[1, :, whole] = held[2, 0:EDGE, whole]
        values = conv(held[2, :, whole].astype(F32), taps_ref[2, :, whole])
        for h in range(heads):
            to = slice((i * heads + h) * D, (i * heads + h + 1) * D)
            rate = jnp.sum(jnp.where(lane == i * heads + h, rates, 0.0), -1, keepdims=True)
            vb_ref[:, to] = (values[:, h * D : (h + 1) * D] * rate).astype(BF16)


def edge_rows(rim, which, raw, taps):
    width = taps.shape[0]
    first = which * (width - 1)
    before = pltpu.roll(rim, (8 - (width - 1) - first) % rim.shape[0], 0)[0:8]
    return conv(jnp.concatenate([before, raw.astype(F32)], 0), taps)[8:]


def solve_heads(lows, rows):
    lane_sub = iota((SUB, rows), 1)
    blocks = rows // SUB
    at, other = iota((rows, rows), 0), iota((rows, rows), 1)
    same = (at // SUB) == (other // SUB)
    packed = []
    for low in lows:
        own = jnp.where(same, low, 0.0)
        total = own[0:SUB]
        for b in range(1, blocks):
            total = total + own[b * SUB : (b + 1) * SUB]
        packed.append(total)
    unit = jnp.where(lane_sub % SUB == iota((SUB, rows), 0), 1.0, 0.0)
    solved = [unit for _ in lows]
    group_start = lane_sub - lane_sub % SUB
    for j in range(SUB - 1):
        for n, total in enumerate(packed):
            spread = jnp.take_along_axis(total, group_start + j, axis=1, mode="promise_in_bounds")
            solved[n] = solved[n] - spread * solved[n][j : j + 1]
    full = [jnp.where(same, jnp.concatenate([x] * blocks, 0), 0.0) for x in solved]
    size = SUB
    while size < rows:
        mask = (at // (2 * size) == other // (2 * size)) & (at // size != other // size)
        lower = [slice(p * size, (p + 1) * size) for p in range(1, rows // size, 2)]
        take = lambda x: jnp.concatenate([x[s] for s in lower], 0)
        small_mask = take(mask)
        parts = [split(x) for x in full]
        links = [split(jnp.where(small_mask, take(low), 0.0)) for low in lows]
        inner = [dot3(link, part) for link, part in zip(links, parts)]
        zeros = jnp.zeros((size, rows), F32)
        spread = []
        for x in inner:
            pieces = []
            for p in range(rows // (2 * size)):
                pieces += [zeros, x[p * size : (p + 1) * size]]
            spread.append(split(jnp.concatenate(pieces, 0)))
        fixes = [dot3((take(part[0]), take(part[1])), s) for part, s in zip(parts, spread)]
        result = []
        for x, fix in zip(full, fixes):
            pieces = []
            for p in range(rows // (2 * size)):
                pieces += [
                    x[2 * p * size : (2 * p + 1) * size],
                    x[(2 * p + 1) * size : (2 * p + 2) * size] - fix[p * size : (p + 1) * size],
                ]
            result.append(jnp.concatenate(pieces, 0))
        full = result
        size *= 2
    return full


def block_kernel(
    group_ref, later_ref, rim_ref, edge_ref, rates_ref, taps_ref, up_ref, down_ref, marks_ref,
    write_ref, low_ref, kin_ref, khi_ref, klo_ref, vb_ref,
    move_ref, made_ref, low_out_ref,
):
    rows = low_ref.shape[0]
    heads = move_ref.shape[0]
    cols = heads * D
    start = pl.multiple_of(group_ref[0] * cols, cols)
    mine = pl.ds(start, cols)
    rim = jnp.where(later_ref[0] > 0, rim_ref[:, mine].astype(F32), 0.0)
    keys = edge_rows(rim, 1, edge_ref[0, :, mine], taps_ref[1, :, mine])
    values = edge_rows(rim, 2, edge_ref[1, :, mine], taps_ref[2, :, mine])
    up, down, marks = up_ref[0:EDGE, mine], down_ref[:, mine], marks_ref[:, mine]
    rates = rates_ref[...]
    lane = iota(rates.shape, 1)
    base = group_ref[0] * heads
    at, other = iota((rows, rows), 0), iota((rows, rows), 1)
    lows, ends, sides = [], [], []
    for h in range(heads):
        c = slice(h * D, (h + 1) * D)
        here = pl.ds(pl.multiple_of(start + h * D, D), D)
        rate = jnp.sum(jnp.where(lane == base + h, rates, 0.0), -1, keepdims=True)
        edge = key_terms(keys[:, c], rate, up[:, c], down[:, c], marks[0:1, c], marks[1:2, c])
        write, low, kin, khi, klo = [
            jnp.concatenate([e, ref[EDGE:, here]], 0)
            for e, ref in zip(edge, (write_ref, low_ref, kin_ref, khi_ref, klo_ref))
        ]
        vb = jnp.concatenate([(values[:, c] * rate).astype(BF16), vb_ref[EDGE:, here]], 0)
        low_out_ref[:, c] = low
        lows.append(jnp.where(at > other, dot_t(write, low), 0.0))
        ends.append((khi, klo))
        sides.append(jnp.concatenate([kin, vb], 1))
    solved = solve_heads(lows, rows)
    made = []
    for t, side in zip(solved, sides):
        both = dot(jnp.concatenate(split(t), 0), side)
        made.append((both[:rows] + both[rows:]).astype(BF16))
    for h in range(heads):
        c = slice(h * D, (h + 1) * D)
        sums = t_dot(ends[h][0], made[h]) + t_dot(ends[h][1], made[h])
        fade = marks[0:1, c] * marks[1:2, c] - 1.0
        move = jnp.where(at == other, fade, 0.0) - sums[:, :D]
        made_ref[h] = made[h]
        move_ref[h, :, :D] = move.astype(BF16)
        move_ref[h, :, D:] = sums[:, D:].astype(BF16)


def local_kernel(count, later_ref, *refs):
    group_refs, refs = refs[:count], refs[count:]
    rim_ref, q_ref, gate_ref, taps_ref, gain_ref, up_ref, marks_ref, *refs = refs
    ins, outs, held, sems = refs[: 2 * count], refs[2 * count : 5 * count], refs[-2], refs[-1]
    rows, cols = outs[0].shape
    heads = cols // D
    starts = [pl.multiple_of(group_refs[i][0] * cols, cols) for i in range(count)]
    copies = {}
    for i in range(count):
        for n, ref in enumerate((q_ref, gate_ref)):
            copies[n, i] = pltpu.make_async_copy(ref.at[:, pl.ds(starts[i], cols)], held.at[n, i], sems.at[n, i])
            copies[n, i].start()
    at, other = iota((rows, rows), 0), iota((rows, rows), 1)
    for i in range(count):
        low_ref, made_ref = ins[2 * i : 2 * i + 2]
        reach_ref, own_ref, scale_ref = outs[3 * i : 3 * i + 3]
        mine = pl.ds(starts[i], cols)
        taps = taps_ref[0, :, mine]
        rim = jnp.where(later_ref[0] > 0, rim_ref[:, mine].astype(F32), 0.0)
        mid = marks_ref[0:1, mine]
        copies[0, i].wait()
        edge = edge_rows(rim, 0, held[0, i, 0:EDGE], taps)
        queries = jnp.concatenate([edge, conv(held[0, i].astype(F32), taps)[EDGE:]], 0) * up_ref[:, mine]
        copies[1, i].wait()
        gate = held[1, i].astype(F32)
        for h in range(heads):
            c = slice(h * D, (h + 1) * D)
            scores = jnp.where(at >= other, dot_t(queries[:, c].astype(BF16), low_ref[:, c]), 0.0)
            both = dot(jnp.concatenate(split(scores), 0), made_ref[h])
            seen = both[:rows] + both[rows:]
            reach_ref[:, c] = (queries[:, c] * mid[:, c] - seen[:, :D]).astype(BF16)
            own_ref[:, c] = seen[:, D:]
            scale_ref[:, c] = gain_ref[...] / (1.0 + jnp.exp(-gate[:, c]))


def follow(pair, state):
    add = pair[:, D:] if state.shape[1] == D else pair
    return (state.astype(F32) + add.astype(F32) + dot(pair[:, :D], state)).astype(BF16)


def chain_kernel(me_ref, *refs):
    pairs, before_ref, whole_ref = refs[:-2], refs[-2], refs[-1]
    count = len(pairs)
    heads = whole_ref.shape[0]
    for m in range(count):

        @pl.when(me_ref[0] == m)
        def _():
            now = [pairs[m][h] for h in range(heads)]
            for b in range(1, count):
                for h in range(heads):
                    before_ref[b - 1, h] = now[h]
                    now[h] = follow(pairs[m ^ b][h], now[h])
            for h in range(heads):
                whole_ref[h] = now[h]


def absorb_kernel(wide, last, upper_ref, mine_ref, theirs_ref, *refs):
    have_ref, (send_ref, ahead_ref) = (refs[0], refs[1:]) if wide else (None, refs)
    part = slice(D, 2 * D) if last else slice(0, 2 * D)
    heads = mine_ref.shape[0]
    for upper in (0, 1):

        @pl.when(upper_ref[0] == upper)
        def _():
            for h in range(heads):
                mine, theirs = mine_ref[h], theirs_ref[h]
                first, then = (theirs, mine) if upper else (mine, theirs)
                send_ref[h] = follow(then, first[:, part])
                if upper:
                    ahead_ref[h] = follow(have_ref[h], theirs) if wide else theirs
                else:
                    ahead_ref[h] = have_ref[h] if wide else jnp.zeros(theirs.shape, BF16)


def starts_kernel(me_ref, upper_ref, came_ref, ahead_ref, before_ref, *outs):
    heads = came_ref.shape[0]
    first = []
    for h in range(heads):
        came = jnp.where(upper_ref[0] > 0, came_ref[h].astype(F32), 0.0).astype(BF16)
        first.append(follow(ahead_ref[h], came))
    for m in range(len(outs)):

        @pl.when(me_ref[0] == m)
        def _():
            for b in range(len(outs)):
                for h in range(heads):
                    outs[m ^ b][h] = follow(before_ref[b - 1, h], first[h]) if b else first[h]


def finish_kernel(count, me_ref, *refs):
    out_ref = refs[-1]
    reach, own, scale, starts = (refs[k * count : (k + 1) * count] for k in range(4))
    heads = starts[0].shape[0]
    for m in range(count):

        @pl.when(me_ref[0] == m)
        def _():
            for g in range(count):
                j = m ^ g
                for h in range(heads):
                    c = slice(h * D, (h + 1) * D)
                    found = own[j][:, c] + dot(reach[j][:, c], starts[j][h])
                    found = found.astype(BF16).astype(F32)
                    mean = jnp.mean(found * found, -1, keepdims=True)
                    at = slice((g * heads + h) * D, (g * heads + h + 1) * D)
                    out_ref[:, at] = (found * lax.rsqrt(mean + 1e-5) * scale[j][:, c]).astype(BF16)


def params():
    return pltpu.CompilerParams(vmem_limit_bytes=VMEM_LIMIT)


def shards(query_raw, key_raw, value_raw, log_decay, beta, conv_weight, out_gate, norm_gain):
    rows, width = query_raw.shape
    groups = lax.axis_size("head")
    spans = lax.axis_size("ctx")
    cols = width // groups
    heads = cols // D
    rim_width = conv_weight.shape[1] - 1
    me = lax.axis_index("head").astype(jnp.int32).reshape(1)
    span = lax.axis_index("ctx").astype(jnp.int32).reshape(1)
    group_ids = [me ^ j for j in range(groups)]
    later = (me + span > 0).astype(jnp.int32)
    uppers = [(span >> bit) & 1 for bit in range((spans - 1).bit_length())]
    (group_ids, later, uppers), query_raw, key_raw, value_raw, log_decay = lax.optimization_barrier(
        ((group_ids, later, uppers), query_raw, key_raw, value_raw, log_decay)
    )
    me_arg = group_ids[0]
    query_raw, key_raw, value_raw, log_decay, out_gate = (
        pltpu.with_memory_space_constraint(x, pltpu.HBM) for x in (query_raw, key_raw, value_raw, log_decay, out_gate)
    )
    beta = beta.T

    smem = pl.BlockSpec(memory_space=pltpu.SMEM)
    vmem = pl.BlockSpec(memory_space=pltpu.VMEM)
    far = pl.BlockSpec(memory_space=pl.ANY)

    tails = pl.pallas_call(
        functools.partial(tails_kernel, rim_width),
        in_specs=[far] * 3,
        out_specs=vmem,
        out_shape=jax.ShapeDtypeStruct((EDGE, width), BF16),
        scratch_shapes=[pltpu.VMEM((3, EDGE, width), BF16), pltpu.SemaphoreType.DMA((3,))],
        compiler_params=params(),
        name="tails",
    )(query_raw, key_raw, value_raw)
    total = groups * spans
    rim = lax.ppermute(tails, ("ctx", "head"), [(i, (i + 1) % total) for i in range(total)])

    wide16 = jax.ShapeDtypeStruct((rows, width), BF16)
    prepared = pl.pallas_call(
        functools.partial(prepare_kernel, groups),
        in_specs=[far] * 3 + [vmem] * 2,
        out_specs=[vmem] * 11,
        out_shape=[wide16] * 6
        + [
            jax.ShapeDtypeStruct((rows, width), F32),
            jax.ShapeDtypeStruct((EDGE, width), F32),
            jax.ShapeDtypeStruct((8, width), F32),
            jax.ShapeDtypeStruct((2, EDGE, width), BF16),
            jax.ShapeDtypeStruct((EDGE, beta.shape[0]), F32),
        ],
        scratch_shapes=[pltpu.VMEM((3, rows, width), BF16), pltpu.SemaphoreType.DMA((3, groups))],
        compiler_params=params(),
        cost_estimate=pl.CostEstimate(flops=20_000_000, bytes_accessed=9_000_000, transcendentals=2_000_000),
        name="prepare",
    )(log_decay, key_raw, value_raw, beta, conv_weight)
    write, low, kin, khi, klo, vb, up, down, marks, edges, rates = prepared

    moves, made, lows = [None] * groups, [None] * groups, [None] * groups
    order = list(range(groups - 1, -1, -1))
    for j in order:
        moves[j], made[j], lows[j] = pl.pallas_call(
            block_kernel,
            in_specs=[smem] * 2 + [vmem] * 13,
            out_specs=[vmem] * 3,
            out_shape=[
                jax.ShapeDtypeStruct((heads, D, 2 * D), BF16),
                jax.ShapeDtypeStruct((heads, rows, 2 * D), BF16),
                jax.ShapeDtypeStruct((rows, cols), BF16),
            ],
            compiler_params=params(),
            name="block",
        )(group_ids[j], later, rim, edges, rates, conv_weight, up, down, marks, write, low, kin, khi, klo, vb)

    def call(kernel, name, in_specs, outs, scratch=()):
        return pl.pallas_call(
            kernel,
            in_specs=in_specs,
            out_specs=[vmem] * len(outs),
            out_shape=[jax.ShapeDtypeStruct(*out) for out in outs],
            scratch_shapes=scratch,
            compiler_params=params(),
            name=name,
        )

    def swap(array, j, axis="head"):
        return lax.ppermute(array, axis, [(i, i ^ j) for i in range(lax.axis_size(axis))])

    block16, block32 = ((rows, cols), BF16), ((rows, cols), F32)
    state, pair = ((heads, D, D), BF16), ((heads, D, 2 * D), BF16)

    def local(js):
        if not js:
            return {}
        got = call(
            functools.partial(local_kernel, len(js)),
            "local",
            [smem] * (1 + len(js)) + [vmem, far, far] + [vmem] * (4 + 2 * len(js)),
            [block16, block32, block32] * len(js),
            [pltpu.VMEM((2, len(js), rows, cols), BF16), pltpu.SemaphoreType.DMA((2, len(js)))],
        )(
            later, *[group_ids[j] for j in js], rim, query_raw, out_gate, conv_weight, norm_gain.reshape(1, D),
            up, marks, *[x for j in js for x in (lows[j], made[j])],
        )
        return {j: got[3 * i : 3 * i + 3] for i, j in enumerate(js)}

    came_pairs = [swap(moves[j], j) if j else moves[j] for j in range(groups)]
    left = list(range(groups))
    came_pairs, found = lax.optimization_barrier((came_pairs, local(left[: groups // 2])))
    left = left[groups // 2 :]

    before, whole = call(
        chain_kernel, "chain", [smem] + [vmem] * groups, [((groups - 1, heads, D, 2 * D), BF16), pair]
    )(me_arg, *came_pairs)

    ahead, bit, send = None, 1, whole if spans > 2 else whole[:, :, D:]
    came, upper = None, later
    while bit < spans:
        last = 2 * bit >= spans
        theirs = swap(send, bit, "ctx")
        if left:
            theirs, mine = lax.optimization_barrier((theirs, local(left)))
            found.update(mine)
            left = []
        upper = uppers[bit.bit_length() - 1]
        if last:
            came = theirs
        else:
            wide, next_last = ahead is not None, 4 * bit >= spans
            send, ahead = call(
                functools.partial(absorb_kernel, wide, next_last),
                "absorb",
                [smem] + [vmem] * (3 if wide else 2),
                [state if next_last else pair, pair],
            )(upper, whole, theirs, *([ahead] if wide else []))
            whole = send
        bit *= 2
    found.update(local(left))
    came = jnp.zeros(*state) if came is None else came
    ahead = jnp.zeros(*pair) if ahead is None else ahead

    starts = call(starts_kernel, "starts", [smem] * 2 + [vmem] * 3, [state] * groups)(
        me_arg, upper, came, ahead, before
    )
    starts = [starts[0]] + [swap(starts[j], j) for j in range(1, groups)]

    reach, own, scale = zip(*[found[j] for j in range(groups)])
    (out,) = call(
        functools.partial(finish_kernel, groups),
        "finish",
        [smem] + [vmem] * (4 * groups),
        [((rows, width), BF16)],
    )(me_arg, *reach, *own, *scale, *starts)
    return out


def solution(mesh):
    tokens = P(("dp", "ctx", "head"), None)
    placed = (tokens, tokens, tokens, tokens, tokens, P(), tokens, P())
    return jax.shard_map(shards, mesh=mesh, in_specs=placed, out_specs=tokens, check_vma=False)
```

time: 63.1 us -> 53.5 us (0.85)
  the two profiles are of different devices: /device:TPU:24 before, /device:TPU:0 now
where the time goes in v2:
time: 53.5 us; the launch traced here: 53.3 us
  Pallas kernels  21.5 us (40%)
  waiting for transfers between devices  19 us (36%)
  starting transfers between devices  12 us (22%)
  local copies, waits for them, and re-layouts  0.66 us (1%)
    ppermute x8, waiting for transfers between devices, swap(): lax.ppermute(array, axis, [(i, i ^ j) for i in range(lax.axis_size(axis))])  17.1 us
    ppermute x8, starting transfers between devices, swap(): lax.ppermute(array, axis, [(i, i ^ j) for i in range(lax.axis_size(axis))])  9.04 us
    pallas_call x4, Pallas kernels, shards(): pl.pallas_call(block_kernel, in_specs=[smem] * 2 + [vmem] * 13, out_specs...  8.14 us
    pallas_call x2, Pallas kernels, local(): call(functools.partial(local_kernel, len(js)), 'local', [smem] * (1 + len...  5.25 us
    pallas_call x1, Pallas kernels, shards(): pl.pallas_call(functools.partial(prepare_kernel, groups), in_specs=[far]...  4.31 us
    ppermute x1, starting transfers between devices, shards(): lax.ppermute(tails, ('ctx', 'head'), [(i, (i + 1) % total) for i in range...  2.99 us
    ppermute x1, waiting for transfers between devices, shards(): lax.ppermute(tails, ('ctx', 'head'), [(i, (i + 1) % total) for i in range...  1.91 us
    pallas_call x1, Pallas kernels, shards(): call(functools.partial(finish_kernel, groups), 'finish', [smem] + [vmem]...  1.36 us
  transfers between devices with their start and end apart: 9, of which 6 were waited for; matrix products, arithmetic and copies ran while one was open for 0% of the time, Pallas kernels for 29%

profile of v2, /device:TPU:0, one launch (start us, length us, event | category | flops | bytes accessed | tf_op | source)
XLA Modules:
  0.0 53.3 jit_solution(2599741056526419498)
XLA Ops:
  0.0 0.0 copy-start
  0.0 0.0 copy-start.2
  0.0 1.0 %tails.1 = bf16[16,2048]{1,0:T(8,128)(2,1)S(1)} custom-call(bf16[128,2048]{1,0:T(8,128)(2,1)} %refs_3_.1, bf16[128,2048]{1,0:T(8,128)(2,1)} %k_ref, bf16[128,2048]{1,0:T(8,128)(2,1)} %v_ref), custom_call_target="tpu_custom_call" | custom-call | tf_op jit(solution)/shard_map/tails/pallas_call | solution.py:379
  1.0 3.0 %collective-permute-start = (bf16[16,2048]{1,0:T(8,128)(2,1)S(1)}, bf16[16,2048]{1,0:T(8,128)(2,1)S(1)}, u32[]{:S(2)}, u32[]{:S(2)}) collective-permute-start(bf16[16,2048]{1,0:T(8,128)(2,1)S(1)} %tails.1), channel_id=1, source_target_pairs={{0,2},{2,4},{4,6},{6,8},{8,10},{10,12},{12,14},{14,16},{16,18},{18... | collective-permute-start | bytes 196616 | tf_op jit(solution)/shard_map/ppermute | solution.py:389
  4.0 0.0 copy-done
  4.0 0.0 copy-done.2
  4.0 4.3 %prepare.1 = (bf16[128,2048]{1,0:T(8,128)(2,1)S(1)}, bf16[128,2048]{1,0:T(8,128)(2,1)S(1)}, bf16[128,2048]{1,0:T(8,128)(2,1)S(1)}, bf16[128,2048]{1,0:T(8,128)(2...) custom-call(bf16[128,2048]{1,0:T(8,128)(2,1)} %g_ref, ...), custom_call_target="tpu_custom_call" | custom-call | flops 20000000 | bytes 9000000 | tf_op jit(solution)/shard_map/prepare/pallas_call | solution.py:392
  8.3 1.9 %collective-permute-done.rim_ref.refs_2_ = bf16[16,2048]{1,0:T(8,128)(2,1)S(1)} collective-permute-done((bf16[16,2048]{1,0:T(8,128)(2,1)S(1)}, bf16[16,2048]{1,0:T(8,128)(2,1)S(1)}, u32[]{:S(2)}, u32[]{:S(2)}) %collective-permute-start) | collective-permute-done | bytes 65568 | tf_op jit(solution)/shard_map/ppermute | solution.py:389
  10.2 2.0 %block.7 = (bf16[4,128,256]{2,1,0:T(8,128)(2,1)S(1)}, bf16[4,128,256]{2,1,0:T(8,128)(2,1)S(1)}, bf16[128,512]{1,0:T(8,128)(2,1)S(1)}) custom-call(s32[1]{0:T(128)S(6)} %xor.11.group_ref.refs_1_, s32[1]{0:T(128)S(6)} %convert_element_type.3.later_ref, bf16[16,2048]{1,0:T(8,128)(2,1)S(1)} %collective-permute-done.rim_ref.refs_2_, ...), custom_call_target="tpu_custom_call" | custom-call | tf_op jit(solution)/shard_map/block/pallas_call | solution.py:414
  12.3 0.6 %collective-permute-start.3 = (bf16[4,128,256]{2,1,0:T(8,128)(2,1)S(1)}, bf16[4,128,256]{2,1,0:T(8,128)(2,1)S(1)}, u32[]{:S(2)}, u32[]{:S(2)}) collective-permute-start(bf16[4,128,256]{2,1,0:T(8,128)(2,1)S(1)} %get-tuple-element.99), channel_id=1, source_target_pairs={{0,6},{2,4},{4,2},{6,0},{1,7},{3,5},{5,3},{7,1},{8,14},{10,12},{12... | collective-permute-start | bytes 786440 | tf_op jit(solution)/shard_map/ppermute | solution.py:439
  12.9 2.0 %block.6 = (bf16[4,128,256]{2,1,0:T(8,128)(2,1)S(1)}, bf16[4,128,256]{2,1,0:T(8,128)(2,1)S(1)}, bf16[128,512]{1,0:T(8,128)(2,1)S(1)}) custom-call(s32[1]{0:T(128)S(6)} %xor.10.group_ref.refs_0_, s32[1]{0:T(128)S(6)} %convert_element_type.3.later_ref, bf16[16,2048]{1,0:T(8,128)(2,1)S(1)} %collective-permute-done.rim_ref.refs_2_, ...), custom_call_target="tpu_custom_call" | custom-call | tf_op jit(solution)/shard_map/block/pallas_call | solution.py:414
  14.9 0.6 %collective-permute-start.2 = (bf16[4,128,256]{2,1,0:T(8,128)(2,1)S(1)}, bf16[4,128,256]{2,1,0:T(8,128)(2,1)S(1)}, u32[]{:S(2)}, u32[]{:S(2)}) collective-permute-start(bf16[4,128,256]{2,1,0:T(8,128)(2,1)S(1)} %get-tuple-element.97), channel_id=1, source_target_pairs={{0,4},{2,6},{4,0},{6,2},{1,5},{3,7},{5,1},{7,3},{8,12},{10,14},{12... | collective-permute-start | bytes 786440 | tf_op jit(solution)/shard_map/ppermute | solution.py:439
  15.5 2.0 %block.5 = (bf16[4,128,256]{2,1,0:T(8,128)(2,1)S(1)}, bf16[4,128,256]{2,1,0:T(8,128)(2,1)S(1)}, bf16[128,512]{1,0:T(8,128)(2,1)S(1)}) custom-call(s32[1]{0:T(128)S(6)} %xor.9.group_ref.refs_1_, s32[1]{0:T(128)S(6)} %convert_element_type.3.later_ref, bf16[16,2048]{1,0:T(8,128)(2,1)S(1)} %collective-permute-done.rim_ref.refs_2_, ...), custom_call_target="tpu_custom_call" | custom-call | tf_op jit(solution)/shard_map/block/pallas_call | solution.py:414
  17.5 2.5 %collective-permute-start.1 = (bf16[4,128,256]{2,1,0:T(8,128)(2,1)S(1)}, bf16[4,128,256]{2,1,0:T(8,128)(2,1)S(1)}, u32[]{:S(2)}, u32[]{:S(2)}) collective-permute-start(bf16[4,128,256]{2,1,0:T(8,128)(2,1)S(1)} %get-tuple-element.95), channel_id=1, source_target_pairs={{0,2},{2,0},{4,6},{6,4},{1,3},{3,1},{5,7},{7,5},{8,10},{10,8},{12,... | collective-permute-start | bytes 786440 | tf_op jit(solution)/shard_map/ppermute | solution.py:439
  20.0 2.0 %block.4 = (bf16[4,128,256]{2,1,0:T(8,128)(2,1)S(1)}, bf16[4,128,256]{2,1,0:T(8,128)(2,1)S(1)}, bf16[128,512]{1,0:T(8,128)(2,1)S(1)}) custom-call(s32[1]{0:T(128)} %bitcast.group_ref.refs_0_.me_ref, s32[1]{0:T(128)S(6)} %convert_element_type.3.later_ref, bf16[16,2048]{1,0:T(8,128)(2,1)S(1)} %collective-permute-done.rim_ref.refs_2_, ...), custom_call_target="tpu_custom_call" | custom-call | tf_op jit(solution)/shard_map/block/pallas_call | solution.py:414
  22.1 0.0 copy-start.1
  22.1 0.6 %copy-done.1 = f32[128]{0:T(128)S(1)} copy-done((f32[128]{0:T(128)S(1)}, f32[128]{0:T(128)}, u32[]{:S(2)}) %copy-start.1) | copy-done | bytes 536
  22.7 2.6 %local.2 = (bf16[128,512]{1,0:T(8,128)(2,1)S(1)}, f32[128,512]{1,0:T(8,128)S(1)}, f32[128,512]{1,0:T(8,128)S(1)}, bf16[128,512]{1,0:T(8,128)(2,1)S(1)}, f32[128,512]{1,0:T(8,128)S(1)}, /*index=5*/f32[128,512]{1,0:T(8,128)S(1)}) custom-call(s32[1]{0:T(128)S(6)} %convert_element_type.3.later_ref, s32[1]{0:T(128)} %bitcast.group_ref.refs_0_.me_ref, ...), custom_call_target="tpu_custom_call" | custom-call | tf_op jit(solution)/shard_map/local/pallas_call | solution.py:447
  25.4 0.0 collective-permute-done.3.refs_3_
  25.4 0.6 %collective-permute-done.2.refs_2_ = bf16[4,128,256]{2,1,0:T(8,128)(2,1)S(1)} collective-permute-done((bf16[4,128,256]{2,1,0:T(8,128)(2,1)S(1)}, bf16[4,128,256]{2,1,0:T(8,128)(2,1)S(1)}, u32[]{:S(2)}, u32[]{:S(2)}) %collective-permute-start.2) | collective-permute-done | bytes 262176 | tf_op jit(solution)/shard_map/ppermute | solution.py:439
  26.0 0.0 collective-permute-done.1.refs_1_
  26.0 0.8 %chain.1 = (bf16[3,4,128,256]{3,2,1,0:T(8,128)(2,1)S(1)}, bf16[4,128,256]{2,1,0:T(8,128)(2,1)S(1)}) custom-call(s32[1]{0:T(128)} %bitcast.group_ref.refs_0_.me_ref, bf16[4,128,256]{2,1,0:T(8,128)(2,1)S(1)} %get-tuple-element.112.refs_0_, bf16[4,128,256]{2,1,0:T(8,128)(2,1)S(1)} %collective-permute-done.1.refs_1_, ...), custom_call_target="tpu_custom_call" | custom-call | tf_op jit(solution)/shard_map/chain/pallas_call | solution.py:464
  26.8 0.4 collective-permute-start.4
  27.3 2.6 %local.3 = (bf16[128,512]{1,0:T(8,128)(2,1)S(1)}, f32[128,512]{1,0:T(8,128)S(1)}, f32[128,512]{1,0:T(8,128)S(1)}, bf16[128,512]{1,0:T(8,128)(2,1)S(1)}, f32[128,512]{1,0:T(8,128)S(1)}, /*index=5*/f32[128,512]{1,0:T(8,128)S(1)}) custom-call(s32[1]{0:T(128)S(6)} %convert_element_type.3.later_ref, s32[1]{0:T(128)S(6)} %xor.10.group_ref.refs_0_, ...), custom_call_target="tpu_custom_call" | custom-call | tf_op jit(solution)/shard_map/local/pallas_call | solution.py:447
  29.9 5.2 %collective-permute-done.4.theirs_ref = bf16[4,128,256]{2,1,0:T(8,128)(2,1)S(1)} collective-permute-done((bf16[4,128,256]{2,1,0:T(8,128)(2,1)S(1)}, bf16[4,128,256]{2,1,0:T(8,128)(2,1)S(1)}, u32[]{:S(2)}, u32[]{:S(2)}) %collective-permute-start.4) | collective-permute-done | bytes 262176 | tf_op jit(solution)/shard_map/ppermute | solution.py:439
  35.1 0.2 absorb.1
  35.3 1.4 %collective-permute-start.5 = (bf16[4,128,128]{2,1,0:T(8,128)(2,1)S(1)}, bf16[4,128,128]{2,1,0:T(8,128)(2,1)S(1)}, u32[]{:S(2)}, u32[]{:S(2)}) collective-permute-start(bf16[4,128,128]{2,1,0:T(8,128)(2,1)S(1)} %get-tuple-element.140), channel_id=1, source_target_pairs={{0,16},{8,24},{16,0},{24,8},{1,17},{9,25},{17,1},{25,9},{2,18},{10... | collective-permute-start | bytes 393224 | tf_op jit(solution)/shard_map/ppermute | solution.py:439
  36.7 6.6 %collective-permute-done.5.came_ref = bf16[4,128,128]{2,1,0:T(8,128)(2,1)S(1)} collective-permute-done((bf16[4,128,128]{2,1,0:T(8,128)(2,1)S(1)}, bf16[4,128,128]{2,1,0:T(8,128)(2,1)S(1)}, u32[]{:S(2)}, u32[]{:S(2)}) %collective-permute-start.5) | collective-permute-done | bytes 131104 | tf_op jit(solution)/shard_map/ppermute | solution.py:439
  43.3 0.5 starts.1
  43.7 0.5 collective-permute-start.6
  44.2 1.7 %collective-permute-start.7 = (bf16[4,128,128]{2,1,0:T(8,128)(2,1)S(1)}, bf16[4,128,128]{2,1,0:T(8,128)(2,1)S(1)}, u32[]{:S(2)}, u32[]{:S(2)}) collective-permute-start(bf16[4,128,128]{2,1,0:T(8,128)(2,1)S(1)} %get-tuple-element.145), channel_id=1, source_target_pairs={{0,4},{2,6},{4,0},{6,2},{1,5},{3,7},{5,1},{7,3},{8,12},{10,14},{12... | collective-permute-start | bytes 393224 | tf_op jit(solution)/shard_map/ppermute | solution.py:439
  45.9 1.4 %collective-permute-start.8 = (bf16[4,128,128]{2,1,0:T(8,128)(2,1)S(1)}, bf16[4,128,128]{2,1,0:T(8,128)(2,1)S(1)}, u32[]{:S(2)}, u32[]{:S(2)}) collective-permute-start(bf16[4,128,128]{2,1,0:T(8,128)(2,1)S(1)} %get-tuple-element.146), channel_id=1, source_target_pairs={{0,6},{2,4},{4,2},{6,0},{1,7},{3,5},{5,3},{7,1},{8,14},{10,12},{12... | collective-permute-start | bytes 393224 | tf_op jit(solution)/shard_map/ppermute | solution.py:439
  47.3 2.9 %collective-permute-done.6.refs_13_ = bf16[4,128,128]{2,1,0:T(8,128)(2,1)S(1)} collective-permute-done((bf16[4,128,128]{2,1,0:T(8,128)(2,1)S(1)}, bf16[4,128,128]{2,1,0:T(8,128)(2,1)S(1)}, u32[]{:S(2)}, u32[]{:S(2)}) %collective-permute-start.6) | collective-permute-done | bytes 131104 | tf_op jit(solution)/shard_map/ppermute | solution.py:439
  50.1 1.8 %collective-permute-done.7.refs_14_ = bf16[4,128,128]{2,1,0:T(8,128)(2,1)S(1)} collective-permute-done((bf16[4,128,128]{2,1,0:T(8,128)(2,1)S(1)}, bf16[4,128,128]{2,1,0:T(8,128)(2,1)S(1)}, u32[]{:S(2)}, u32[]{:S(2)}) %collective-permute-start.7) | collective-permute-done | bytes 131104 | tf_op jit(solution)/shard_map/ppermute | solution.py:439
  52.0 0.0 collective-permute-done.8.refs_15_
  52.0 1.4 %finish.1 = bf16[128,2048]{1,0:T(8,128)(2,1)} custom-call(s32[1]{0:T(128)} %bitcast.group_ref.refs_0_.me_ref, bf16[128,512]{1,0:T(8,128)(2,1)S(1)} %get-tuple-element.110.refs_0_, bf16[128,512]{1,0:T(8,128)(2,1)S(1)} %get-tuple-element.111.refs_1_, bf16[128,512]{1,0:T(8,128)(2,1)S(1)} %get-tuple-element.127.refs_2_, ...), custom_call_target="tpu_custom_call" | custom-call | tf_op jit(solution)/shard_map/finish/pallas_call | solution.py:500
Async XLA Ops:
  0.0 4.0 %copy-start = (f32[3,4,2048]{2,1,0:T(4,128)S(1)}, f32[3,4,2048]{2,1,0:T(4,128)}, u32[]{:S(2)}) copy-start(f32[3,4,2048]{2,1,0:T(4,128)} %refs_5_.3) | copy-start | bytes 294916
  0.0 4.0 %copy-start.2 = (bf16[128,16]{0,1:T(8,128)(2,1)S(1)}, bf16[128,16]{0,1:T(8,128)(2,1)}, u32[]{:S(2)}) copy-start(bf16[128,16]{0,1:T(8,128)(2,1)} %param.12) | copy-start | bytes 12292
  1.0 9.2 %collective-permute-start = (bf16[16,2048]{1,0:T(8,128)(2,1)S(1)}, bf16[16,2048]{1,0:T(8,128)(2,1)S(1)}, u32[]{:S(2)}, u32[]{:S(2)}) collective-permute-start(bf16[16,2048]{1,0:T(8,128)(2,1)S(1)} %tails.1), channel_id=1, source_target_pairs={{0,2},{2,4},{4,6},{6,8},{8,10},{10,12},{12,14},{14,16},{16,18},{18... | collective-permute-start | bytes 196616 | tf_op jit(solution)/shard_map/ppermute | solution.py:389
  12.3 13.1 %collective-permute-start.3 = (bf16[4,128,256]{2,1,0:T(8,128)(2,1)S(1)}, bf16[4,128,256]{2,1,0:T(8,128)(2,1)S(1)}, u32[]{:S(2)}, u32[]{:S(2)}) collective-permute-start(bf16[4,128,256]{2,1,0:T(8,128)(2,1)S(1)} %get-tuple-element.99), channel_id=1, source_target_pairs={{0,6},{2,4},{4,2},{6,0},{1,7},{3,5},{5,3},{7,1},{8,14},{10,12},{12... | collective-permute-start | bytes 786440 | tf_op jit(solution)/shard_map/ppermute | solution.py:439
  14.9 11.1 %collective-permute-start.2 = (bf16[4,128,256]{2,1,0:T(8,128)(2,1)S(1)}, bf16[4,128,256]{2,1,0:T(8,128)(2,1)S(1)}, u32[]{:S(2)}, u32[]{:S(2)}) collective-permute-start(bf16[4,128,256]{2,1,0:T(8,128)(2,1)S(1)} %get-tuple-element.97), channel_id=1, source_target_pairs={{0,4},{2,6},{4,0},{6,2},{1,5},{3,7},{5,1},{7,3},{8,12},{10,14},{12... | collective-permute-start | bytes 786440 | tf_op jit(solution)/shard_map/ppermute | solution.py:439
  17.5 8.5 %collective-permute-start.1 = (bf16[4,128,256]{2,1,0:T(8,128)(2,1)S(1)}, bf16[4,128,256]{2,1,0:T(8,128)(2,1)S(1)}, u32[]{:S(2)}, u32[]{:S(2)}) collective-permute-start(bf16[4,128,256]{2,1,0:T(8,128)(2,1)S(1)} %get-tuple-element.95), channel_id=1, source_target_pairs={{0,2},{2,0},{4,6},{6,4},{1,3},{3,1},{5,7},{7,5},{8,10},{10,8},{12,... | collective-permute-start | bytes 786440 | tf_op jit(solution)/shard_map/ppermute | solution.py:439
  22.1 0.7 %copy-start.1 = (f32[128]{0:T(128)S(1)}, f32[128]{0:T(128)}, u32[]{:S(2)}) copy-start(f32[128]{0:T(128)} %param.15) | copy-start | bytes 1540
  26.8 8.3 %collective-permute-start.4 = (bf16[4,128,256]{2,1,0:T(8,128)(2,1)S(1)}, bf16[4,128,256]{2,1,0:T(8,128)(2,1)S(1)}, u32[]{:S(2)}, u32[]{:S(2)}) collective-permute-start(bf16[4,128,256]{2,1,0:T(8,128)(2,1)S(1)} %get-tuple-element.116.mine_ref), channel_id=1, source_target_pairs={{0,8},{8,0},{16,24},{24,16},{1,9},{9,1},{17,25},{25,17},{2,10},{10... | collective-permute-start | bytes 786440 | tf_op jit(solution)/shard_map/ppermute | solution.py:439
  35.3 8.0 %collective-permute-start.5 = (bf16[4,128,128]{2,1,0:T(8,128)(2,1)S(1)}, bf16[4,128,128]{2,1,0:T(8,128)(2,1)S(1)}, u32[]{:S(2)}, u32[]{:S(2)}) collective-permute-start(bf16[4,128,128]{2,1,0:T(8,128)(2,1)S(1)} %get-tuple-element.140), channel_id=1, source_target_pairs={{0,16},{8,24},{16,0},{24,8},{1,17},{9,25},{17,1},{25,9},{2,18},{10... | collective-permute-start | bytes 393224 | tf_op jit(solution)/shard_map/ppermute | solution.py:439
  43.7 6.4 %collective-permute-start.6 = (bf16[4,128,128]{2,1,0:T(8,128)(2,1)S(1)}, bf16[4,128,128]{2,1,0:T(8,128)(2,1)S(1)}, u32[]{:S(2)}, u32[]{:S(2)}) collective-permute-start(bf16[4,128,128]{2,1,0:T(8,128)(2,1)S(1)} %get-tuple-element.144), channel_id=1, source_target_pairs={{0,2},{2,0},{4,6},{6,4},{1,3},{3,1},{5,7},{7,5},{8,10},{10,8},{12,... | collective-permute-start | bytes 393224 | tf_op jit(solution)/shard_map/ppermute | solution.py:439
  44.2 7.8 %collective-permute-start.7 = (bf16[4,128,128]{2,1,0:T(8,128)(2,1)S(1)}, bf16[4,128,128]{2,1,0:T(8,128)(2,1)S(1)}, u32[]{:S(2)}, u32[]{:S(2)}) collective-permute-start(bf16[4,128,128]{2,1,0:T(8,128)(2,1)S(1)} %get-tuple-element.145), channel_id=1, source_target_pairs={{0,4},{2,6},{4,0},{6,2},{1,5},{3,7},{5,1},{7,3},{8,12},{10,14},{12... | collective-permute-start | bytes 393224 | tf_op jit(solution)/shard_map/ppermute | solution.py:439
  45.9 6.1 %collective-permute-start.8 = (bf16[4,128,128]{2,1,0:T(8,128)(2,1)S(1)}, bf16[4,128,128]{2,1,0:T(8,128)(2,1)S(1)}, u32[]{:S(2)}, u32[]{:S(2)}) collective-permute-start(bf16[4,128,128]{2,1,0:T(8,128)(2,1)S(1)} %get-tuple-element.146), channel_id=1, source_target_pairs={{0,6},{2,4},{4,2},{6,0},{1,7},{3,5},{5,3},{7,1},{8,14},{10,12},{12... | collective-permute-start | bytes 393224 | tf_op jit(solution)/shard_map/ppermute | solution.py:439

commit v3 on v2

--- a/solution.py
+++ b/solution.py
@@ -1,4 +1,5 @@
 import functools
+import itertools
 
 import jax
 import jax.numpy as jnp
@@ -12,6 +13,7 @@
 EDGE = 16
 F32 = jnp.float32
 BF16 = jnp.bfloat16
+FIRST = 1
 VMEM_LIMIT = 32 * 1024 * 1024
 
 
@@ -41,7 +43,8 @@
 
 
 def silu(u):
-    return u / (1.0 + jnp.exp(-u))
+    half = 0.5 * u
+    return half + half * jnp.tanh(half)
 
 
 def conv(x, taps):
@@ -83,17 +86,10 @@
 def prepare_kernel(
     groups, g_ref, k_ref, v_ref, beta_ref, taps_ref,
     write_ref, low_ref, kin_ref, khi_ref, klo_ref, vb_ref, up_ref, down_ref, marks_ref, edge_ref, rates_ref,
-    held, sems,
 ):
     rows, width = g_ref.shape
     cols = width // groups
     heads = cols // D
-    copies = {}
-    for i in range(groups):
-        for n, ref in enumerate((g_ref, k_ref, v_ref)):
-            c = pl.ds(i * cols, cols)
-            copies[n, i] = pltpu.make_async_copy(ref.at[:, c], held.at[n, :, c], sems.at[n, i])
-            copies[n, i].start()
     middle = rows // 2 - 1
     at, other = iota((rows, rows), 0), iota((rows, rows), 1)
     plus = jnp.where((other <= at) & (other > middle), 1.0, 0.0)
@@ -104,18 +100,16 @@
     lane = iota(rates.shape, 1)
     for i in range(groups):
         whole = slice(i * cols, (i + 1) * cols)
-        copies[0, i].wait()
-        sums = dot(summing, held[0, :, whole])
+        sums = dot(summing, g_ref[:, whole])
         up = jnp.exp(sums)
         down = jnp.exp(-sums)
         up_ref[:, whole] = up
         down_ref[:, whole] = down[:EDGE]
-        mid = jnp.exp(held[0, 0:EDGE, whole].astype(F32)[0:1] - sums[0:1])
+        mid = jnp.exp(g_ref[0:EDGE, whole].astype(F32)[0:1] - sums[0:1])
         end = up[rows - 1 : rows]
         marks_ref[:, whole] = jnp.concatenate([mid, end] * 4, 0)
-        copies[1, i].wait()
-        edge_ref[0, :, whole] = held[1, 0:EDGE, whole]
-        keys = conv(held[1, :, whole].astype(F32), taps_ref[1, :, whole])
+        edge_ref[0, :, whole] = k_ref[0:EDGE, whole]
+        keys = conv(k_ref[:, whole].astype(F32), taps_ref[1, :, whole])
         for h in range(heads):
             c = slice(h * D, (h + 1) * D)
             to = slice((i * heads + h) * D, (i * heads + h + 1) * D)
@@ -123,9 +117,8 @@
             out = key_terms(keys[:, c], rate, up[:, c], down[:, c], mid[:, c], end[:, c])
             for ref, value in zip((write_ref, low_ref, kin_ref, khi_ref, klo_ref), out):
                 ref[:, to] = value
-        copies[2, i].wait()
-        edge_ref[1, :, whole] = held[2, 0:EDGE, whole]
-        values = conv(held[2, :, whole].astype(F32), taps_ref[2, :, whole])
+        edge_ref[1, :, whole] = v_ref[0:EDGE, whole]
+        values = conv(v_ref[:, whole].astype(F32), taps_ref[2, :, whole])
         for h in range(heads):
             to = slice((i * heads + h) * D, (i * heads + h + 1) * D)
             rate = jnp.sum(jnp.where(lane == i * heads + h, rates, 0.0), -1, keepdims=True)
@@ -166,14 +159,21 @@
         take = lambda x: jnp.concatenate([x[s] for s in lower], 0)
         small_mask = take(mask)
         parts = [split(x) for x in full]
-        links = [split(jnp.where(small_mask, take(low), 0.0)) for low in lows]
+        links = []
+        for low in lows:
+            masked = jnp.where(small_mask, take(low), 0.0)
+            total = masked[:size]
+            for p in range(1, rows // (2 * size)):
+                total = total + masked[p * size : (p + 1) * size]
+            links.append(split(total))
         inner = [dot3(link, part) for link, part in zip(links, parts)]
         zeros = jnp.zeros((size, rows), F32)
         spread = []
         for x in inner:
             pieces = []
             for p in range(rows // (2 * size)):
-                pieces += [zeros, x[p * size : (p + 1) * size]]
+                own = jnp.where(iota((size, rows), 1) // (2 * size) == p, x, 0.0) if 2 * size < rows else x
+                pieces += [zeros, own]
             spread.append(split(jnp.concatenate(pieces, 0)))
         fixes = [dot3((take(part[0]), take(part[1])), s) for part, s in zip(parts, spread)]
         result = []
@@ -270,81 +270,150 @@
             seen = both[:rows] + both[rows:]
             reach_ref[:, c] = (queries[:, c] * mid[:, c] - seen[:, :D]).astype(BF16)
             own_ref[:, c] = seen[:, D:]
-            scale_ref[:, c] = gain_ref[...] / (1.0 + jnp.exp(-gate[:, c]))
-
-
-def follow(pair, state):
-    add = pair[:, D:] if state.shape[1] == D else pair
-    return (state.astype(F32) + add.astype(F32) + dot(pair[:, :D], state)).astype(BF16)
+            scale_ref[:, c] = gain_ref[...] * (0.5 + 0.5 * jnp.tanh(0.5 * gate[:, c]))
+
+
+def follow(move, add, ahead):
+    return (ahead.astype(F32) + add.astype(F32) + dot(move, ahead)).astype(BF16)
+
+
+def follow_pair(pair, ahead):
+    return follow(pair[:, :D], pair, ahead)
 
 
 def chain_kernel(me_ref, *refs):
-    pairs, before_ref, whole_ref = refs[:-2], refs[-2], refs[-1]
-    count = len(pairs)
-    heads = whole_ref.shape[0]
-    for m in range(count):
+    pairs, move_ref, add_ref = refs[:-2], refs[-2], refs[-1]
+    heads = move_ref.shape[0]
+    for m in range(len(pairs)):
+
+        @pl.when(me_ref[0] == m)
+        def _():
+            steps = [[pairs[m ^ b][h] for h in range(heads)] for b in range(len(pairs))]
+            while len(steps) > 1:
+                steps = [
+                    [follow_pair(steps[b + 1][h], steps[b][h]) for h in range(heads)] for b in range(0, len(steps), 2)
+                ]
+            for h in range(heads):
+                move_ref[h] = steps[0][h][:, :D]
+                add_ref[h] = steps[0][h][:, D:]
+
+
+def prefix_kernel(me_ref, *refs):
+    pairs, before_ref = refs[:-1], refs[-1]
+    heads = before_ref.shape[1]
+    for m in range(len(pairs)):
 
         @pl.when(me_ref[0] == m)
         def _():
             now = [pairs[m][h] for h in range(heads)]
-            for b in range(1, count):
+            for b in range(len(pairs) - 1):
                 for h in range(heads):
-                    before_ref[b - 1, h] = now[h]
-                    now[h] = follow(pairs[m ^ b][h], now[h])
-            for h in range(heads):
-                whole_ref[h] = now[h]
-
-
-def absorb_kernel(wide, last, upper_ref, mine_ref, theirs_ref, *refs):
-    have_ref, (send_ref, ahead_ref) = (refs[0], refs[1:]) if wide else (None, refs)
-    part = slice(D, 2 * D) if last else slice(0, 2 * D)
-    heads = mine_ref.shape[0]
-    for upper in (0, 1):
-
-        @pl.when(upper_ref[0] == upper)
+                    if b:
+                        now[h] = follow_pair(pairs[m ^ b][h], now[h])
+                    before_ref[b, h] = now[h]
+
+
+def absorb_kernel(count, wide, sends, which_ref, *refs):
+    parts, refs = refs[:count], refs[count:]
+    if sends:
+        own_move, own_add, refs = refs[0], refs[1], refs[2:]
+    have, outs = (refs[:2], refs[2:]) if wide else (None, refs)
+    heads = parts[0].shape[0]
+    for d in range(-1, count):
+
+        @pl.when(which_ref[0] == d)
         def _():
             for h in range(heads):
-                mine, theirs = mine_ref[h], theirs_ref[h]
-                first, then = (theirs, mine) if upper else (mine, theirs)
-                send_ref[h] = follow(then, first[:, part])
-                if upper:
-                    ahead_ref[h] = follow(have_ref[h], theirs) if wide else theirs
+                if d < 0:
+                    ahead = have[1][h] if wide else jnp.zeros(parts[0].shape[1:], BF16)
                 else:
-                    ahead_ref[h] = have_ref[h] if wide else jnp.zeros(theirs.shape, BF16)
-
-
-def starts_kernel(me_ref, upper_ref, came_ref, ahead_ref, before_ref, *outs):
-    heads = came_ref.shape[0]
-    first = []
-    for h in range(heads):
-        came = jnp.where(upper_ref[0] > 0, came_ref[h].astype(F32), 0.0).astype(BF16)
-        first.append(follow(ahead_ref[h], came))
+                    ahead = follow(have[0][h], have[1][h], parts[d][h]) if wide else parts[d][h]
+                outs[0][h] = ahead
+                if sends:
+                    outs[1][h] = follow(own_move[h], own_add[h], ahead)
+
+
+def absorb_four_kernel(span_ref, move_ref, add_ref, came_ref, ahead_ref, state_ref, mixed_ref):
+    for upper in (0, 1):
+
+        @pl.when(span_ref[0] & 1 == upper)
+        def _():
+            for h in range(add_ref.shape[0]):
+                ahead = came_ref[h] if upper else jnp.zeros(came_ref.shape[1:], BF16)
+                state = follow(move_ref[h], add_ref[h], ahead) if upper else add_ref[h]
+                ahead_ref[h] = ahead
+                state_ref[h] = state
+                mixed_ref[h] = state if upper else move_ref[h]
+
+
+def starts_four_kernel(me_ref, span_ref, ahead_ref, near_ref, far_ref, before_ref, *outs):
+    heads = ahead_ref.shape[0]
+
+    def state_ahead(h):
+        both = follow(near_ref[h], ahead_ref[h], far_ref[h])
+        state = jnp.where(span_ref[0] == 3, both.astype(F32), ahead_ref[h].astype(F32))
+        return jnp.where(span_ref[0] == 2, near_ref[h].astype(F32), state).astype(BF16)
+
+    give_starts(me_ref, before_ref, [state_ahead(h) for h in range(heads)], outs)
+
+
+def give_starts(me_ref, before_ref, first, outs):
+    heads = len(first)
+    later = [
+        [follow(before_ref[b, h, :, :D], before_ref[b, h, :, D:], first[h]) for h in range(heads)]
+        for b in range(len(outs) - 1)
+    ]
     for m in range(len(outs)):
 
         @pl.when(me_ref[0] == m)
         def _():
             for b in range(len(outs)):
                 for h in range(heads):
-                    outs[m ^ b][h] = follow(before_ref[b - 1, h], first[h]) if b else first[h]
-
-
-def finish_kernel(count, me_ref, *refs):
-    out_ref = refs[-1]
+                    outs[m ^ b][h] = later[b - 1][h] if b else first[h]
+
+
+def starts_kernel(count, me_ref, which_ref, *refs):
+    parts, (move_ref, add_ref, before_ref, *outs) = refs[:count], refs[count:]
+    heads = move_ref.shape[0]
+
+    def state_ahead(h):
+        came = jnp.zeros(move_ref.shape[1:], F32)
+        for d in range(count):
+            came = jnp.where(which_ref[0] == d, parts[d][h].astype(F32), came)
+        return follow(move_ref[h], add_ref[h], came.astype(BF16))
+
+    give_starts(me_ref, before_ref, [state_ahead(h) for h in range(heads)], outs)
+
+
+def finish_kernel(count, more, *refs):
+    groups, refs = refs[:count], refs[count:]
+    refs = refs[1:] if more else refs
     reach, own, scale, starts = (refs[k * count : (k + 1) * count] for k in range(4))
+    out_ref, held, sems = refs[4 * count :]
     heads = starts[0].shape[0]
-    for m in range(count):
-
-        @pl.when(me_ref[0] == m)
-        def _():
-            for g in range(count):
-                j = m ^ g
-                for h in range(heads):
-                    c = slice(h * D, (h + 1) * D)
-                    found = own[j][:, c] + dot(reach[j][:, c], starts[j][h])
-                    found = found.astype(BF16).astype(F32)
-                    mean = jnp.mean(found * found, -1, keepdims=True)
-                    at = slice((g * heads + h) * D, (g * heads + h + 1) * D)
-                    out_ref[:, at] = (found * lax.rsqrt(mean + 1e-5) * scale[j][:, c]).astype(BF16)
+    cols = heads * D
+    copies = []
+    for n in range(count):
+        for h in range(heads):
+            c = slice(h * D, (h + 1) * D)
+            found = own[n][:, c] + dot(reach[n][:, c], starts[n][h])
+            found = found.astype(BF16).astype(F32)
+            mean = jnp.mean(found * found, -1, keepdims=True)
+            held[n, :, c] = (found * lax.rsqrt(mean + 1e-5) * scale[n][:, c]).astype(BF16)
+        to = pl.ds(pl.multiple_of(groups[n][0] * cols, cols), cols)
+        copies.append(pltpu.make_async_copy(held.at[n], out_ref.at[:, to], sems.at[n]))
+        copies[n].start()
+    for copy in copies:
+        copy.wait()
+
+
+def whole_route(pairs, count):
+    sources = [i for i in range(count) if i not in [a for a, _ in pairs]]
+    targets = [i for i in range(count) if i not in [b for _, b in pairs]]
+    if len(sources) <= 5:
+        cost = lambda order: sum(abs(a - b) if a != b else count * count for a, b in zip(sources, order))
+        targets = min(itertools.permutations(targets), key=cost)
+    return pairs + list(zip(sources, targets))
 
 
 def params():
@@ -362,11 +431,13 @@
     span = lax.axis_index("ctx").astype(jnp.int32).reshape(1)
     group_ids = [me ^ j for j in range(groups)]
     later = (me + span > 0).astype(jnp.int32)
-    uppers = [(span >> bit) & 1 for bit in range((spans - 1).bit_length())]
-    (group_ids, later, uppers), query_raw, key_raw, value_raw, log_decay = lax.optimization_barrier(
-        ((group_ids, later, uppers), query_raw, key_raw, value_raw, log_decay)
+    rounds = (spans - 1).bit_length()
+    places = [jnp.where((span >> r) & 1 > 0, span & ((1 << r) - 1), -1) for r in range(rounds)]
+    (group_ids, later, places, span), query_raw, key_raw, value_raw, log_decay = lax.optimization_barrier(
+        ((group_ids, later, places, span), query_raw, key_raw, value_raw, log_decay)
     )
     me_arg = group_ids[0]
+    near = [pltpu.with_memory_space_constraint(x, pltpu.VMEM) for x in (log_decay, key_raw, value_raw)]
     query_raw, key_raw, value_raw, log_decay, out_gate = (
         pltpu.with_memory_space_constraint(x, pltpu.HBM) for x in (query_raw, key_raw, value_raw, log_decay, out_gate)
     )
@@ -391,7 +462,7 @@
     wide16 = jax.ShapeDtypeStruct((rows, width), BF16)
     prepared = pl.pallas_call(
         functools.partial(prepare_kernel, groups),
-        in_specs=[far] * 3 + [vmem] * 2,
+        in_specs=[vmem] * 5,
         out_specs=[vmem] * 11,
         out_shape=[wide16] * 6
         + [
@@ -401,11 +472,10 @@
             jax.ShapeDtypeStruct((2, EDGE, width), BF16),
             jax.ShapeDtypeStruct((EDGE, beta.shape[0]), F32),
         ],
-        scratch_shapes=[pltpu.VMEM((3, rows, width), BF16), pltpu.SemaphoreType.DMA((3, groups))],
         compiler_params=params(),
         cost_estimate=pl.CostEstimate(flops=20_000_000, bytes_accessed=9_000_000, transcendentals=2_000_000),
         name="prepare",
-    )(log_decay, key_raw, value_raw, beta, conv_weight)
+    )(*near, beta, conv_weight)
     write, low, kin, khi, klo, vb, up, down, marks, edges, rates = prepared
 
     moves, made, lows = [None] * groups, [None] * groups, [None] * groups
@@ -460,50 +530,82 @@
     left = list(range(groups))
     came_pairs, found = lax.optimization_barrier((came_pairs, local(left[: groups // 2])))
     left = left[groups // 2 :]
-
-    before, whole = call(
-        chain_kernel, "chain", [smem] + [vmem] * groups, [((groups - 1, heads, D, 2 * D), BF16), pair]
+    move, add = call(chain_kernel, "chain", [smem] + [vmem] * groups, [state] * 2)(me_arg, *came_pairs)
+
+    def tell(array, r):
+        half = 1 << r
+        routes = [
+            [(low + half - 1, low + half + d) for low in range(0, spans, 2 * half) if low + half + d < spans]
+            for d in range(half)
+        ]
+        return [lax.ppermute(array, "ctx", whole_route(route, spans)) for route in routes if route]
+
+    def absorb(r, parts, own, have):
+        wide, sends = have is not None, own is not None
+        return call(
+            functools.partial(absorb_kernel, len(parts), wide, sends),
+            "absorb",
+            [smem] + [vmem] * (len(parts) + 2 * wide + 2 * sends),
+            [state] * (1 + sends),
+        )(places[r], *parts, *(own or ()), *(have or ()))
+
+    adds = tell(add, 0) if rounds else []
+    ahead, send_move = None, move
+    if spans == 4:
+        ahead, told, mixed = call(absorb_four_kernel, "absorb", [smem] + [vmem] * 3, [state] * 3)(
+            span, move, add, adds[0]
+        )
+        adds = [
+            lax.ppermute(mixed, "ctx", whole_route([(0, 1), (1, 2), (2, 3)], 4)),
+            lax.ppermute(told, "ctx", [(1, 3), (3, 2), (2, 1), (0, 0)]),
+        ]
+    for r in range(rounds - 1 if spans != 4 else 0):
+        moves_in = tell(send_move, r)
+        got_add = absorb(r, adds, (move, add), ahead)
+        adds = tell(got_add[1], r + 1)
+        more = r + 2 < rounds
+        got_move = absorb(r, moves_in, (move, move) if more else None, (ahead[0], ahead[0]) if ahead else None)
+        ahead = (got_move[0], got_add[0])
+        send_move = got_move[1] if more else None
+    (before,) = call(
+        prefix_kernel, "prefix", [smem] + [vmem] * groups, [((groups - 1, heads, D, 2 * D), BF16)]
     )(me_arg, *came_pairs)
-
-    ahead, bit, send = None, 1, whole if spans > 2 else whole[:, :, D:]
-    came, upper = None, later
-    while bit < spans:
-        last = 2 * bit >= spans
-        theirs = swap(send, bit, "ctx")
-        if left:
-            theirs, mine = lax.optimization_barrier((theirs, local(left)))
-            found.update(mine)
-            left = []
-        upper = uppers[bit.bit_length() - 1]
-        if last:
-            came = theirs
-        else:
-            wide, next_last = ahead is not None, 4 * bit >= spans
-            send, ahead = call(
-                functools.partial(absorb_kernel, wide, next_last),
-                "absorb",
-                [smem] + [vmem] * (3 if wide else 2),
-                [state if next_last else pair, pair],
-            )(upper, whole, theirs, *([ahead] if wide else []))
-            whole = send
-        bit *= 2
-    found.update(local(left))
-    came = jnp.zeros(*state) if came is None else came
-    ahead = jnp.zeros(*pair) if ahead is None else ahead
-
-    starts = call(starts_kernel, "starts", [smem] * 2 + [vmem] * 3, [state] * groups)(
-        me_arg, upper, came, ahead, before
-    )
+    adds, before, mine = lax.optimization_barrier((adds, before, local(left)))
+    found.update(mine)
+    if spans == 4:
+        starts = call(starts_four_kernel, "starts", [smem] * 2 + [vmem] * 4, [state] * groups)(
+            me_arg, span, ahead, *adds, before
+        )
+    else:
+        ahead = (jnp.zeros(*state),) * 2 if ahead is None else ahead
+        starts = call(
+            functools.partial(starts_kernel, len(adds)),
+            "starts",
+            [smem] * 2 + [vmem] * (len(adds) + 3),
+            [state] * groups,
+        )(me_arg, places[-1] if rounds else later, *adds, *ahead, before)
     starts = [starts[0]] + [swap(starts[j], j) for j in range(1, groups)]
 
-    reach, own, scale = zip(*[found[j] for j in range(groups)])
-    (out,) = call(
-        functools.partial(finish_kernel, groups),
-        "finish",
-        [smem] + [vmem] * (4 * groups),
-        [((rows, width), BF16)],
-    )(me_arg, *reach, *own, *scale, *starts)
-    return out
+    def finish(js, out):
+        more = out is not None
+        return pl.pallas_call(
+            functools.partial(finish_kernel, len(js), more),
+            in_specs=[smem] * len(js) + [far] * more + [vmem] * (4 * len(js)),
+            out_specs=far,
+            out_shape=jax.ShapeDtypeStruct((rows, width), BF16),
+            scratch_shapes=[pltpu.VMEM((len(js), rows, cols), BF16), pltpu.SemaphoreType.DMA((len(js),))],
+            input_output_aliases={len(js): 0} if more else {},
+            compiler_params=params(),
+            name="finish",
+        )(
+            *[group_ids[j] for j in js], *([out] if more else []),
+            *[found[j][k] for k in range(3) for j in js], *[starts[j] for j in js],
+        )
+
+    first = [j for j in (0, FIRST) if j < groups]
+    rest = [j for j in range(groups) if j not in first]
+    out = finish(first, None)
+    return finish(rest, out) if rest else out
 
 
 def solution(mesh):

time: 53.5 us -> 48.7 us (0.910)
  waiting for transfers between devices: 19 us -> 14.5 us
  Pallas kernels: 21.5 us -> 20.3 us
  local copies, waits for them, and re-layouts: 0.66 us -> 1.7 us
    ppermute x8 -> x6, waiting for transfers between devices: 17.1 us -> 2.71 us  [swap(): lax.ppermute(array, axis, [(i, i ^ j) for i in range(lax.axis_size(axis))])]
    ppermute x0 -> x3, waiting for transfers between devices: none -> 9.11 us  [the longest x1 5.41 us: tell(): lax.ppermute(array, 'ctx', whole_route(route, spans))]
    ppermute x8 -> x6, starting transfers between devices: 9.04 us -> 7.21 us  [swap(): lax.ppermute(array, axis, [(i, i ^ j) for i in range(lax.axis_size(axis))])]
    ppermute x0 -> x3, starting transfers between devices: none -> 1.38 us  [the longest x1 0.84 us: shards(): lax.ppermute(told, 'ctx', [(1, 3), (3, 2), (2, 1), (0, 0)])]
    pallas_call x5 -> x7, Pallas kernels: 7.12 us -> 6.04 us  [the longest x1 2.52 us: shards(): pl.pallas_call(functools.partial(prepare_kernel, groups), in_specs=[vmem]...]
    unnamed x6 -> x12, local copies, waits for them, and re-layouts: 0.66 us -> 1.7 us
    ppermute x1, waiting for transfers between devices: 1.91 us -> 2.65 us  [shards(): lax.ppermute(tails, ('ctx', 'head'), [(i, (i + 1) % total) for i in range...]
  transfers between devices with their start and end apart: 9 -> 10, of which waited for: 6 -> 6; matrix products, arithmetic and copies ran while one was open for 0% -> 0% of each run, Pallas kernels for 29% -> 31%
where the time goes in v3:
time: 48.7 us; the launch traced here: 48.4 us
  Pallas kernels  20.3 us (42%)
  waiting for transfers between devices  14.5 us (30%)
  starting transfers between devices  11.6 us (24%)
  local copies, waits for them, and re-layouts  1.7 us (3%)
    pallas_call x4, Pallas kernels, shards(): pl.pallas_call(block_kernel, in_specs=[smem] * 2 + [vmem] * 13, out_specs...  7.91 us
    ppermute x6, starting transfers between devices, swap(): lax.ppermute(array, axis, [(i, i ^ j) for i in range(lax.axis_size(axis))])  7.21 us
    ppermute x1, waiting for transfers between devices, tell(): lax.ppermute(array, 'ctx', whole_route(route, spans))  5.41 us
    pallas_call x2, Pallas kernels, local(): call(functools.partial(local_kernel, len(js)), 'local', [smem] * (1 + len...  5.28 us
    ppermute x1, waiting for transfers between devices, shards(): lax.ppermute(mixed, 'ctx', whole_route([(0, 1), (1, 2), (2, 3)], 4))  3.71 us
    ppermute x1, starting transfers between devices, shards(): lax.ppermute(tails, ('ctx', 'head'), [(i, (i + 1) % total) for i in range...  3 us
    ppermute x6, waiting for transfers between devices, swap(): lax.ppermute(array, axis, [(i, i ^ j) for i in range(lax.axis_size(axis))])  2.71 us
    ppermute x1, waiting for transfers between devices, shards(): lax.ppermute(tails, ('ctx', 'head'), [(i, (i + 1) % total) for i in range...  2.65 us
  transfers between devices with their start and end apart: 10, of which 6 were waited for; matrix products, arithmetic and copies ran while one was open for 0% of the time, Pallas kernels for 31%

profile of v3, /device:TPU:0, one launch (start us, length us, event | category | flops | bytes accessed | tf_op | source)
XLA Modules:
  0.0 48.4 jit_solution(5173628295821091850)
XLA Ops:
  0.0 0.0 copy-start
  0.0 0.0 copy-start.1
  0.0 0.0 copy-start.2
  0.0 0.0 copy-start.5
  0.0 1.0 %tails.1 = bf16[16,2048]{1,0:T(8,128)(2,1)S(1)} custom-call(bf16[128,2048]{1,0:T(8,128)(2,1)} %refs_3_.1, bf16[128,2048]{1,0:T(8,128)(2,1)} %k_ref, bf16[128,2048]{1,0:T(8,128)(2,1)} %v_ref), custom_call_target="tpu_custom_call" | custom-call | tf_op jit(solution)/shard_map/tails/pallas_call | solution.py:450
  1.1 3.0 %collective-permute-start = (bf16[16,2048]{1,0:T(8,128)(2,1)S(1)}, bf16[16,2048]{1,0:T(8,128)(2,1)S(1)}, u32[]{:S(2)}, u32[]{:S(2)}) collective-permute-start(bf16[16,2048]{1,0:T(8,128)(2,1)S(1)} %tails.1), channel_id=1, source_target_pairs={{0,2},{2,4},{4,6},{6,8},{8,10},{10,12},{12,14},{14,16},{16,18},{18... | collective-permute-start | bytes 196616 | tf_op jit(solution)/shard_map/ppermute | solution.py:460
  4.1 0.0 copy-done
  4.1 0.0 copy-done.1
  4.1 0.0 copy-done.2
  4.1 0.0 copy-done.5
  4.1 0.0 copy-start.4
  4.1 1.0 %copy-done.4 = bf16[128,2048]{1,0:T(8,128)(2,1)S(1)} copy-done((bf16[128,2048]{1,0:T(8,128)(2,1)S(1)}, bf16[128,2048]{1,0:T(8,128)(2,1)}, u32[]{:S(2)}) %copy-start.4) | copy-done | bytes 524312
  5.1 2.5 %prepare.1 = (bf16[128,2048]{1,0:T(8,128)(2,1)S(1)}, bf16[128,2048]{1,0:T(8,128)(2,1)S(1)}, bf16[128,2048]{1,0:T(8,128)(2,1)S(1)}, bf16[128,2048]{1,0:T(8,128)(2...) custom-call(bf16[128,2048]{1,0:T(8,128)(2,1)S(1)} %copy-done.4, ...), custom_call_target="tpu_custom_call" | custom-call | flops 20000000 | bytes 9000000 | tf_op jit(solution)/shard_map/prepare/pallas_call | solution.py:463
  7.6 2.7 %collective-permute-done.rim_ref.refs_2_ = bf16[16,2048]{1,0:T(8,128)(2,1)S(1)} collective-permute-done((bf16[16,2048]{1,0:T(8,128)(2,1)S(1)}, bf16[16,2048]{1,0:T(8,128)(2,1)S(1)}, u32[]{:S(2)}, u32[]{:S(2)}) %collective-permute-start) | collective-permute-done | bytes 65568 | tf_op jit(solution)/shard_map/ppermute | solution.py:460
  10.3 2.0 %block.7 = (bf16[4,128,256]{2,1,0:T(8,128)(2,1)S(1)}, bf16[4,128,256]{2,1,0:T(8,128)(2,1)S(1)}, bf16[128,512]{1,0:T(8,128)(2,1)S(1)}) custom-call(s32[1]{0:T(128)S(6)} %xor.11.group_ref.refs_1_, s32[1]{0:T(128)S(6)} %convert_element_type.3.later_ref, bf16[16,2048]{1,0:T(8,128)(2,1)S(1)} %collective-permute-done.rim_ref.refs_2_, ...), custom_call_target="tpu_custom_call" | custom-call | tf_op jit(solution)/shard_map/block/pallas_call | solution.py:484
  12.3 0.1 collective-permute-start.3
  12.4 2.0 %block.6 = (bf16[4,128,256]{2,1,0:T(8,128)(2,1)S(1)}, bf16[4,128,256]{2,1,0:T(8,128)(2,1)S(1)}, bf16[128,512]{1,0:T(8,128)(2,1)S(1)}) custom-call(s32[1]{0:T(128)S(6)} %xor.10.group_ref.refs_0_, s32[1]{0:T(128)S(6)} %convert_element_type.3.later_ref, bf16[16,2048]{1,0:T(8,128)(2,1)S(1)} %collective-permute-done.rim_ref.refs_2_, ...), custom_call_target="tpu_custom_call" | custom-call | tf_op jit(solution)/shard_map/block/pallas_call | solution.py:484
  14.4 0.3 collective-permute-start.2
  14.7 2.0 %block.5 = (bf16[4,128,256]{2,1,0:T(8,128)(2,1)S(1)}, bf16[4,128,256]{2,1,0:T(8,128)(2,1)S(1)}, bf16[128,512]{1,0:T(8,128)(2,1)S(1)}) custom-call(s32[1]{0:T(128)S(6)} %xor.9.group_ref.refs_1_, s32[1]{0:T(128)S(6)} %convert_element_type.3.later_ref, bf16[16,2048]{1,0:T(8,128)(2,1)S(1)} %collective-permute-done.rim_ref.refs_2_, ...), custom_call_target="tpu_custom_call" | custom-call | tf_op jit(solution)/shard_map/block/pallas_call | solution.py:484
  16.7 3.2 %collective-permute-start.1 = (bf16[4,128,256]{2,1,0:T(8,128)(2,1)S(1)}, bf16[4,128,256]{2,1,0:T(8,128)(2,1)S(1)}, u32[]{:S(2)}, u32[]{:S(2)}) collective-permute-start(bf16[4,128,256]{2,1,0:T(8,128)(2,1)S(1)} %get-tuple-element.99), channel_id=1, source_target_pairs={{0,2},{2,0},{4,6},{6,4},{1,3},{3,1},{5,7},{7,5},{8,10},{10,8},{12,... | collective-permute-start | bytes 786440 | tf_op jit(solution)/shard_map/ppermute | solution.py:509
  19.9 2.0 %block.4 = (bf16[4,128,256]{2,1,0:T(8,128)(2,1)S(1)}, bf16[4,128,256]{2,1,0:T(8,128)(2,1)S(1)}, bf16[128,512]{1,0:T(8,128)(2,1)S(1)}) custom-call(s32[1]{0:T(128)} %bitcast.group_ref.refs_0_.me_ref, s32[1]{0:T(128)S(6)} %convert_element_type.3.later_ref, bf16[16,2048]{1,0:T(8,128)(2,1)S(1)} %collective-permute-done.rim_ref.refs_2_, ...), custom_call_target="tpu_custom_call" | custom-call | tf_op jit(solution)/shard_map/block/pallas_call | solution.py:484
  21.9 0.0 copy-start.3
  21.9 0.6 %copy-done.3 = f32[128]{0:T(128)S(1)} copy-done((f32[128]{0:T(128)S(1)}, f32[128]{0:T(128)}, u32[]{:S(2)}) %copy-start.3) | copy-done | bytes 536
  22.6 2.6 %local.2 = (bf16[128,512]{1,0:T(8,128)(2,1)S(1)}, f32[128,512]{1,0:T(8,128)S(1)}, f32[128,512]{1,0:T(8,128)S(1)}, bf16[128,512]{1,0:T(8,128)(2,1)S(1)}, f32[128,512]{1,0:T(8,128)S(1)}, /*index=5*/f32[128,512]{1,0:T(8,128)S(1)}) custom-call(s32[1]{0:T(128)S(6)} %convert_element_type.3.later_ref, s32[1]{0:T(128)} %bitcast.group_ref.refs_0_.me_ref, ...), custom_call_target="tpu_custom_call" | custom-call | tf_op jit(solution)/shard_map/local/pallas_call | solution.py:517
  25.2 0.0 collective-permute-done.3.refs_3_
  25.2 0.8 %collective-permute-done.2.refs_2_ = bf16[4,128,256]{2,1,0:T(8,128)(2,1)S(1)} collective-permute-done((bf16[4,128,256]{2,1,0:T(8,128)(2,1)S(1)}, bf16[4,128,256]{2,1,0:T(8,128)(2,1)S(1)}, u32[]{:S(2)}, u32[]{:S(2)}) %collective-permute-start.2) | collective-permute-done | bytes 262176 | tf_op jit(solution)/shard_map/ppermute | solution.py:509
  26.0 0.0 collective-permute-done.1.refs_1_
  26.0 0.5 chain.1
  26.5 0.1 collective-permute-start.4
  26.6 5.4 %collective-permute-done.4.came_ref = bf16[4,128,128]{2,1,0:T(8,128)(2,1)S(1)} collective-permute-done((bf16[4,128,128]{2,1,0:T(8,128)(2,1)S(1)}, bf16[4,128,128]{2,1,0:T(8,128)(2,1)S(1)}, u32[]{:S(2)}, u32[]{:S(2)}) %collective-permute-start.4) | collective-permute-done | bytes 131104 | tf_op jit(solution)/shard_map/ppermute | solution.py:541
  32.0 0.5 collective-permute-start.5
  32.5 0.8 %collective-permute-start.6 = (bf16[4,128,128]{2,1,0:T(8,128)(2,1)S(1)}, bf16[4,128,128]{2,1,0:T(8,128)(2,1)S(1)}, u32[]{:S(2)}, u32[]{:S(2)}) collective-permute-start(bf16[4,128,128]{2,1,0:T(8,128)(2,1)S(1)} %get-tuple-element.127), channel_id=1, source_target_pairs={{8,24},{24,16},{16,8},{0,0},{9,25},{25,17},{17,9},{1,1},{10,26},{2... | collective-permute-start | bytes 393224 | tf_op jit(solution)/shard_map/ppermute | solution.py:560
  33.4 2.6 %local.3 = (bf16[128,512]{1,0:T(8,128)(2,1)S(1)}, f32[128,512]{1,0:T(8,128)S(1)}, f32[128,512]{1,0:T(8,128)S(1)}, bf16[128,512]{1,0:T(8,128)(2,1)S(1)}, f32[128,512]{1,0:T(8,128)S(1)}, /*index=5*/f32[128,512]{1,0:T(8,128)S(1)}) custom-call(s32[1]{0:T(128)S(6)} %convert_element_type.3.later_ref, s32[1]{0:T(128)S(6)} %xor.10.group_ref.refs_0_, ...), custom_call_target="tpu_custom_call" | custom-call | tf_op jit(solution)/shard_map/local/pallas_call | solution.py:517
  36.0 0.4 prefix.1.before_ref
  36.5 3.7 %collective-permute-done.5.near_ref = bf16[4,128,128]{2,1,0:T(8,128)(2,1)S(1)} collective-permute-done((bf16[4,128,128]{2,1,0:T(8,128)(2,1)S(1)}, bf16[4,128,128]{2,1,0:T(8,128)(2,1)S(1)}, u32[]{:S(2)}, u32[]{:S(2)}) %collective-permute-start.5) | collective-permute-done | bytes 131104 | tf_op jit(solution)/shard_map/ppermute | solution.py:559
  40.2 0.0 collective-permute-done.6.far_ref
  40.2 0.5 starts.1
  40.7 0.1 collective-permute-start.7
  40.7 0.5 collective-permute-start.8
  41.2 3.0 %collective-permute-start.9 = (bf16[4,128,128]{2,1,0:T(8,128)(2,1)S(1)}, bf16[4,128,128]{2,1,0:T(8,128)(2,1)S(1)}, u32[]{:S(2)}, u32[]{:S(2)}) collective-permute-start(bf16[4,128,128]{2,1,0:T(8,128)(2,1)S(1)} %get-tuple-element.150), channel_id=1, source_target_pairs={{0,6},{2,4},{4,2},{6,0},{1,7},{3,5},{5,3},{7,1},{8,14},{10,12},{12... | collective-permute-start | bytes 393224 | tf_op jit(solution)/shard_map/ppermute | solution.py:509
  44.2 1.5 %collective-permute-done.7.refs_9_ = bf16[4,128,128]{2,1,0:T(8,128)(2,1)S(1)} collective-permute-done((bf16[4,128,128]{2,1,0:T(8,128)(2,1)S(1)}, bf16[4,128,128]{2,1,0:T(8,128)(2,1)S(1)}, u32[]{:S(2)}, u32[]{:S(2)}) %collective-permute-start.7) | collective-permute-done | bytes 131104 | tf_op jit(solution)/shard_map/ppermute | solution.py:509
  45.7 1.1 %finish.2.refs_2_ = bf16[128,2048]{1,0:T(8,128)(2,1)} custom-call(s32[1]{0:T(128)} %bitcast.group_ref.refs_0_.me_ref, s32[1]{0:T(128)S(6)} %xor.9.group_ref.refs_1_, bf16[128,512]{1,0:T(8,128)(2,1)S(1)} %get-tuple-element.112.refs_2_, bf16[128,512]{1,0:T(8,128)(2,1)S(1)} %get-tuple-element.113.refs_3_, f32[128,512]{1,0:T(8,128)S(1)} %get-tuple-element.114.refs_4_, ...), custom_call_target="tpu_custom_call" | custom-call | tf_op jit(solution)/shard_map/finish/pallas_call | solution.py:591
  46.8 0.0 collective-permute-done.8.refs_9_
  46.8 0.4 collective-permute-done.9.refs_10_
  47.2 1.0 %finish.3 = bf16[128,2048]{1,0:T(8,128)(2,1)} custom-call(s32[1]{0:T(128)S(6)} %xor.10.group_ref.refs_0_, s32[1]{0:T(128)S(6)} %xor.11.group_ref.refs_1_, bf16[128,2048]{1,0:T(8,128)(2,1)} %finish.2.refs_2_, bf16[128,512]{1,0:T(8,128)(2,1)S(1)} %get-tuple-element.143.refs_3_, ...), custom_call_target="tpu_custom_call", output_to_operand_aliasing={{}: (2, {})} | custom-call | tf_op jit(solution)/shard_map/finish/pallas_call | solution.py:591
  (1 shorter events, 0.0 us)
Async XLA Ops:
  0.0 4.1 %copy-start = (f32[3,4,2048]{2,1,0:T(4,128)S(1)}, f32[3,4,2048]{2,1,0:T(4,128)}, u32[]{:S(2)}) copy-start(f32[3,4,2048]{2,1,0:T(4,128)} %refs_5_.3) | copy-start | bytes 294916
  0.0 4.1 %copy-start.1 = (bf16[128,2048]{1,0:T(8,128)(2,1)S(1)}, bf16[128,2048]{1,0:T(8,128)(2,1)}, u32[]{:S(2)}) copy-start(bf16[128,2048]{1,0:T(8,128)(2,1)} %k_ref) | copy-start | bytes 1572868
  0.0 4.1 %copy-start.2 = (bf16[128,2048]{1,0:T(8,128)(2,1)S(1)}, bf16[128,2048]{1,0:T(8,128)(2,1)}, u32[]{:S(2)}) copy-start(bf16[128,2048]{1,0:T(8,128)(2,1)} %v_ref) | copy-start | bytes 1572868
  0.0 4.1 %copy-start.5 = (bf16[128,16]{0,1:T(8,128)(2,1)S(1)}, bf16[128,16]{0,1:T(8,128)(2,1)}, u32[]{:S(2)}) copy-start(bf16[128,16]{0,1:T(8,128)(2,1)} %param.12) | copy-start | bytes 12292
  1.1 9.2 %collective-permute-start = (bf16[16,2048]{1,0:T(8,128)(2,1)S(1)}, bf16[16,2048]{1,0:T(8,128)(2,1)S(1)}, u32[]{:S(2)}, u32[]{:S(2)}) collective-permute-start(bf16[16,2048]{1,0:T(8,128)(2,1)S(1)} %tails.1), channel_id=1, source_target_pairs={{0,2},{2,4},{4,6},{6,8},{8,10},{10,12},{12,14},{14,16},{16,18},{18... | collective-permute-start | bytes 196616 | tf_op jit(solution)/shard_map/ppermute | solution.py:460
  4.1 1.0 %copy-start.4 = (bf16[128,2048]{1,0:T(8,128)(2,1)S(1)}, bf16[128,2048]{1,0:T(8,128)(2,1)}, u32[]{:S(2)}) copy-start(bf16[128,2048]{1,0:T(8,128)(2,1)} %g_ref) | copy-start | bytes 1572868
  12.3 12.9 %collective-permute-start.3 = (bf16[4,128,256]{2,1,0:T(8,128)(2,1)S(1)}, bf16[4,128,256]{2,1,0:T(8,128)(2,1)S(1)}, u32[]{:S(2)}, u32[]{:S(2)}) collective-permute-start(bf16[4,128,256]{2,1,0:T(8,128)(2,1)S(1)} %get-tuple-element.101), channel_id=1, source_target_pairs={{0,6},{2,4},{4,2},{6,0},{1,7},{3,5},{5,3},{7,1},{8,14},{10,12},{12... | collective-permute-start | bytes 786440 | tf_op jit(solution)/shard_map/ppermute | solution.py:509
  14.4 11.7 %collective-permute-start.2 = (bf16[4,128,256]{2,1,0:T(8,128)(2,1)S(1)}, bf16[4,128,256]{2,1,0:T(8,128)(2,1)S(1)}, u32[]{:S(2)}, u32[]{:S(2)}) collective-permute-start(bf16[4,128,256]{2,1,0:T(8,128)(2,1)S(1)} %get-tuple-element.100), channel_id=1, source_target_pairs={{0,4},{2,6},{4,0},{6,2},{1,5},{3,7},{5,1},{7,3},{8,12},{10,14},{12... | collective-permute-start | bytes 786440 | tf_op jit(solution)/shard_map/ppermute | solution.py:509
  16.7 9.4 %collective-permute-start.1 = (bf16[4,128,256]{2,1,0:T(8,128)(2,1)S(1)}, bf16[4,128,256]{2,1,0:T(8,128)(2,1)S(1)}, u32[]{:S(2)}, u32[]{:S(2)}) collective-permute-start(bf16[4,128,256]{2,1,0:T(8,128)(2,1)S(1)} %get-tuple-element.99), channel_id=1, source_target_pairs={{0,2},{2,0},{4,6},{6,4},{1,3},{3,1},{5,7},{7,5},{8,10},{10,8},{12,... | collective-permute-start | bytes 786440 | tf_op jit(solution)/shard_map/ppermute | solution.py:509
  21.9 0.7 %copy-start.3 = (f32[128]{0:T(128)S(1)}, f32[128]{0:T(128)}, u32[]{:S(2)}) copy-start(f32[128]{0:T(128)} %param.15) | copy-start | bytes 1540
  26.5 5.5 %collective-permute-start.4 = (bf16[4,128,128]{2,1,0:T(8,128)(2,1)S(1)}, bf16[4,128,128]{2,1,0:T(8,128)(2,1)S(1)}, u32[]{:S(2)}, u32[]{:S(2)}) collective-permute-start(bf16[4,128,128]{2,1,0:T(8,128)(2,1)S(1)} %get-tuple-element.124.add_ref), channel_id=1, source_target_pairs={{0,8},{16,24},{8,0},{24,16},{1,9},{17,25},{9,1},{25,17},{2,10},{18... | collective-permute-start | bytes 393224 | tf_op jit(solution)/shard_map/ppermute | solution.py:541
  32.0 8.1 %collective-permute-start.5 = (bf16[4,128,128]{2,1,0:T(8,128)(2,1)S(1)}, bf16[4,128,128]{2,1,0:T(8,128)(2,1)S(1)}, u32[]{:S(2)}, u32[]{:S(2)}) collective-permute-start(bf16[4,128,128]{2,1,0:T(8,128)(2,1)S(1)} %get-tuple-element.126), channel_id=1, source_target_pairs={{0,8},{8,16},{16,24},{24,0},{1,9},{9,17},{17,25},{25,1},{2,10},{10... | collective-permute-start | bytes 393224 | tf_op jit(solution)/shard_map/ppermute | solution.py:559
  32.5 7.7 %collective-permute-start.6 = (bf16[4,128,128]{2,1,0:T(8,128)(2,1)S(1)}, bf16[4,128,128]{2,1,0:T(8,128)(2,1)S(1)}, u32[]{:S(2)}, u32[]{:S(2)}) collective-permute-start(bf16[4,128,128]{2,1,0:T(8,128)(2,1)S(1)} %get-tuple-element.127), channel_id=1, source_target_pairs={{8,24},{24,16},{16,8},{0,0},{9,25},{25,17},{17,9},{1,1},{10,26},{2... | collective-permute-start | bytes 393224 | tf_op jit(solution)/shard_map/ppermute | solution.py:560
  40.7 5.0 %collective-permute-start.7 = (bf16[4,128,128]{2,1,0:T(8,128)(2,1)S(1)}, bf16[4,128,128]{2,1,0:T(8,128)(2,1)S(1)}, u32[]{:S(2)}, u32[]{:S(2)}) collective-permute-start(bf16[4,128,128]{2,1,0:T(8,128)(2,1)S(1)} %get-tuple-element.142), channel_id=1, source_target_pairs={{0,2},{2,0},{4,6},{6,4},{1,3},{3,1},{5,7},{7,5},{8,10},{10,8},{12,... | collective-permute-start | bytes 393224 | tf_op jit(solution)/shard_map/ppermute | solution.py:509
  40.7 6.0 %collective-permute-start.8 = (bf16[4,128,128]{2,1,0:T(8,128)(2,1)S(1)}, bf16[4,128,128]{2,1,0:T(8,128)(2,1)S(1)}, u32[]{:S(2)}, u32[]{:S(2)}) collective-permute-start(bf16[4,128,128]{2,1,0:T(8,128)(2,1)S(1)} %get-tuple-element.149), channel_id=1, source_target_pairs={{0,4},{2,6},{4,0},{6,2},{1,5},{3,7},{5,1},{7,3},{8,12},{10,14},{12... | collective-permute-start | bytes 393224 | tf_op jit(solution)/shard_map/ppermute | solution.py:509
  41.2 6.0 %collective-permute-start.9 = (bf16[4,128,128]{2,1,0:T(8,128)(2,1)S(1)}, bf16[4,128,128]{2,1,0:T(8,128)(2,1)S(1)}, u32[]{:S(2)}, u32[]{:S(2)}) collective-permute-start(bf16[4,128,128]{2,1,0:T(8,128)(2,1)S(1)} %get-tuple-element.150), channel_id=1, source_target_pairs={{0,6},{2,4},{4,2},{6,0},{1,7},{3,5},{5,3},{7,1},{8,14},{10,12},{12... | collective-permute-start | bytes 393224 | tf_op jit(solution)/shard_map/ppermute | solution.py:509

commit v4 on v3

--- a/solution.py
+++ b/solution.py
@@ -86,8 +86,11 @@
 def prepare_kernel(
     groups, g_ref, k_ref, v_ref, beta_ref, taps_ref,
     write_ref, low_ref, kin_ref, khi_ref, klo_ref, vb_ref, up_ref, down_ref, marks_ref, edge_ref, rates_ref,
+    held, sem,
 ):
     rows, width = g_ref.shape
+    copy = pltpu.make_async_copy(g_ref, held, sem)
+    copy.start()
     cols = width // groups
     heads = cols // D
     middle = rows // 2 - 1
@@ -100,15 +103,24 @@
     lane = iota(rates.shape, 1)
     for i in range(groups):
         whole = slice(i * cols, (i + 1) * cols)
-        sums = dot(summing, g_ref[:, whole])
+        edge_ref[0, :, whole] = k_ref[0:EDGE, whole]
+        edge_ref[1, :, whole] = v_ref[0:EDGE, whole]
+        values = conv(v_ref[:, whole].astype(F32), taps_ref[2, :, whole])
+        for h in range(heads):
+            to = slice((i * heads + h) * D, (i * heads + h + 1) * D)
+            rate = jnp.sum(jnp.where(lane == i * heads + h, rates, 0.0), -1, keepdims=True)
+            vb_ref[:, to] = (values[:, h * D : (h + 1) * D] * rate).astype(BF16)
+    copy.wait()
+    for i in range(groups):
+        whole = slice(i * cols, (i + 1) * cols)
+        sums = dot(summing, held[:, whole])
         up = jnp.exp(sums)
         down = jnp.exp(-sums)
         up_ref[:, whole] = up
         down_ref[:, whole] = down[:EDGE]
-        mid = jnp.exp(g_ref[0:EDGE, whole].astype(F32)[0:1] - sums[0:1])
+        mid = jnp.exp(held[0:EDGE, whole].astype(F32)[0:1] - sums[0:1])
         end = up[rows - 1 : rows]
         marks_ref[:, whole] = jnp.concatenate([mid, end] * 4, 0)
-        edge_ref[0, :, whole] = k_ref[0:EDGE, whole]
         keys = conv(k_ref[:, whole].astype(F32), taps_ref[1, :, whole])
         for h in range(heads):
             c = slice(h * D, (h + 1) * D)
@@ -117,12 +129,6 @@
             out = key_terms(keys[:, c], rate, up[:, c], down[:, c], mid[:, c], end[:, c])
             for ref, value in zip((write_ref, low_ref, kin_ref, khi_ref, klo_ref), out):
                 ref[:, to] = value
-        edge_ref[1, :, whole] = v_ref[0:EDGE, whole]
-        values = conv(v_ref[:, whole].astype(F32), taps_ref[2, :, whole])
-        for h in range(heads):
-            to = slice((i * heads + h) * D, (i * heads + h + 1) * D)
-            rate = jnp.sum(jnp.where(lane == i * heads + h, rates, 0.0), -1, keepdims=True)
-            vb_ref[:, to] = (values[:, h * D : (h + 1) * D] * rate).astype(BF16)
 
 
 def edge_rows(rim, which, raw, taps):
@@ -144,13 +150,18 @@
         for b in range(1, blocks):
             total = total + own[b * SUB : (b + 1) * SUB]
         packed.append(total)
+    half = SUB // 2
     unit = jnp.where(lane_sub % SUB == iota((SUB, rows), 0), 1.0, 0.0)
-    solved = [unit for _ in lows]
-    group_start = lane_sub - lane_sub % SUB
+    solved = [[unit[:half], unit[half:]] for _ in lows]
+    group_start = (lane_sub - lane_sub % SUB)[:half]
     for j in range(SUB - 1):
         for n, total in enumerate(packed):
-            spread = jnp.take_along_axis(total, group_start + j, axis=1, mode="promise_in_bounds")
-            solved[n] = solved[n] - spread * solved[n][j : j + 1]
+            row = solved[n][j // half][j % half : j % half + 1]
+            for part in range((j + 1) // half, 2):
+                rows_here = total[part * half : (part + 1) * half]
+                spread = jnp.take_along_axis(rows_here, group_start + j, axis=1, mode="promise_in_bounds")
+                solved[n][part] = solved[n][part] - spread * row
+    solved = [jnp.concatenate(parts, 0) for parts in solved]
     full = [jnp.where(same, jnp.concatenate([x] * blocks, 0), 0.0) for x in solved]
     size = SUB
     while size < rows:
@@ -190,52 +201,51 @@
     return full
 
 
-def block_kernel(
-    group_ref, later_ref, rim_ref, edge_ref, rates_ref, taps_ref, up_ref, down_ref, marks_ref,
-    write_ref, low_ref, kin_ref, khi_ref, klo_ref, vb_ref,
-    move_ref, made_ref, low_out_ref,
-):
+def block_kernel(count, later_ref, *refs):
+    group_refs, refs = refs[:count], refs[count:]
+    rim_ref, edge_ref, rates_ref, taps_ref, up_ref, down_ref, marks_ref, *refs = refs
+    write_ref, low_ref, kin_ref, khi_ref, klo_ref, vb_ref, *outs = refs
     rows = low_ref.shape[0]
-    heads = move_ref.shape[0]
+    heads = outs[0].shape[0]
     cols = heads * D
-    start = pl.multiple_of(group_ref[0] * cols, cols)
-    mine = pl.ds(start, cols)
-    rim = jnp.where(later_ref[0] > 0, rim_ref[:, mine].astype(F32), 0.0)
-    keys = edge_rows(rim, 1, edge_ref[0, :, mine], taps_ref[1, :, mine])
-    values = edge_rows(rim, 2, edge_ref[1, :, mine], taps_ref[2, :, mine])
-    up, down, marks = up_ref[0:EDGE, mine], down_ref[:, mine], marks_ref[:, mine]
     rates = rates_ref[...]
     lane = iota(rates.shape, 1)
-    base = group_ref[0] * heads
     at, other = iota((rows, rows), 0), iota((rows, rows), 1)
-    lows, ends, sides = [], [], []
-    for h in range(heads):
-        c = slice(h * D, (h + 1) * D)
-        here = pl.ds(pl.multiple_of(start + h * D, D), D)
-        rate = jnp.sum(jnp.where(lane == base + h, rates, 0.0), -1, keepdims=True)
-        edge = key_terms(keys[:, c], rate, up[:, c], down[:, c], marks[0:1, c], marks[1:2, c])
-        write, low, kin, khi, klo = [
-            jnp.concatenate([e, ref[EDGE:, here]], 0)
-            for e, ref in zip(edge, (write_ref, low_ref, kin_ref, khi_ref, klo_ref))
-        ]
-        vb = jnp.concatenate([(values[:, c] * rate).astype(BF16), vb_ref[EDGE:, here]], 0)
-        low_out_ref[:, c] = low
-        lows.append(jnp.where(at > other, dot_t(write, low), 0.0))
-        ends.append((khi, klo))
-        sides.append(jnp.concatenate([kin, vb], 1))
+    lows, ends, sides, fades = [], [], [], []
+    for n in range(count):
+        start = pl.multiple_of(group_refs[n][0] * cols, cols)
+        mine = pl.ds(start, cols)
+        rim = jnp.where(later_ref[0] > 0, rim_ref[:, mine].astype(F32), 0.0)
+        keys = edge_rows(rim, 1, edge_ref[0, :, mine], taps_ref[1, :, mine])
+        values = edge_rows(rim, 2, edge_ref[1, :, mine], taps_ref[2, :, mine])
+        up, down, marks = up_ref[0:EDGE, mine], down_ref[:, mine], marks_ref[:, mine]
+        for h in range(heads):
+            c = slice(h * D, (h + 1) * D)
+            here = pl.ds(pl.multiple_of(start + h * D, D), D)
+            rate = jnp.sum(jnp.where(lane == group_refs[n][0] * heads + h, rates, 0.0), -1, keepdims=True)
+            edge = key_terms(keys[:, c], rate, up[:, c], down[:, c], marks[0:1, c], marks[1:2, c])
+            write, low, kin, khi, klo = [
+                jnp.concatenate([e, ref[EDGE:, here]], 0)
+                for e, ref in zip(edge, (write_ref, low_ref, kin_ref, khi_ref, klo_ref))
+            ]
+            vb = jnp.concatenate([(values[:, c] * rate).astype(BF16), vb_ref[EDGE:, here]], 0)
+            outs[3 * n + 2][:, c] = low
+            lows.append(jnp.where(at > other, dot_t(write, low), 0.0))
+            ends.append((khi, klo))
+            sides.append(jnp.concatenate([kin, vb], 1))
+            fades.append(marks[0:1, c] * marks[1:2, c] - 1.0)
     solved = solve_heads(lows, rows)
     made = []
     for t, side in zip(solved, sides):
         both = dot(jnp.concatenate(split(t), 0), side)
         made.append((both[:rows] + both[rows:]).astype(BF16))
-    for h in range(heads):
-        c = slice(h * D, (h + 1) * D)
-        sums = t_dot(ends[h][0], made[h]) + t_dot(ends[h][1], made[h])
-        fade = marks[0:1, c] * marks[1:2, c] - 1.0
+    for k, fade in enumerate(fades):
+        n, h = divmod(k, heads)
+        sums = t_dot(ends[k][0], made[k]) + t_dot(ends[k][1], made[k])
         move = jnp.where(at == other, fade, 0.0) - sums[:, :D]
-        made_ref[h] = made[h]
-        move_ref[h, :, :D] = move.astype(BF16)
-        move_ref[h, :, D:] = sums[:, D:].astype(BF16)
+        outs[3 * n + 1][h] = made[k]
+        outs[3 * n][h, :, :D] = move.astype(BF16)
+        outs[3 * n][h, :, D:] = sums[:, D:].astype(BF16)
 
 
 def local_kernel(count, later_ref, *refs):
@@ -416,6 +426,12 @@
     return pairs + list(zip(sources, targets))
 
 
+def block_order(groups):
+    if groups != 4:
+        return [[j] for j in range(groups - 1, -1, -1)]
+    return [[3], [1, 2, 0]]
+
+
 def params():
     return pltpu.CompilerParams(vmem_limit_bytes=VMEM_LIMIT)
 
@@ -437,7 +453,7 @@
         ((group_ids, later, places, span), query_raw, key_raw, value_raw, log_decay)
     )
     me_arg = group_ids[0]
-    near = [pltpu.with_memory_space_constraint(x, pltpu.VMEM) for x in (log_decay, key_raw, value_raw)]
+    near = [pltpu.with_memory_space_constraint(x, pltpu.VMEM) for x in (key_raw, value_raw)]
     query_raw, key_raw, value_raw, log_decay, out_gate = (
         pltpu.with_memory_space_constraint(x, pltpu.HBM) for x in (query_raw, key_raw, value_raw, log_decay, out_gate)
     )
@@ -462,8 +478,9 @@
     wide16 = jax.ShapeDtypeStruct((rows, width), BF16)
     prepared = pl.pallas_call(
         functools.partial(prepare_kernel, groups),
-        in_specs=[vmem] * 5,
+        in_specs=[far] + [vmem] * 4,
         out_specs=[vmem] * 11,
+        scratch_shapes=[pltpu.VMEM((rows, width), BF16), pltpu.SemaphoreType.DMA],
         out_shape=[wide16] * 6
         + [
             jax.ShapeDtypeStruct((rows, width), F32),
@@ -475,24 +492,8 @@
         compiler_params=params(),
         cost_estimate=pl.CostEstimate(flops=20_000_000, bytes_accessed=9_000_000, transcendentals=2_000_000),
         name="prepare",
-    )(*near, beta, conv_weight)
+    )(log_decay, *near, beta, conv_weight)
     write, low, kin, khi, klo, vb, up, down, marks, edges, rates = prepared
-
-    moves, made, lows = [None] * groups, [None] * groups, [None] * groups
-    order = list(range(groups - 1, -1, -1))
-    for j in order:
-        moves[j], made[j], lows[j] = pl.pallas_call(
-            block_kernel,
-            in_specs=[smem] * 2 + [vmem] * 13,
-            out_specs=[vmem] * 3,
-            out_shape=[
-                jax.ShapeDtypeStruct((heads, D, 2 * D), BF16),
-                jax.ShapeDtypeStruct((heads, rows, 2 * D), BF16),
-                jax.ShapeDtypeStruct((rows, cols), BF16),
-            ],
-            compiler_params=params(),
-            name="block",
-        )(group_ids[j], later, rim, edges, rates, conv_weight, up, down, marks, write, low, kin, khi, klo, vb)
 
     def call(kernel, name, in_specs, outs, scratch=()):
         return pl.pallas_call(
@@ -526,6 +527,19 @@
         )
         return {j: got[3 * i : 3 * i + 3] for i, j in enumerate(js)}
 
+    moves, made, lows = ({} for _ in range(3))
+    for js in block_order(groups):
+        got = call(
+            functools.partial(block_kernel, len(js)),
+            "block",
+            [smem] * (1 + len(js)) + [vmem] * 13,
+            [pair, ((heads, rows, 2 * D), BF16), block16] * len(js),
+        )(
+            later, *[group_ids[j] for j in js], rim, edges, rates, conv_weight, up, down, marks, write, low, kin, khi,
+            klo, vb,
+        )
+        for n, j in enumerate(js):
+            moves[j], made[j], lows[j] = got[3 * n : 3 * n + 3]
     came_pairs = [swap(moves[j], j) if j else moves[j] for j in range(groups)]
     left = list(range(groups))
     came_pairs, found = lax.optimization_barrier((came_pairs, local(left[: groups // 2])))
@@ -550,6 +564,8 @@
         )(places[r], *parts, *(own or ()), *(have or ()))
 
     adds = tell(add, 0) if rounds else []
+    adds, mine = lax.optimization_barrier((adds, local(left)))
+    found.update(mine)
     ahead, send_move = None, move
     if spans == 4:
         ahead, told, mixed = call(absorb_four_kernel, "absorb", [smem] + [vmem] * 3, [state] * 3)(
@@ -570,8 +586,7 @@
     (before,) = call(
         prefix_kernel, "prefix", [smem] + [vmem] * groups, [((groups - 1, heads, D, 2 * D), BF16)]
     )(me_arg, *came_pairs)
-    adds, before, mine = lax.optimization_barrier((adds, before, local(left)))
-    found.update(mine)
+    adds, before = lax.optimization_barrier((adds, before))
     if spans == 4:
         starts = call(starts_four_kernel, "starts", [smem] * 2 + [vmem] * 4, [state] * groups)(
             me_arg, span, ahead, *adds, before

time: 48.7 us -> 47.6 us (0.977)
  waiting for transfers between devices: 14.5 us -> 17.5 us
  Pallas kernels: 20.3 us -> 18 us
  local copies, waits for them, and re-layouts: 1.7 us -> 0.67 us
  starting transfers between devices: 11.6 us -> 11.1 us
    ppermute x6, waiting for transfers between devices: 2.71 us -> 6.05 us  [swap(): lax.ppermute(array, axis, [(i, i ^ j) for i in range(lax.axis_size(axis))])]
    ppermute x1, waiting for transfers between devices: 5.41 us -> 2.3 us  [tell(): lax.ppermute(array, 'ctx', whole_route(route, spans))]
    pallas_call x5 -> x3, Pallas kernels: 10.4 us -> 8.12 us  [the longest x2 5.35 us: shards(): call(functools.partial(block_kernel, len(js)), 'block', [smem] * (1 + len...]
    ppermute x1, waiting for transfers between devices: 3.71 us -> 5.68 us  [shards(): lax.ppermute(mixed, 'ctx', whole_route([(0, 1), (1, 2), (2, 3)], 4))]
    unnamed x12 -> x10, local copies, waits for them, and re-layouts: 1.7 us -> 0.67 us
    ppermute x1, waiting for transfers between devices: 2.65 us -> 3.45 us  [shards(): lax.ppermute(tails, ('ctx', 'head'), [(i, (i + 1) % total) for i in range...]
  transfers between devices with their start and end apart: 10 -> 10, of which waited for: 6 -> 7; matrix products, arithmetic and copies ran while one was open for 0% -> 0% of each run, Pallas kernels for 31% -> 27%
where the time goes in v4:
time: 47.6 us; the launch traced here: 47.3 us
  Pallas kernels  18 us (38%)
  waiting for transfers between devices  17.5 us (37%)
  starting transfers between devices  11.1 us (23%)
  local copies, waits for them, and re-layouts  0.67 us (1%)
    ppermute x6, starting transfers between devices, swap(): lax.ppermute(array, axis, [(i, i ^ j) for i in range(lax.axis_size(axis))])  7.14 us
    ppermute x6, waiting for transfers between devices, swap(): lax.ppermute(array, axis, [(i, i ^ j) for i in range(lax.axis_size(axis))])  6.05 us
    ppermute x1, waiting for transfers between devices, shards(): lax.ppermute(mixed, 'ctx', whole_route([(0, 1), (1, 2), (2, 3)], 4))  5.68 us
    pallas_call x2, Pallas kernels, shards(): call(functools.partial(block_kernel, len(js)), 'block', [smem] * (1 + len...  5.35 us
    pallas_call x2, Pallas kernels, local(): call(functools.partial(local_kernel, len(js)), 'local', [smem] * (1 + len...  5.28 us
    ppermute x1, waiting for transfers between devices, shards(): lax.ppermute(tails, ('ctx', 'head'), [(i, (i + 1) % total) for i in range...  3.45 us
    ppermute x1, starting transfers between devices, shards(): lax.ppermute(tails, ('ctx', 'head'), [(i, (i + 1) % total) for i in range...  3 us
    pallas_call x1, Pallas kernels, shards(): pl.pallas_call(functools.partial(prepare_kernel, groups), in_specs=[far]...  2.77 us
  transfers between devices with their start and end apart: 10, of which 7 were waited for; matrix products, arithmetic and copies ran while one was open for 0% of the time, Pallas kernels for 27%

profile of v4, /device:TPU:0, one launch (start us, length us, event | category | flops | bytes accessed | tf_op | source)
XLA Modules:
  0.0 47.3 jit_solution(17737517685663285821)
XLA Ops:
  0.0 0.0 copy-start
  0.0 0.0 copy-start.1
  0.0 0.0 copy-start.2
  0.0 0.0 copy-start.4
  0.0 1.0 %tails.1 = bf16[16,2048]{1,0:T(8,128)(2,1)S(1)} custom-call(bf16[128,2048]{1,0:T(8,128)(2,1)} %refs_3_.1, bf16[128,2048]{1,0:T(8,128)(2,1)} %k_ref, bf16[128,2048]{1,0:T(8,128)(2,1)} %v_ref), custom_call_target="tpu_custom_call" | custom-call | tf_op jit(solution)/shard_map/tails/pallas_call | solution.py:466
  1.1 3.0 %collective-permute-start = (bf16[16,2048]{1,0:T(8,128)(2,1)S(1)}, bf16[16,2048]{1,0:T(8,128)(2,1)S(1)}, u32[]{:S(2)}, u32[]{:S(2)}) collective-permute-start(bf16[16,2048]{1,0:T(8,128)(2,1)S(1)} %tails.1), channel_id=1, source_target_pairs={{0,2},{2,4},{4,6},{6,8},{8,10},{10,12},{12,14},{14,16},{16,18},{18... | collective-permute-start | bytes 196616 | tf_op jit(solution)/shard_map/ppermute | solution.py:476
  4.1 0.0 copy-done
  4.1 0.0 copy-done.1
  4.1 0.0 copy-done.2
  4.1 0.0 copy-done.4
  4.1 2.8 %prepare.1 = (bf16[128,2048]{1,0:T(8,128)(2,1)S(1)}, bf16[128,2048]{1,0:T(8,128)(2,1)S(1)}, bf16[128,2048]{1,0:T(8,128)(2,1)S(1)}, bf16[128,2048]{1,0:T(8,128)(2...) custom-call(bf16[128,2048]{1,0:T(8,128)(2,1)} %g_ref, ...), custom_call_target="tpu_custom_call" | custom-call | flops 20000000 | bytes 9000000 | tf_op jit(solution)/shard_map/prepare/pallas_call | solution.py:479
  6.9 3.4 %collective-permute-done.refs_3_.refs_1_.refs_2_ = bf16[16,2048]{1,0:T(8,128)(2,1)S(1)} collective-permute-done((bf16[16,2048]{1,0:T(8,128)(2,1)S(1)}, bf16[16,2048]{1,0:T(8,128)(2,1)S(1)}, u32[]{:S(2)}, u32[]{:S(2)}) %collective-permute-start) | collective-permute-done | bytes 65568 | tf_op jit(solution)/shard_map/ppermute | solution.py:476
  10.3 1.9 %block.3 = (bf16[4,128,256]{2,1,0:T(8,128)(2,1)S(1)}, bf16[4,128,256]{2,1,0:T(8,128)(2,1)S(1)}, bf16[128,512]{1,0:T(8,128)(2,1)S(1)}) custom-call(s32[1]{0:T(128)S(6)} %convert_element_type.3.later_ref, s32[1]{0:T(128)S(6)} %xor.11.refs_0_.refs_1_, bf16[16,2048]{1,0:T(8,128)(2,1)S(1)} %collective-permute-done.refs_3_.refs_1_.refs_2_, ...), custom_call_target="tpu_custom_call" | custom-call | tf_op jit(solution)/shard_map/block/pallas_call | solution.py:532
  12.2 0.1 collective-permute-start.3
  12.3 3.5 %block.2 = (bf16[4,128,256]{2,1,0:T(8,128)(2,1)S(1)}, bf16[4,128,256]{2,1,0:T(8,128)(2,1)S(1)}, bf16[128,512]{1,0:T(8,128)(2,1)S(1)}, bf16[4,128,256]{2,1,0:T(8,...) custom-call(s32[1]{0:T(128)S(6)} %convert_element_type.3.later_ref, ...), custom_call_target="tpu_custom_call" | custom-call | tf_op jit(solution)/shard_map/block/pallas_call | solution.py:532
  15.7 0.5 collective-permute-start.1
  16.2 3.1 %collective-permute-start.2 = (bf16[4,128,256]{2,1,0:T(8,128)(2,1)S(1)}, bf16[4,128,256]{2,1,0:T(8,128)(2,1)S(1)}, u32[]{:S(2)}, u32[]{:S(2)}) collective-permute-start(bf16[4,128,256]{2,1,0:T(8,128)(2,1)S(1)} %get-tuple-element.101), channel_id=1, source_target_pairs={{0,4},{2,6},{4,0},{6,2},{1,5},{3,7},{5,1},{7,3},{8,12},{10,14},{12... | collective-permute-start | bytes 786440 | tf_op jit(solution)/shard_map/ppermute | solution.py:510
  19.3 0.0 copy-start.3
  19.3 0.7 %copy-done.3 = f32[128]{0:T(128)S(1)} copy-done((f32[128]{0:T(128)S(1)}, f32[128]{0:T(128)}, u32[]{:S(2)}) %copy-start.3) | copy-done | bytes 536
  19.9 2.6 %local.2 = (bf16[128,512]{1,0:T(8,128)(2,1)S(1)}, f32[128,512]{1,0:T(8,128)S(1)}, f32[128,512]{1,0:T(8,128)S(1)}, bf16[128,512]{1,0:T(8,128)(2,1)S(1)}, f32[128,512]{1,0:T(8,128)S(1)}, /*index=5*/f32[128,512]{1,0:T(8,128)S(1)}) custom-call(s32[1]{0:T(128)S(6)} %convert_element_type.3.later_ref, s32[1]{0:T(128)} %bitcast.refs_2_.refs_0_.me_ref, ...), custom_call_target="tpu_custom_call" | custom-call | tf_op jit(solution)/shard_map/local/pallas_call | solution.py:518
  22.6 0.0 collective-permute-done.3.refs_3_
  22.6 0.6 %collective-permute-done.1.refs_1_ = bf16[4,128,256]{2,1,0:T(8,128)(2,1)S(1)} collective-permute-done((bf16[4,128,256]{2,1,0:T(8,128)(2,1)S(1)}, bf16[4,128,256]{2,1,0:T(8,128)(2,1)S(1)}, u32[]{:S(2)}, u32[]{:S(2)}) %collective-permute-start.1) | collective-permute-done | bytes 262176 | tf_op jit(solution)/shard_map/ppermute | solution.py:510
  23.2 2.9 %collective-permute-done.2.refs_2_ = bf16[4,128,256]{2,1,0:T(8,128)(2,1)S(1)} collective-permute-done((bf16[4,128,256]{2,1,0:T(8,128)(2,1)S(1)}, bf16[4,128,256]{2,1,0:T(8,128)(2,1)S(1)}, u32[]{:S(2)}, u32[]{:S(2)}) %collective-permute-start.2) | collective-permute-done | bytes 262176 | tf_op jit(solution)/shard_map/ppermute | solution.py:510
  26.1 0.5 chain.1
  26.6 0.1 collective-permute-start.4
  26.6 2.6 %local.3 = (bf16[128,512]{1,0:T(8,128)(2,1)S(1)}, f32[128,512]{1,0:T(8,128)S(1)}, f32[128,512]{1,0:T(8,128)S(1)}, bf16[128,512]{1,0:T(8,128)(2,1)S(1)}, f32[128,512]{1,0:T(8,128)S(1)}, /*index=5*/f32[128,512]{1,0:T(8,128)S(1)}) custom-call(s32[1]{0:T(128)S(6)} %convert_element_type.3.later_ref, s32[1]{0:T(128)S(6)} %xor.10.refs_1_.refs_0_, ...), custom_call_target="tpu_custom_call" | custom-call | tf_op jit(solution)/shard_map/local/pallas_call | solution.py:518
  29.3 2.3 %collective-permute-done.4.came_ref = bf16[4,128,128]{2,1,0:T(8,128)(2,1)S(1)} collective-permute-done((bf16[4,128,128]{2,1,0:T(8,128)(2,1)S(1)}, bf16[4,128,128]{2,1,0:T(8,128)(2,1)S(1)}, u32[]{:S(2)}, u32[]{:S(2)}) %collective-permute-start.4) | collective-permute-done | bytes 131104 | tf_op jit(solution)/shard_map/ppermute | solution.py:555
  31.6 0.2 collective-permute-start.5
  31.8 0.7 %collective-permute-start.6 = (bf16[4,128,128]{2,1,0:T(8,128)(2,1)S(1)}, bf16[4,128,128]{2,1,0:T(8,128)(2,1)S(1)}, u32[]{:S(2)}, u32[]{:S(2)}) collective-permute-start(bf16[4,128,128]{2,1,0:T(8,128)(2,1)S(1)} %get-tuple-element.139), channel_id=1, source_target_pairs={{8,24},{24,16},{16,8},{0,0},{9,25},{25,17},{17,9},{1,1},{10,26},{2... | collective-permute-start | bytes 393224 | tf_op jit(solution)/shard_map/ppermute | solution.py:576
  32.5 0.4 prefix.1.before_ref
  33.0 5.7 %collective-permute-done.5.near_ref = bf16[4,128,128]{2,1,0:T(8,128)(2,1)S(1)} collective-permute-done((bf16[4,128,128]{2,1,0:T(8,128)(2,1)S(1)}, bf16[4,128,128]{2,1,0:T(8,128)(2,1)S(1)}, u32[]{:S(2)}, u32[]{:S(2)}) %collective-permute-start.5) | collective-permute-done | bytes 131104 | tf_op jit(solution)/shard_map/ppermute | solution.py:575
  38.6 0.0 collective-permute-done.6.far_ref
  38.6 0.5 starts.1
  39.1 0.1 collective-permute-start.7
  39.2 1.2 %collective-permute-start.8 = (bf16[4,128,128]{2,1,0:T(8,128)(2,1)S(1)}, bf16[4,128,128]{2,1,0:T(8,128)(2,1)S(1)}, u32[]{:S(2)}, u32[]{:S(2)}) collective-permute-start(bf16[4,128,128]{2,1,0:T(8,128)(2,1)S(1)} %get-tuple-element.151), channel_id=1, source_target_pairs={{0,4},{2,6},{4,0},{6,2},{1,5},{3,7},{5,1},{7,3},{8,12},{10,14},{12... | collective-permute-start | bytes 393224 | tf_op jit(solution)/shard_map/ppermute | solution.py:510
  40.4 2.3 %collective-permute-start.9 = (bf16[4,128,128]{2,1,0:T(8,128)(2,1)S(1)}, bf16[4,128,128]{2,1,0:T(8,128)(2,1)S(1)}, u32[]{:S(2)}, u32[]{:S(2)}) collective-permute-start(bf16[4,128,128]{2,1,0:T(8,128)(2,1)S(1)} %get-tuple-element.152), channel_id=1, source_target_pairs={{0,6},{2,4},{4,2},{6,0},{1,7},{3,5},{5,3},{7,1},{8,14},{10,12},{12... | collective-permute-start | bytes 393224 | tf_op jit(solution)/shard_map/ppermute | solution.py:510
  42.7 1.5 %collective-permute-done.7.refs_9_ = bf16[4,128,128]{2,1,0:T(8,128)(2,1)S(1)} collective-permute-done((bf16[4,128,128]{2,1,0:T(8,128)(2,1)S(1)}, bf16[4,128,128]{2,1,0:T(8,128)(2,1)S(1)}, u32[]{:S(2)}, u32[]{:S(2)}) %collective-permute-start.7) | collective-permute-done | bytes 131104 | tf_op jit(solution)/shard_map/ppermute | solution.py:510
  44.1 1.1 %finish.2.refs_2_ = bf16[128,2048]{1,0:T(8,128)(2,1)} custom-call(s32[1]{0:T(128)} %bitcast.refs_2_.refs_0_.me_ref, s32[1]{0:T(128)S(6)} %xor.9.refs_0_.refs_1_, bf16[128,512]{1,0:T(8,128)(2,1)S(1)} %get-tuple-element.113.refs_2_, bf16[128,512]{1,0:T(8,128)(2,1)S(1)} %get-tuple-element.114.refs_3_, f32[128,512]{1,0:T(8,128)S(1)} %get-tuple-element.115.refs_4_, ...), custom_call_target="tpu_custom_call" | custom-call | tf_op jit(solution)/shard_map/finish/pallas_call | solution.py:606
  45.2 0.0 collective-permute-done.8.refs_9_
  45.2 1.1 %collective-permute-done.9.refs_10_ = bf16[4,128,128]{2,1,0:T(8,128)(2,1)S(1)} collective-permute-done((bf16[4,128,128]{2,1,0:T(8,128)(2,1)S(1)}, bf16[4,128,128]{2,1,0:T(8,128)(2,1)S(1)}, u32[]{:S(2)}, u32[]{:S(2)}) %collective-permute-start.9) | collective-permute-done | bytes 131104 | tf_op jit(solution)/shard_map/ppermute | solution.py:510
  46.3 1.1 %finish.3 = bf16[128,2048]{1,0:T(8,128)(2,1)} custom-call(s32[1]{0:T(128)S(6)} %xor.10.refs_1_.refs_0_, s32[1]{0:T(128)S(6)} %xor.11.refs_0_.refs_1_, bf16[128,2048]{1,0:T(8,128)(2,1)} %finish.2.refs_2_, bf16[128,512]{1,0:T(8,128)(2,1)S(1)} %get-tuple-element.145.refs_3_, ...), custom_call_target="tpu_custom_call", output_to_operand_aliasing={{}: (2, {})} | custom-call | tf_op jit(solution)/shard_map/finish/pallas_call | solution.py:606
  (1 shorter events, 0.0 us)
Async XLA Ops:
  0.0 4.1 %copy-start = (f32[3,4,2048]{2,1,0:T(4,128)S(1)}, f32[3,4,2048]{2,1,0:T(4,128)}, u32[]{:S(2)}) copy-start(f32[3,4,2048]{2,1,0:T(4,128)} %refs_5_.3) | copy-start | bytes 294916
  0.0 4.1 %copy-start.1 = (bf16[128,2048]{1,0:T(8,128)(2,1)S(1)}, bf16[128,2048]{1,0:T(8,128)(2,1)}, u32[]{:S(2)}) copy-start(bf16[128,2048]{1,0:T(8,128)(2,1)} %k_ref) | copy-start | bytes 1572868
  0.0 4.1 %copy-start.2 = (bf16[128,2048]{1,0:T(8,128)(2,1)S(1)}, bf16[128,2048]{1,0:T(8,128)(2,1)}, u32[]{:S(2)}) copy-start(bf16[128,2048]{1,0:T(8,128)(2,1)} %v_ref) | copy-start | bytes 1572868
  0.0 4.1 %copy-start.4 = (bf16[128,16]{0,1:T(8,128)(2,1)S(1)}, bf16[128,16]{0,1:T(8,128)(2,1)}, u32[]{:S(2)}) copy-start(bf16[128,16]{0,1:T(8,128)(2,1)} %param.12) | copy-start | bytes 12292
  1.1 9.2 %collective-permute-start = (bf16[16,2048]{1,0:T(8,128)(2,1)S(1)}, bf16[16,2048]{1,0:T(8,128)(2,1)S(1)}, u32[]{:S(2)}, u32[]{:S(2)}) collective-permute-start(bf16[16,2048]{1,0:T(8,128)(2,1)S(1)} %tails.1), channel_id=1, source_target_pairs={{0,2},{2,4},{4,6},{6,8},{8,10},{10,12},{12,14},{14,16},{16,18},{18... | collective-permute-start | bytes 196616 | tf_op jit(solution)/shard_map/ppermute | solution.py:476
  12.2 10.4 %collective-permute-start.3 = (bf16[4,128,256]{2,1,0:T(8,128)(2,1)S(1)}, bf16[4,128,256]{2,1,0:T(8,128)(2,1)S(1)}, u32[]{:S(2)}, u32[]{:S(2)}) collective-permute-start(bf16[4,128,256]{2,1,0:T(8,128)(2,1)S(1)} %get-tuple-element.102), channel_id=1, source_target_pairs={{0,6},{2,4},{4,2},{6,0},{1,7},{3,5},{5,3},{7,1},{8,14},{10,12},{12... | collective-permute-start | bytes 786440 | tf_op jit(solution)/shard_map/ppermute | solution.py:510
  15.7 7.4 %collective-permute-start.1 = (bf16[4,128,256]{2,1,0:T(8,128)(2,1)S(1)}, bf16[4,128,256]{2,1,0:T(8,128)(2,1)S(1)}, u32[]{:S(2)}, u32[]{:S(2)}) collective-permute-start(bf16[4,128,256]{2,1,0:T(8,128)(2,1)S(1)} %get-tuple-element.100), channel_id=1, source_target_pairs={{0,2},{2,0},{4,6},{6,4},{1,3},{3,1},{5,7},{7,5},{8,10},{10,8},{12,... | collective-permute-start | bytes 786440 | tf_op jit(solution)/shard_map/ppermute | solution.py:510
  16.2 9.9 %collective-permute-start.2 = (bf16[4,128,256]{2,1,0:T(8,128)(2,1)S(1)}, bf16[4,128,256]{2,1,0:T(8,128)(2,1)S(1)}, u32[]{:S(2)}, u32[]{:S(2)}) collective-permute-start(bf16[4,128,256]{2,1,0:T(8,128)(2,1)S(1)} %get-tuple-element.101), channel_id=1, source_target_pairs={{0,4},{2,6},{4,0},{6,2},{1,5},{3,7},{5,1},{7,3},{8,12},{10,14},{12... | collective-permute-start | bytes 786440 | tf_op jit(solution)/shard_map/ppermute | solution.py:510
  19.3 0.7 %copy-start.3 = (f32[128]{0:T(128)S(1)}, f32[128]{0:T(128)}, u32[]{:S(2)}) copy-start(f32[128]{0:T(128)} %param.15) | copy-start | bytes 1540
  26.6 5.0 %collective-permute-start.4 = (bf16[4,128,128]{2,1,0:T(8,128)(2,1)S(1)}, bf16[4,128,128]{2,1,0:T(8,128)(2,1)S(1)}, u32[]{:S(2)}, u32[]{:S(2)}) collective-permute-start(bf16[4,128,128]{2,1,0:T(8,128)(2,1)S(1)} %get-tuple-element.125.add_ref), channel_id=1, source_target_pairs={{0,8},{16,24},{8,0},{24,16},{1,9},{17,25},{9,1},{25,17},{2,10},{18... | collective-permute-start | bytes 393224 | tf_op jit(solution)/shard_map/ppermute | solution.py:555
  31.6 7.0 %collective-permute-start.5 = (bf16[4,128,128]{2,1,0:T(8,128)(2,1)S(1)}, bf16[4,128,128]{2,1,0:T(8,128)(2,1)S(1)}, u32[]{:S(2)}, u32[]{:S(2)}) collective-permute-start(bf16[4,128,128]{2,1,0:T(8,128)(2,1)S(1)} %get-tuple-element.138), channel_id=1, source_target_pairs={{0,8},{8,16},{16,24},{24,0},{1,9},{9,17},{17,25},{25,1},{2,10},{10... | collective-permute-start | bytes 393224 | tf_op jit(solution)/shard_map/ppermute | solution.py:575
  31.8 6.8 %collective-permute-start.6 = (bf16[4,128,128]{2,1,0:T(8,128)(2,1)S(1)}, bf16[4,128,128]{2,1,0:T(8,128)(2,1)S(1)}, u32[]{:S(2)}, u32[]{:S(2)}) collective-permute-start(bf16[4,128,128]{2,1,0:T(8,128)(2,1)S(1)} %get-tuple-element.139), channel_id=1, source_target_pairs={{8,24},{24,16},{16,8},{0,0},{9,25},{25,17},{17,9},{1,1},{10,26},{2... | collective-permute-start | bytes 393224 | tf_op jit(solution)/shard_map/ppermute | solution.py:576
  39.1 5.0 %collective-permute-start.7 = (bf16[4,128,128]{2,1,0:T(8,128)(2,1)S(1)}, bf16[4,128,128]{2,1,0:T(8,128)(2,1)S(1)}, u32[]{:S(2)}, u32[]{:S(2)}) collective-permute-start(bf16[4,128,128]{2,1,0:T(8,128)(2,1)S(1)} %get-tuple-element.144), channel_id=1, source_target_pairs={{0,2},{2,0},{4,6},{6,4},{1,3},{3,1},{5,7},{7,5},{8,10},{10,8},{12,... | collective-permute-start | bytes 393224 | tf_op jit(solution)/shard_map/ppermute | solution.py:510
  39.2 6.0 %collective-permute-start.8 = (bf16[4,128,128]{2,1,0:T(8,128)(2,1)S(1)}, bf16[4,128,128]{2,1,0:T(8,128)(2,1)S(1)}, u32[]{:S(2)}, u32[]{:S(2)}) collective-permute-start(bf16[4,128,128]{2,1,0:T(8,128)(2,1)S(1)} %get-tuple-element.151), channel_id=1, source_target_pairs={{0,4},{2,6},{4,0},{6,2},{1,5},{3,7},{5,1},{7,3},{8,12},{10,14},{12... | collective-permute-start | bytes 393224 | tf_op jit(solution)/shard_map/ppermute | solution.py:510
  40.4 5.9 %collective-permute-start.9 = (bf16[4,128,128]{2,1,0:T(8,128)(2,1)S(1)}, bf16[4,128,128]{2,1,0:T(8,128)(2,1)S(1)}, u32[]{:S(2)}, u32[]{:S(2)}) collective-permute-start(bf16[4,128,128]{2,1,0:T(8,128)(2,1)S(1)} %get-tuple-element.152), channel_id=1, source_target_pairs={{0,6},{2,4},{4,2},{6,0},{1,7},{3,5},{5,3},{7,1},{8,14},{10,12},{12... | collective-permute-start | bytes 393224 | tf_op jit(solution)/shard_map/ppermute | solution.py:510
